TPU v7x, 32 devices: a whole 2x2x4 slice. The times are simulated.
32 devices in a mesh: groups: 2 (over y), doc: 8 (over z, x), layer: 2 (over core).
Axes of the slice: x: 2, y: 2, z: 4, core: 2. Of those that a mesh axis runs over, the one named last changes fastest.
Arguments:
- queries: bfloat16 [2, 2, 4096, 768], P('layer', None, 'doc', 'groups'), parts along dimension 3, may hold values from -6 to 6
- inverse_fisher: bfloat16 [2, 2, 4096, 4096], P('layer', None, 'doc'), as said below
- documents: bfloat16 [2, 3584, 2, 4096], P('layer', ('groups', 'doc')), parts along dimension 1, may hold values from -0.0625 to 0.0625
- doc_order: int32 [16, 224], P(('groups', 'doc')), parts along dimension 0, may hold values from 0 to 223, each once within a row
Outputs:
- influence: float32 [3584, 384], P(('groups', 'doc')), parts along dimension 0
There are 2 independent parts, one for each index of `groups`. A program takes and returns all parts, laid end to end along the dimension named above; an argument that names none is the same for every part. Nothing has to cross between parts.
Inputs may be any that keep to these rules, and one draw needn't show every extreme that they name: Each row of doc_order holds every number of 0 to 223 once. inverse_fisher[l, m] is symmetric.
All inputs are finite; a program needn't handle non-finite values.
Results may differ from a plain program's by a relative error of at most 0.0029.
Values may be sent and summed in bfloat16 or wider, within the bound.
No kernel may reach another device: no remote copies, remote signals or barrier semaphores. Data moves between devices by JAX's collectives and lax.ppermute only.
A program may use at most 64 MiB of HBM per device.

v0:
```python
import jax
import jax.numpy as jnp
from jax import lax
from jax.sharding import PartitionSpec as P


def per_device(queries, inverse_fisher, documents, doc_order):
    fisher_cols = inverse_fisher[0]
    query_slab = queries[0]
    store = documents[0]
    modules = fisher_cols.shape[0]
    width = fisher_cols.shape[2]
    n_query = query_slab.shape[2]
    n_rows = store.shape[0]
    full_queries = lax.all_gather(query_slab, "doc", axis=1, tiled=True)
    precond = jnp.einsum(
        "mji,miq->mjq", fisher_cols, full_queries, preferred_element_type=jnp.float32
    ).astype(jnp.bfloat16)
    full_precond = lax.all_gather(precond, "doc", axis=1, tiled=True)
    layer_scores = jnp.dot(
        store.reshape(n_rows, modules * width),
        full_precond.reshape(modules * width, n_query),
        preferred_element_type=jnp.float32,
    )
    total = lax.psum(layer_scores, "layer")
    return jnp.zeros_like(total).at[doc_order[0]].set(total)


def solution(mesh):
    in_specs = (
        P("layer", None, "doc", "groups"),
        P("layer", None, "doc", None),
        P("layer", ("groups", "doc"), None, None),
        P(("groups", "doc"), None),
    )
    out_specs = P(("groups", "doc"), None)
    return jax.shard_map(
        per_device, mesh=mesh, in_specs=in_specs, out_specs=out_specs, check_vma=False
    )
```

profile of v0, /device:TPU:0, one launch (start us, length us, event | category | flops | bytes accessed | tf_op | source)
XLA Modules:
  0.0 251.7 jit_solution(10432870034970858176)
XLA Ops:
  6.5 0.0 all-gather.6.cloned.1.call-start
  6.5 0.7 all-gather.6.cloned.1.call-update
  7.3 0.0 all-gather.4.cloned.1.call-start
  7.3 104.0 %all-gather.6.cloned.1.call-done = bf16[1,2,4096,384]{3,2,1,0:T(8,128)(2,1)} async-done(((bf16[1,2,512,384]{3,2,1,0:T(8,128)(2,1)}), bf16[1,2,4096,384]{3,2,1,0:T(8,128)(2,1)}) %all-gather.6.cloned.1.call-update) | async-done | bytes 6291472 | tf_op jit(solution)/shard_map/all_gather | solution.py:15
  111.3 10.6 %fusion.3 = bf16[2,512,384]{2,1,0:T(8,128)(2,1)} fusion(bf16[1,2,4096,384]{3,2,1,0:T(8,128)(2,1)} %all-gather.6.cloned.1.call-done, bf16[1,2,512,4096]{3,2,1,0:T(8,128)(2,1)} %param.5), kind=kOutput, calls=%fused_computation.4 | convolution fusion | flops 3221618688 | bytes 15466496 | tf_op jit(solution)/shard_map/mji,miq->mjq/dot_general | solution.py:16
  121.9 0.0 all-gather.4.cloned.1.call-update
  121.9 0.0 all-reduce.2.cloned.1.call-start
  121.9 6.4 %copy.5 = bf16[28,8,2,4096]{3,1,2,0:T(8,128)(2,1)} copy(bf16[28,8,2,4096]{3,2,1,0:T(2,128)(2,1)} %bitcast.22) | data formatting | bytes 7340032
  128.3 90.9 %all-gather.4.cloned.1.call-done = bf16[2,4096,384]{2,1,0:T(8,128)(2,1)} async-done(((bf16[2,512,384]{2,1,0:T(8,128)(2,1)}), bf16[2,4096,384]{2,1,0:T(8,128)(2,1)}) %all-gather.4.cloned.1.call-update) | async-done | bytes 6291472 | tf_op jit(solution)/shard_map/all_gather | solution.py:19
  219.2 0.0 copy-start
  219.3 6.7 %convolution_bitcast_fusion = f32[224,384]{1,0:T(8,128)} fusion(bf16[224,8192]{1,0:T(8,128)(2,1)} %bitcast.23, bf16[8192,384]{1,0:T(8,128)(2,1)} %bitcast.25), kind=kOutput, calls=%fused_computation.5 | convolution fusion | flops 1409286144 | bytes 10305536 | tf_op jit(solution)/shard_map/dot_general | solution.py:20
  226.0 0.0 all-reduce.2.cloned.1.call-update
  226.0 0.0 copy-done
  226.0 16.7 %all-reduce.2.cloned.1.call-done = f32[224,384]{1,0:T(8,128)} async-done(((f32[224,384]{1,0:T(8,128)}), f32[224,384]{1,0:T(8,128)}) %all-reduce.2.cloned.1.call-update) | async-done | bytes 344080 | tf_op jit(solution)/shard_map/psum | solution.py:25
  242.7 2.5 scatter_custom_fusion
  (1 shorter events, 0.0 us)
Async XLA Ops:
  6.5 104.8 %all-gather.6.cloned.1.call-start = ((), (), s32[]{:S(2)}) async-start(), calls=%async_computation.2 | async-start | bytes 7077888 | tf_op jit(solution)/shard_map/all_gather | solution.py:15
  7.3 212.0 %all-gather.4.cloned.1.call-start = ((), (), s32[]{:S(2)}) async-start(), calls=%async_computation | async-start | bytes 7077888 | tf_op jit(solution)/shard_map/all_gather | solution.py:19
  121.9 120.9 %all-reduce.2.cloned.1.call-start = ((), (), s32[]{:S(2)}) async-start(), calls=%async_computation.1 | async-start | bytes 688128 | tf_op jit(solution)/shard_map/psum | solution.py:25
  219.2 6.7 %copy-start = (s32[1,224]{1,0:T(1,128)S(1)}, s32[1,224]{1,0:T(1,128)}, u32[]{:S(2)}) copy-start(s32[1,224]{1,0:T(1,128)} %param.7) | copy-start | bytes 2692
Sparse Core Ops, SparseCore 0:
  9.5 101.7 all-gather.5
  122.0 97.1 all-gather.3
  226.1 16.5 all-reduce.1
where the time goes:
time: 252 us
  waiting for transfers between devices  212 us (84%)
  matrix products  17.3 us (7%)
  between operations  13.1 us (5%)
  local copies, waits for them, and re-layouts  8.86 us (4%)
    all_gather x1, waiting for transfers between devices, per_device(): full_queries = lax.all_gather(query_slab, 'doc', axis=1, tiled=True)  104 us
    all_gather x1, waiting for transfers between devices, per_device(): full_precond = lax.all_gather(precond, 'doc', axis=1, tiled=True)  90.9 us
    psum x1, waiting for transfers between devices, per_device(): total = lax.psum(layer_scores, 'layer')  16.7 us
    dot_general x1, matrix products, per_device(): jnp.einsum('mji,miq->mjq', fisher_cols, full_queries, preferred_element_t...  10.6 us
    dot_general x1, matrix products, per_device(): jnp.dot(store.reshape(n_rows, modules * width), full_precond.reshape(modu...  6.72 us
    unnamed x3, local copies, waits for them, and re-layouts  6.4 us
  transfers between devices with their start and end apart: 3, of which 3 were waited for; matrix products, arithmetic and copies ran while one was open for 3% of the time, Pallas kernels for 0%

commit v1 on v0

v1 whole, which is shorter than its diff:
```python
import jax
import jax.numpy as jnp
import numpy as np
from jax import lax
from jax.sharding import PartitionSpec as P


def ring_order(n):
    half = n // 2
    return [2 * i for i in range(half)] + [2 * i + 1 for i in reversed(range(half))]


def dot(a, b):
    return jnp.dot(a, b, preferred_element_type=jnp.float32)


def place_documents(store, order):
    n_rows = store.shape[0]
    place = (order[None, :] == lax.broadcasted_iota(jnp.int32, (n_rows, n_rows), 0)).astype(store.dtype)
    return dot(place, store.reshape(n_rows, -1)).astype(store.dtype)


def make_per_device(n):
    ring = ring_order(n)
    where = np.zeros(n, np.int32)
    where[ring] = np.arange(n)
    up = [(ring[i], ring[(i + 1) % n]) for i in range(n)]
    down = [(b, a) for a, b in up]

    def ring_gather(blocks, use):
        m_all = len(blocks)
        for m in range(m_all):
            use(m, blocks[m], 0)
        going_up, going_down = list(blocks), list(blocks)
        for step in range(1, n // 2 + 1):
            for m in range(m_all):
                last = step == n // 2
                if not last or m % 2 == 0:
                    going_up[m] = lax.ppermute(going_up[m], "doc", up)
                    use(m, going_up[m], step)
                if not last or m % 2 == 1:
                    going_down[m] = lax.ppermute(going_down[m], "doc", down)
                    use(m, going_down[m], -step)

    def per_device(queries, inverse_fisher, documents, doc_order):
        fisher = inverse_fisher[0]
        query = queries[0]
        modules, depth, width = fisher.shape
        at = jnp.asarray(where)[lax.axis_index("doc")]
        ring_of = jnp.asarray(np.asarray(ring, np.int32))

        def first(shift):
            return ring_of[(at - shift + n) % n] * depth

        placed = place_documents(documents[0], doc_order[0])
        acc = [None] * modules

        def add_precond(m, block, shift):
            part = dot(lax.dynamic_slice_in_dim(fisher[m], first(shift), depth, 1), block)
            acc[m] = part if acc[m] is None else acc[m] + part

        ring_gather([query[m] for m in range(modules)], add_precond)
        precond = [a.astype(jnp.bfloat16) for a in acc]
        score = [None]

        def add_score(m, block, shift):
            part = dot(lax.dynamic_slice_in_dim(placed, m * width + first(shift), depth, 1), block)
            score[0] = part if score[0] is None else score[0] + part

        ring_gather(precond, add_score)
        return score[0] + lax.ppermute(score[0], "layer", [(0, 1), (1, 0)])

    return per_device


def per_device_any(queries, inverse_fisher, documents, doc_order):
    fisher = inverse_fisher[0]
    placed = place_documents(documents[0], doc_order[0])
    full_queries = lax.all_gather(queries[0], "doc", axis=1, tiled=True)
    precond = jnp.einsum("mji,miq->mjq", fisher, full_queries, preferred_element_type=jnp.float32).astype(jnp.bfloat16)
    full_precond = lax.all_gather(precond, "doc", axis=1, tiled=True)
    score = dot(placed, full_precond.reshape(-1, full_precond.shape[2]))
    return lax.psum(score, "layer")


def solution(mesh):
    n = mesh.shape["doc"]
    per_device = make_per_device(n) if n == 8 and mesh.shape["layer"] == 2 else per_device_any
    in_specs = (
        P("layer", None, "doc", "groups"),
        P("layer", None, "doc", None),
        P("layer", ("groups", "doc"), None, None),
        P(("groups", "doc"), None),
    )
    out_specs = P(("groups", "doc"), None)
    return jax.shard_map(per_device, mesh=mesh, in_specs=in_specs, out_specs=out_specs, check_vma=False)
```

time: 252 us -> 150 us (0.60)
  waiting for transfers between devices: 212 us -> 70.9 us
  starting transfers between devices: 0.08 us -> 29.2 us
  local copies, waits for them, and re-layouts: 8.86 us -> 16.5 us
  matrix products: 17.3 us -> 19.9 us
    all_gather x2 -> x0, waiting for transfers between devices: 195 us -> none  [the longest x1 104 us: per_device(): full_queries = lax.all_gather(query_slab, 'doc', axis=1, tiled=True)]
    ppermute x0 -> x29, waiting for transfers between devices: none -> 70.9 us  [the longest x14 48.4 us: ring_gather(): going_down[m] = lax.ppermute(going_down[m], 'doc', down)]
    ppermute x0 -> x29, starting transfers between devices: none -> 29.2 us  [the longest x14 17 us: ring_gather(): going_up[m] = lax.ppermute(going_up[m], 'doc', up)]
    psum x1 -> x0, waiting for transfers between devices: 16.7 us -> none  [per_device(): total = lax.psum(layer_scores, 'layer')]
    slice x0 -> x1, local copies, waits for them, and re-layouts: none -> 6 us  [add_precond(): fisher[m]]
    dynamic_slice x0 -> x2, local copies, waits for them, and re-layouts: none -> 2.93 us  [the longest x1 1.69 us: first(): return ring_of[(at - shift + n) % n] * depth]
    dot_general x2 -> x33, matrix products: 17.3 us -> 19.9 us  [dot(): return jnp.dot(a, b, preferred_element_type=jnp.float32)]
    unnamed x3 -> x9, local copies, waits for them, and re-layouts: 6.4 us -> 6.41 us
  transfers between devices with their start and end apart: 3 -> 29, of which waited for: 3 -> 14; matrix products, arithmetic and copies ran while one was open for 3% -> 23% of each run, Pallas kernels for 0% -> 0%
where the time goes in v1:
time: 150 us; the launch traced here: 149 us
  waiting for transfers between devices  70.9 us (47%)
  starting transfers between devices  29.2 us (19%)
  matrix products  19.9 us (13%)
  local copies, waits for them, and re-layouts  16.5 us (11%)
  between operations  11.9 us (8%)
    ppermute x14, waiting for transfers between devices, ring_gather(): going_down[m] = lax.ppermute(going_down[m], 'doc', down)  48.4 us
    ppermute x14, waiting for transfers between devices, ring_gather(): going_up[m] = lax.ppermute(going_up[m], 'doc', up)  20.9 us
    dot_general x33, matrix products, dot(): return jnp.dot(a, b, preferred_element_type=jnp.float32)  19.9 us
    ppermute x14, starting transfers between devices, ring_gather(): going_up[m] = lax.ppermute(going_up[m], 'doc', up)  17 us
    ppermute x14, starting transfers between devices, ring_gather(): going_down[m] = lax.ppermute(going_down[m], 'doc', down)  12.2 us
    unnamed x9, local copies, waits for them, and re-layouts  6.41 us
    slice x1, local copies, waits for them, and re-layouts, add_precond(): fisher[m]  6 us
  transfers between devices with their start and end apart: 29, of which 14 were waited for; matrix products, arithmetic and copies ran while one was open for 23% of the time, Pallas kernels for 0%

profile of v1, /device:TPU:0, one launch (start us, length us, event | category | flops | bytes accessed | tf_op | source)
XLA Modules:
  0.0 149.2 jit_solution(16820230607330489605)
XLA Ops:
  1.2 3.1 %collective-permute-start = (bf16[512,384]{1,0:T(8,128)(2,1)S(1)}, bf16[512,384]{1,0:T(8,128)(2,1)}, u32[]{:S(2)}, u32[]{:S(2)}) collective-permute-start(bf16[512,384]{1,0:T(8,128)(2,1)S(1)} %get-tuple-element.7), channel_id=1, source_target_pairs={{0,4},{4,8},{8,12},{12,14},{14,10},{10,6},{6,2},{2,0},{1,5},{5,9},... | collective-permute-start | bytes 1179656 | tf_op jit(solution)/shard_map/ppermute | solution.py:39
  4.3 2.0 %collective-permute-start.7 = (bf16[512,384]{1,0:T(8,128)(2,1)S(1)}, bf16[512,384]{1,0:T(8,128)(2,1)S(1)}, u32[]{:S(2)}, u32[]{:S(2)}) collective-permute-start(bf16[512,384]{1,0:T(8,128)(2,1)S(1)} %get-tuple-element.8), channel_id=1, source_target_pairs={{0,4},{4,8},{8,12},{12,14},{14,10},{10,6},{6,2},{2,0},{1,5},{5,9},... | collective-permute-start | bytes 1179656 | tf_op jit(solution)/shard_map/ppermute | solution.py:39
  13.5 1.7 %fusion.115 = (s32[1]{0:T(128)}, s32[1]{0:T(128)}, s32[1]{0:T(128)}, s32[1]{0:T(128)}, s32[1]{0:T(128)}, /*index=5*/s32[1]{0:T(128)}, s32[1]{0:T(128)}, s32[1]{0:T(128)}, s32[1]{0:T(128)}) fusion(s32[8]{0:T(128)} %constant.185.clone, s32[]{:T(128)S(6)} %select_n.244, s32[]{:T(128)S(6)} %select_n.241, s32[]{:T(128)S(6)} %select_n.238, s32[]{:T(128)S(6)} %select_n.235, ...), kind=kLoop, calls=%fused_computation.134 | loop fusion | bytes 108 | tf_op jit(solution)/shard_map/dynamic_slice | solution.py:53
  20.7 6.0 %fusion.114 = (bf16[1,1,512,4096]{3,2,1,0:T(8,128)(2,1)}, bf16[1,1,512,4096]{3,2,1,0:T(8,128)(2,1)}) fusion(bf16[1,2,512,4096]{3,2,1,0:T(8,128)(2,1)} %param.7), kind=kLoop, calls=%fused_computation.133 | loop fusion | bytes 16777216 | tf_op jit(solution)/shard_map/slice | solution.py:59
  26.7 6.4 %copy.7 = bf16[28,8,2,4096]{3,1,2,0:T(8,128)(2,1)} copy(bf16[28,8,2,4096]{3,2,1,0:T(2,128)(2,1)} %bitcast.108) | data formatting | bytes 7340032
  33.1 1.5 fusion.36
  34.6 1.5 fusion.25
  36.2 3.3 %convolution_convert_fusion = bf16[224,8192]{1,0:T(8,128)(2,1)S(1)} fusion(bf16[224,8192]{1,0:T(8,128)(2,1)} %bitcast.107, s32[224]{0:T(256)S(1)} %bitcast.109), kind=kOutput, calls=%fused_computation | convolution fusion | flops 823968768 | bytes 7340928 | tf_op jit(solution)/shard_map/dot_general | solution.py:14
  39.5 2.0 %collective-permute-start.3 = (bf16[512,384]{1,0:T(8,128)(2,1)}, bf16[512,384]{1,0:T(8,128)(2,1)S(1)}, u32[]{:S(2)}, u32[]{:S(2)}) collective-permute-start(bf16[512,384]{1,0:T(8,128)(2,1)} %collective-permute-done.1), channel_id=1, source_target_pairs={{4,0},{8,4},{12,8},{14,12},{10,14},{6,10},{2,6},{0,2},{5,1},{9,5},... | collective-permute-start | bytes 1179656 | tf_op jit(solution)/shard_map/ppermute | solution.py:42
  41.7 2.0 %collective-permute-start.9 = (bf16[512,384]{1,0:T(8,128)(2,1)S(1)}, bf16[512,384]{1,0:T(8,128)(2,1)S(1)}, u32[]{:S(2)}, u32[]{:S(2)}) collective-permute-start(bf16[512,384]{1,0:T(8,128)(2,1)S(1)} %collective-permute-done.7), channel_id=1, source_target_pairs={{0,4},{4,8},{8,12},{12,14},{14,10},{10,6},{6,2},{2,0},{1,5},{5,9},... | collective-permute-start | bytes 1179656 | tf_op jit(solution)/shard_map/ppermute | solution.py:39
  43.6 1.4 convolution_add_fusion.9
  45.7 1.4 convolution_add_fusion.8
  47.1 1.4 convolution_add_fusion.3
  48.6 3.3 %collective-permute-done.3 = bf16[512,384]{1,0:T(8,128)(2,1)S(1)} collective-permute-done((bf16[512,384]{1,0:T(8,128)(2,1)}, bf16[512,384]{1,0:T(8,128)(2,1)S(1)}, u32[]{:S(2)}, u32[]{:S(2)}) %collective-permute-start.3) | collective-permute-done | bytes 393248 | tf_op jit(solution)/shard_map/ppermute | solution.py:42
  51.8 1.9 %collective-permute-start.5 = (bf16[512,384]{1,0:T(8,128)(2,1)S(1)}, bf16[512,384]{1,0:T(8,128)(2,1)S(1)}, u32[]{:S(2)}, u32[]{:S(2)}) collective-permute-start(bf16[512,384]{1,0:T(8,128)(2,1)S(1)} %collective-permute-done.3), channel_id=1, source_target_pairs={{4,0},{8,4},{12,8},{14,12},{10,14},{6,10},{2,6},{0,2},{5,1},{9,5},... | collective-permute-start | bytes 1179656 | tf_op jit(solution)/shard_map/ppermute | solution.py:42
  53.9 6.3 %collective-permute-done.10 = bf16[512,384]{1,0:T(8,128)(2,1)S(1)} collective-permute-done((bf16[512,384]{1,0:T(8,128)(2,1)}, bf16[512,384]{1,0:T(8,128)(2,1)S(1)}, u32[]{:S(2)}, u32[]{:S(2)}) %collective-permute-start.10) | collective-permute-done | bytes 393248 | tf_op jit(solution)/shard_map/ppermute | solution.py:42
  60.3 1.9 %collective-permute-start.12 = (bf16[512,384]{1,0:T(8,128)(2,1)S(1)}, bf16[512,384]{1,0:T(8,128)(2,1)S(1)}, u32[]{:S(2)}, u32[]{:S(2)}) collective-permute-start(bf16[512,384]{1,0:T(8,128)(2,1)S(1)} %collective-permute-done.10), channel_id=1, source_target_pairs={{4,0},{8,4},{12,8},{14,12},{10,14},{6,10},{2,6},{0,2},{5,1},{9,5},... | collective-permute-start | bytes 1179656 | tf_op jit(solution)/shard_map/ppermute | solution.py:42
  64.1 6.5 %collective-permute-done.4 = bf16[512,384]{1,0:T(8,128)(2,1)S(1)} collective-permute-done((bf16[512,384]{1,0:T(8,128)(2,1)S(1)}, bf16[512,384]{1,0:T(8,128)(2,1)S(1)}, u32[]{:S(2)}, u32[]{:S(2)}) %collective-permute-start.4) | collective-permute-done | bytes 393248 | tf_op jit(solution)/shard_map/ppermute | solution.py:39
  70.8 4.3 %collective-permute-done.12 = bf16[512,384]{1,0:T(8,128)(2,1)S(1)} collective-permute-done((bf16[512,384]{1,0:T(8,128)(2,1)S(1)}, bf16[512,384]{1,0:T(8,128)(2,1)S(1)}, u32[]{:S(2)}, u32[]{:S(2)}) %collective-permute-start.12) | collective-permute-done | bytes 393248 | tf_op jit(solution)/shard_map/ppermute | solution.py:42
  75.1 1.7 %collective-permute-start.13 = (bf16[512,384]{1,0:T(8,128)(2,1)S(1)}, bf16[512,384]{1,0:T(8,128)(2,1)S(1)}, u32[]{:S(2)}, u32[]{:S(2)}) collective-permute-start(bf16[512,384]{1,0:T(8,128)(2,1)S(1)} %collective-permute-done.12), channel_id=1, source_target_pairs={{4,0},{8,4},{12,8},{14,12},{10,14},{6,10},{2,6},{0,2},{5,1},{9,5},... | collective-permute-start | bytes 1179656 | tf_op jit(solution)/shard_map/ppermute | solution.py:42
  79.5 4.7 %collective-permute-done.13 = bf16[512,384]{1,0:T(8,128)(2,1)S(1)} collective-permute-done((bf16[512,384]{1,0:T(8,128)(2,1)S(1)}, bf16[512,384]{1,0:T(8,128)(2,1)S(1)}, u32[]{:S(2)}, u32[]{:S(2)}) %collective-permute-start.13) | collective-permute-done | bytes 393248 | tf_op jit(solution)/shard_map/ppermute | solution.py:42
  84.6 1.5 %collective-permute-start.16 = (bf16[512,384]{1,0:T(8,128)(2,1)S(1)}, bf16[512,384]{1,0:T(8,128)(2,1)S(1)}, u32[]{:S(2)}, u32[]{:S(2)}) collective-permute-start(bf16[512,384]{1,0:T(8,128)(2,1)S(1)} %fusion.5), channel_id=1, source_target_pairs={{0,4},{4,8},{8,12},{12,14},{14,10},{10,6},{6,2},{2,0},{1,5},{5,9},... | collective-permute-start | bytes 1179656 | tf_op jit(solution)/shard_map/ppermute | solution.py:39
  89.8 14.0 %collective-permute-done.15 = bf16[512,384]{1,0:T(8,128)(2,1)S(1)} collective-permute-done((bf16[512,384]{1,0:T(8,128)(2,1)S(1)}, bf16[512,384]{1,0:T(8,128)(2,1)S(1)}, u32[]{:S(2)}, u32[]{:S(2)}) %collective-permute-start.15) | collective-permute-done | bytes 393248 | tf_op jit(solution)/shard_map/ppermute | solution.py:42
  104.4 1.4 collective-permute-start.20
  107.0 1.5 %collective-permute-start.18 = (bf16[512,384]{1,0:T(8,128)(2,1)S(1)}, bf16[512,384]{1,0:T(8,128)(2,1)S(1)}, u32[]{:S(2)}, u32[]{:S(2)}) collective-permute-start(bf16[512,384]{1,0:T(8,128)(2,1)S(1)} %collective-permute-done.14), channel_id=1, source_target_pairs={{0,4},{4,8},{8,12},{12,14},{14,10},{10,6},{6,2},{2,0},{1,5},{5,9},... | collective-permute-start | bytes 1179656 | tf_op jit(solution)/shard_map/ppermute | solution.py:39
  109.1 6.8 %collective-permute-done.19 = bf16[512,384]{1,0:T(8,128)(2,1)S(1)} collective-permute-done((bf16[512,384]{1,0:T(8,128)(2,1)S(1)}, bf16[512,384]{1,0:T(8,128)(2,1)S(1)}, u32[]{:S(2)}, u32[]{:S(2)}) %collective-permute-start.19) | collective-permute-done | bytes 393248 | tf_op jit(solution)/shard_map/ppermute | solution.py:42
  116.5 5.6 %collective-permute-done.18 = bf16[512,384]{1,0:T(8,128)(2,1)S(1)} collective-permute-done((bf16[512,384]{1,0:T(8,128)(2,1)S(1)}, bf16[512,384]{1,0:T(8,128)(2,1)S(1)}, u32[]{:S(2)}, u32[]{:S(2)}) %collective-permute-start.18) | collective-permute-done | bytes 393248 | tf_op jit(solution)/shard_map/ppermute | solution.py:39
  123.3 1.9 %collective-permute-start.24 = (bf16[512,384]{1,0:T(8,128)(2,1)S(1)}, bf16[512,384]{1,0:T(8,128)(2,1)S(1)}, u32[]{:S(2)}, u32[]{:S(2)}) collective-permute-start(bf16[512,384]{1,0:T(8,128)(2,1)S(1)} %collective-permute-done.20), channel_id=1, source_target_pairs={{0,4},{4,8},{8,12},{12,14},{14,10},{10,6},{6,2},{2,0},{1,5},{5,9},... | collective-permute-start | bytes 1179656 | tf_op jit(solution)/shard_map/ppermute | solution.py:39
  126.5 7.6 %collective-permute-done.22 = bf16[512,384]{1,0:T(8,128)(2,1)S(1)} collective-permute-done((bf16[512,384]{1,0:T(8,128)(2,1)S(1)}, bf16[512,384]{1,0:T(8,128)(2,1)S(1)}, u32[]{:S(2)}, u32[]{:S(2)}) %collective-permute-start.22) | collective-permute-done | bytes 393248 | tf_op jit(solution)/shard_map/ppermute | solution.py:39
  135.3 3.1 %collective-permute-done.25 = bf16[512,384]{1,0:T(8,128)(2,1)S(1)} collective-permute-done((bf16[512,384]{1,0:T(8,128)(2,1)S(1)}, bf16[512,384]{1,0:T(8,128)(2,1)S(1)}, u32[]{:S(2)}, u32[]{:S(2)}) %collective-permute-start.25) | collective-permute-done | bytes 393248 | tf_op jit(solution)/shard_map/ppermute | solution.py:42
  140.2 5.9 %collective-permute-done.27 = bf16[512,384]{1,0:T(8,128)(2,1)S(1)} collective-permute-done((bf16[512,384]{1,0:T(8,128)(2,1)S(1)}, bf16[512,384]{1,0:T(8,128)(2,1)S(1)}, u32[]{:S(2)}, u32[]{:S(2)}) %collective-permute-start.27) | collective-permute-done | bytes 393248 | tf_op jit(solution)/shard_map/ppermute | solution.py:42
  146.8 1.6 %collective-permute-done.28 = f32[224,384]{1,0:T(8,128)S(1)} collective-permute-done((f32[224,384]{1,0:T(8,128)S(1)}, f32[224,384]{1,0:T(8,128)S(1)}, u32[]{:S(2)}, u32[]{:S(2)}) %collective-permute-start.28) | collective-permute-done | bytes 344096 | tf_op jit(solution)/shard_map/ppermute | solution.py:71
  (73 shorter events, 22.0 us)
Async XLA Ops:
  1.2 40.3 %collective-permute-start = (bf16[512,384]{1,0:T(8,128)(2,1)S(1)}, bf16[512,384]{1,0:T(8,128)(2,1)}, u32[]{:S(2)}, u32[]{:S(2)}) collective-permute-start(bf16[512,384]{1,0:T(8,128)(2,1)S(1)} %get-tuple-element.7), channel_id=1, source_target_pairs={{0,4},{4,8},{8,12},{12,14},{14,10},{10,6},{6,2},{2,0},{1,5},{5,9},... | collective-permute-start | bytes 1179656 | tf_op jit(solution)/shard_map/ppermute | solution.py:39
  4.3 35.2 %collective-permute-start.1 = (bf16[512,384]{1,0:T(8,128)(2,1)S(1)}, bf16[512,384]{1,0:T(8,128)(2,1)}, u32[]{:S(2)}, u32[]{:S(2)}) collective-permute-start(bf16[512,384]{1,0:T(8,128)(2,1)S(1)} %get-tuple-element.7), channel_id=1, source_target_pairs={{4,0},{8,4},{12,8},{14,12},{10,14},{6,10},{2,6},{0,2},{5,1},{9,5},... | collective-permute-start | bytes 1179656 | tf_op jit(solution)/shard_map/ppermute | solution.py:42
  4.3 37.4 %collective-permute-start.7 = (bf16[512,384]{1,0:T(8,128)(2,1)S(1)}, bf16[512,384]{1,0:T(8,128)(2,1)S(1)}, u32[]{:S(2)}, u32[]{:S(2)}) collective-permute-start(bf16[512,384]{1,0:T(8,128)(2,1)S(1)} %get-tuple-element.8), channel_id=1, source_target_pairs={{0,4},{4,8},{8,12},{12,14},{14,10},{10,6},{6,2},{2,0},{1,5},{5,9},... | collective-permute-start | bytes 1179656 | tf_op jit(solution)/shard_map/ppermute | solution.py:39
  6.3 39.2 %collective-permute-start.8 = (bf16[512,384]{1,0:T(8,128)(2,1)S(1)}, bf16[512,384]{1,0:T(8,128)(2,1)}, u32[]{:S(2)}, u32[]{:S(2)}) collective-permute-start(bf16[512,384]{1,0:T(8,128)(2,1)S(1)} %get-tuple-element.8), channel_id=1, source_target_pairs={{4,0},{8,4},{12,8},{14,12},{10,14},{6,10},{2,6},{0,2},{5,1},{9,5},... | collective-permute-start | bytes 1179656 | tf_op jit(solution)/shard_map/ppermute | solution.py:42
  26.7 9.5 %copy-start.3 = (s32[1,224]{1,0:T(1,128)S(1)}, s32[1,224]{1,0:T(1,128)}, u32[]{:S(2)}) copy-start(s32[1,224]{1,0:T(1,128)} %param.9) | copy-start | bytes 2692
  36.2 7.5 %copy-start = (bf16[1,1,512,4096]{3,2,1,0:T(8,128)(2,1)S(1)}, bf16[1,1,512,4096]{3,2,1,0:T(8,128)(2,1)}, u32[]{:S(2)}) copy-start(bf16[1,1,512,4096]{3,2,1,0:T(8,128)(2,1)} %get-tuple-element.5) | copy-start | bytes 12582916
  36.2 8.9 %copy-start.1 = (bf16[1,1,512,4096]{3,2,1,0:T(8,128)(2,1)S(1)}, bf16[1,1,512,4096]{3,2,1,0:T(8,128)(2,1)}, u32[]{:S(2)}) copy-start(bf16[1,1,512,4096]{3,2,1,0:T(8,128)(2,1)} %get-tuple-element.6) | copy-start | bytes 12582916
  39.5 12.3 %collective-permute-start.3 = (bf16[512,384]{1,0:T(8,128)(2,1)}, bf16[512,384]{1,0:T(8,128)(2,1)S(1)}, u32[]{:S(2)}, u32[]{:S(2)}) collective-permute-start(bf16[512,384]{1,0:T(8,128)(2,1)} %collective-permute-done.1), channel_id=1, source_target_pairs={{4,0},{8,4},{12,8},{14,12},{10,14},{6,10},{2,6},{0,2},{5,1},{9,5},... | collective-permute-start | bytes 1179656 | tf_op jit(solution)/shard_map/ppermute | solution.py:42
  41.5 12.3 %collective-permute-start.2 = (bf16[512,384]{1,0:T(8,128)(2,1)}, bf16[512,384]{1,0:T(8,128)(2,1)S(1)}, u32[]{:S(2)}, u32[]{:S(2)}) collective-permute-start(bf16[512,384]{1,0:T(8,128)(2,1)} %collective-permute-done), channel_id=1, source_target_pairs={{0,4},{4,8},{8,12},{12,14},{14,10},{10,6},{6,2},{2,0},{1,5},{5,9},... | collective-permute-start | bytes 1179656 | tf_op jit(solution)/shard_map/ppermute | solution.py:39
  41.7 21.0 %collective-permute-start.9 = (bf16[512,384]{1,0:T(8,128)(2,1)S(1)}, bf16[512,384]{1,0:T(8,128)(2,1)S(1)}, u32[]{:S(2)}, u32[]{:S(2)}) collective-permute-start(bf16[512,384]{1,0:T(8,128)(2,1)S(1)} %collective-permute-done.7), channel_id=1, source_target_pairs={{0,4},{4,8},{8,12},{12,14},{14,10},{10,6},{6,2},{2,0},{1,5},{5,9},... | collective-permute-start | bytes 1179656 | tf_op jit(solution)/shard_map/ppermute | solution.py:39
  45.5 14.7 %collective-permute-start.10 = (bf16[512,384]{1,0:T(8,128)(2,1)}, bf16[512,384]{1,0:T(8,128)(2,1)S(1)}, u32[]{:S(2)}, u32[]{:S(2)}) collective-permute-start(bf16[512,384]{1,0:T(8,128)(2,1)} %collective-permute-done.8), channel_id=1, source_target_pairs={{4,0},{8,4},{12,8},{14,12},{10,14},{6,10},{2,6},{0,2},{5,1},{9,5},... | collective-permute-start | bytes 1179656 | tf_op jit(solution)/shard_map/ppermute | solution.py:42
  51.8 24.9 %collective-permute-start.5 = (bf16[512,384]{1,0:T(8,128)(2,1)S(1)}, bf16[512,384]{1,0:T(8,128)(2,1)S(1)}, u32[]{:S(2)}, u32[]{:S(2)}) collective-permute-start(bf16[512,384]{1,0:T(8,128)(2,1)S(1)} %collective-permute-done.3), channel_id=1, source_target_pairs={{4,0},{8,4},{12,8},{14,12},{10,14},{6,10},{2,6},{0,2},{5,1},{9,5},... | collective-permute-start | bytes 1179656 | tf_op jit(solution)/shard_map/ppermute | solution.py:42
  53.8 16.9 %collective-permute-start.4 = (bf16[512,384]{1,0:T(8,128)(2,1)S(1)}, bf16[512,384]{1,0:T(8,128)(2,1)S(1)}, u32[]{:S(2)}, u32[]{:S(2)}) collective-permute-start(bf16[512,384]{1,0:T(8,128)(2,1)S(1)} %collective-permute-done.2), channel_id=1, source_target_pairs={{0,4},{4,8},{8,12},{12,14},{14,10},{10,6},{6,2},{2,0},{1,5},{5,9},... | collective-permute-start | bytes 1179656 | tf_op jit(solution)/shard_map/ppermute | solution.py:39
  60.3 14.8 %collective-permute-start.12 = (bf16[512,384]{1,0:T(8,128)(2,1)S(1)}, bf16[512,384]{1,0:T(8,128)(2,1)S(1)}, u32[]{:S(2)}, u32[]{:S(2)}) collective-permute-start(bf16[512,384]{1,0:T(8,128)(2,1)S(1)} %collective-permute-done.10), channel_id=1, source_target_pairs={{4,0},{8,4},{12,8},{14,12},{10,14},{6,10},{2,6},{0,2},{5,1},{9,5},... | collective-permute-start | bytes 1179656 | tf_op jit(solution)/shard_map/ppermute | solution.py:42
  62.7 16.4 %collective-permute-start.11 = (bf16[512,384]{1,0:T(8,128)(2,1)S(1)}, bf16[512,384]{1,0:T(8,128)(2,1)S(1)}, u32[]{:S(2)}, u32[]{:S(2)}) collective-permute-start(bf16[512,384]{1,0:T(8,128)(2,1)S(1)} %collective-permute-done.9), channel_id=1, source_target_pairs={{0,4},{4,8},{8,12},{12,14},{14,10},{10,6},{6,2},{2,0},{1,5},{5,9},... | collective-permute-start | bytes 1179656 | tf_op jit(solution)/shard_map/ppermute | solution.py:39
  70.6 16.1 %collective-permute-start.6 = (bf16[512,384]{1,0:T(8,128)(2,1)S(1)}, bf16[512,384]{1,0:T(8,128)(2,1)S(1)}, u32[]{:S(2)}, u32[]{:S(2)}) collective-permute-start(bf16[512,384]{1,0:T(8,128)(2,1)S(1)} %collective-permute-done.4), channel_id=1, source_target_pairs={{0,4},{4,8},{8,12},{12,14},{14,10},{10,6},{6,2},{2,0},{1,5},{5,9},... | collective-permute-start | bytes 1179656 | tf_op jit(solution)/shard_map/ppermute | solution.py:39
  75.1 9.1 %collective-permute-start.13 = (bf16[512,384]{1,0:T(8,128)(2,1)S(1)}, bf16[512,384]{1,0:T(8,128)(2,1)S(1)}, u32[]{:S(2)}, u32[]{:S(2)}) collective-permute-start(bf16[512,384]{1,0:T(8,128)(2,1)S(1)} %collective-permute-done.12), channel_id=1, source_target_pairs={{4,0},{8,4},{12,8},{14,12},{10,14},{6,10},{2,6},{0,2},{5,1},{9,5},... | collective-permute-start | bytes 1179656 | tf_op jit(solution)/shard_map/ppermute | solution.py:42
  84.6 19.8 %collective-permute-start.16 = (bf16[512,384]{1,0:T(8,128)(2,1)S(1)}, bf16[512,384]{1,0:T(8,128)(2,1)S(1)}, u32[]{:S(2)}, u32[]{:S(2)}) collective-permute-start(bf16[512,384]{1,0:T(8,128)(2,1)S(1)} %fusion.5), channel_id=1, source_target_pairs={{0,4},{4,8},{8,12},{12,14},{14,10},{10,6},{6,2},{2,0},{1,5},{5,9},... | collective-permute-start | bytes 1179656 | tf_op jit(solution)/shard_map/ppermute | solution.py:39
  86.1 19.7 %collective-permute-start.17 = (bf16[512,384]{1,0:T(8,128)(2,1)S(1)}, bf16[512,384]{1,0:T(8,128)(2,1)S(1)}, u32[]{:S(2)}, u32[]{:S(2)}) collective-permute-start(bf16[512,384]{1,0:T(8,128)(2,1)S(1)} %fusion.5), channel_id=1, source_target_pairs={{4,0},{8,4},{12,8},{14,12},{10,14},{6,10},{2,6},{0,2},{5,1},{9,5},... | collective-permute-start | bytes 1179656 | tf_op jit(solution)/shard_map/ppermute | solution.py:42
  87.1 16.7 %collective-permute-start.15 = (bf16[512,384]{1,0:T(8,128)(2,1)S(1)}, bf16[512,384]{1,0:T(8,128)(2,1)S(1)}, u32[]{:S(2)}, u32[]{:S(2)}) collective-permute-start(bf16[512,384]{1,0:T(8,128)(2,1)S(1)} %fusion.4), channel_id=1, source_target_pairs={{4,0},{8,4},{12,8},{14,12},{10,14},{6,10},{2,6},{0,2},{5,1},{9,5},... | collective-permute-start | bytes 1179656 | tf_op jit(solution)/shard_map/ppermute | solution.py:42
  88.6 18.4 %collective-permute-start.14 = (bf16[512,384]{1,0:T(8,128)(2,1)S(1)}, bf16[512,384]{1,0:T(8,128)(2,1)S(1)}, u32[]{:S(2)}, u32[]{:S(2)}) collective-permute-start(bf16[512,384]{1,0:T(8,128)(2,1)S(1)} %fusion.4), channel_id=1, source_target_pairs={{0,4},{4,8},{8,12},{12,14},{14,10},{10,6},{6,2},{2,0},{1,5},{5,9},... | collective-permute-start | bytes 1179656 | tf_op jit(solution)/shard_map/ppermute | solution.py:39
  103.8 12.1 %collective-permute-start.19 = (bf16[512,384]{1,0:T(8,128)(2,1)S(1)}, bf16[512,384]{1,0:T(8,128)(2,1)S(1)}, u32[]{:S(2)}, u32[]{:S(2)}) collective-permute-start(bf16[512,384]{1,0:T(8,128)(2,1)S(1)} %collective-permute-done.15), channel_id=1, source_target_pairs={{4,0},{8,4},{12,8},{14,12},{10,14},{6,10},{2,6},{0,2},{5,1},{9,5},... | collective-permute-start | bytes 1179656 | tf_op jit(solution)/shard_map/ppermute | solution.py:42
  104.4 18.9 %collective-permute-start.20 = (bf16[512,384]{1,0:T(8,128)(2,1)S(1)}, bf16[512,384]{1,0:T(8,128)(2,1)S(1)}, u32[]{:S(2)}, u32[]{:S(2)}) collective-permute-start(bf16[512,384]{1,0:T(8,128)(2,1)S(1)} %collective-permute-done.16), channel_id=1, source_target_pairs={{0,4},{4,8},{8,12},{12,14},{14,10},{10,6},{6,2},{2,0},{1,5},{5,9},... | collective-permute-start | bytes 1179656 | tf_op jit(solution)/shard_map/ppermute | solution.py:39
  105.9 19.8 %collective-permute-start.21 = (bf16[512,384]{1,0:T(8,128)(2,1)S(1)}, bf16[512,384]{1,0:T(8,128)(2,1)S(1)}, u32[]{:S(2)}, u32[]{:S(2)}) collective-permute-start(bf16[512,384]{1,0:T(8,128)(2,1)S(1)} %collective-permute-done.17), channel_id=1, source_target_pairs={{4,0},{8,4},{12,8},{14,12},{10,14},{6,10},{2,6},{0,2},{5,1},{9,5},... | collective-permute-start | bytes 1179656 | tf_op jit(solution)/shard_map/ppermute | solution.py:42
  107.0 15.1 %collective-permute-start.18 = (bf16[512,384]{1,0:T(8,128)(2,1)S(1)}, bf16[512,384]{1,0:T(8,128)(2,1)S(1)}, u32[]{:S(2)}, u32[]{:S(2)}) collective-permute-start(bf16[512,384]{1,0:T(8,128)(2,1)S(1)} %collective-permute-done.14), channel_id=1, source_target_pairs={{0,4},{4,8},{8,12},{12,14},{14,10},{10,6},{6,2},{2,0},{1,5},{5,9},... | collective-permute-start | bytes 1179656 | tf_op jit(solution)/shard_map/ppermute | solution.py:39
  115.9 23.4 %collective-permute-start.23 = (bf16[512,384]{1,0:T(8,128)(2,1)S(1)}, bf16[512,384]{1,0:T(8,128)(2,1)S(1)}, u32[]{:S(2)}, u32[]{:S(2)}) collective-permute-start(bf16[512,384]{1,0:T(8,128)(2,1)S(1)} %collective-permute-done.19), channel_id=1, source_target_pairs={{4,0},{8,4},{12,8},{14,12},{10,14},{6,10},{2,6},{0,2},{5,1},{9,5},... | collective-permute-start | bytes 1179656 | tf_op jit(solution)/shard_map/ppermute | solution.py:42
  122.1 12.1 %collective-permute-start.22 = (bf16[512,384]{1,0:T(8,128)(2,1)S(1)}, bf16[512,384]{1,0:T(8,128)(2,1)S(1)}, u32[]{:S(2)}, u32[]{:S(2)}) collective-permute-start(bf16[512,384]{1,0:T(8,128)(2,1)S(1)} %collective-permute-done.18), channel_id=1, source_target_pairs={{0,4},{4,8},{8,12},{12,14},{14,10},{10,6},{6,2},{2,0},{1,5},{5,9},... | collective-permute-start | bytes 1179656 | tf_op jit(solution)/shard_map/ppermute | solution.py:39
  123.3 16.4 %collective-permute-start.24 = (bf16[512,384]{1,0:T(8,128)(2,1)S(1)}, bf16[512,384]{1,0:T(8,128)(2,1)S(1)}, u32[]{:S(2)}, u32[]{:S(2)}) collective-permute-start(bf16[512,384]{1,0:T(8,128)(2,1)S(1)} %collective-permute-done.20), channel_id=1, source_target_pairs={{0,4},{4,8},{8,12},{12,14},{14,10},{10,6},{6,2},{2,0},{1,5},{5,9},... | collective-permute-start | bytes 1179656 | tf_op jit(solution)/shard_map/ppermute | solution.py:39
  125.7 12.7 %collective-permute-start.25 = (bf16[512,384]{1,0:T(8,128)(2,1)S(1)}, bf16[512,384]{1,0:T(8,128)(2,1)S(1)}, u32[]{:S(2)}, u32[]{:S(2)}) collective-permute-start(bf16[512,384]{1,0:T(8,128)(2,1)S(1)} %collective-permute-done.21), channel_id=1, source_target_pairs={{4,0},{8,4},{12,8},{14,12},{10,14},{6,10},{2,6},{0,2},{5,1},{9,5},... | collective-permute-start | bytes 1179656 | tf_op jit(solution)/shard_map/ppermute | solution.py:42
  134.1 12.3 %collective-permute-start.26 = (bf16[512,384]{1,0:T(8,128)(2,1)S(1)}, bf16[512,384]{1,0:T(8,128)(2,1)S(1)}, u32[]{:S(2)}, u32[]{:S(2)}) collective-permute-start(bf16[512,384]{1,0:T(8,128)(2,1)S(1)} %collective-permute-done.22), channel_id=1, source_target_pairs={{0,4},{4,8},{8,12},{12,14},{14,10},{10,6},{6,2},{2,0},{1,5},{5,9},... | collective-permute-start | bytes 1179656 | tf_op jit(solution)/shard_map/ppermute | solution.py:39
  138.4 7.8 %collective-permute-start.27 = (bf16[512,384]{1,0:T(8,128)(2,1)S(1)}, bf16[512,384]{1,0:T(8,128)(2,1)S(1)}, u32[]{:S(2)}, u32[]{:S(2)}) collective-permute-start(bf16[512,384]{1,0:T(8,128)(2,1)S(1)} %collective-permute-done.25), channel_id=1, source_target_pairs={{4,0},{8,4},{12,8},{14,12},{10,14},{6,10},{2,6},{0,2},{5,1},{9,5},... | collective-permute-start | bytes 1179656 | tf_op jit(solution)/shard_map/ppermute | solution.py:42
  146.8 1.7 %collective-permute-start.28 = (f32[224,384]{1,0:T(8,128)S(1)}, f32[224,384]{1,0:T(8,128)S(1)}, u32[]{:S(2)}, u32[]{:S(2)}) collective-permute-start(f32[224,384]{1,0:T(8,128)S(1)} %fusion.9), channel_id=1, source_target_pairs={{0,1},{1,0},{2,3},{3,2},{4,5},{5,4},{6,7},{7,6},{8,9},{9,8},{10,11... | collective-permute-start | bytes 1032200 | tf_op jit(solution)/shard_map/ppermute | solution.py:71
  (1 other events, 6.4 us)

commit v2 on v0

v2 whole, which is shorter than its diff:
```python
import functools

import jax
import jax.numpy as jnp
import numpy as np
from jax import lax
from jax.experimental import pallas as pl
from jax.experimental.pallas import tpu as pltpu
from jax.sharding import PartitionSpec as P

VMEM_LIMIT = 40 * 1024 * 1024


def dot(a, b):
    return jnp.dot(a, b, preferred_element_type=jnp.float32)


def ring_order(n):
    half = n // 2
    return [2 * i for i in range(half)] + [2 * i + 1 for i in reversed(range(half))]


def precond_kernel(count, has_acc, table, *refs):
    del table
    fisher, blocks = refs[:count], refs[count : 2 * count]
    total = refs[2 * count][...] if has_acc else None
    out = refs[-1]
    for f, block in zip(fisher, blocks):
        part = dot(f[0], block[...])
        total = part if total is None else total + part
    out[...] = total.astype(out.dtype)


def add_precond(table, fisher, m, entries, acc, dtype):
    _, depth, _ = fisher.shape
    width = entries[0][1].shape[1]
    whole = pl.BlockSpec((depth, width), lambda i, t: (0, 0))
    in_specs = [pl.BlockSpec((1, depth, depth), lambda i, t, k=k: (m, 0, t[k])) for k, _ in entries]
    in_specs += [whole] * (len(entries) + (acc is not None))
    operands = [fisher] * len(entries) + [a for _, a in entries] + ([acc] if acc is not None else [])
    return pl.pallas_call(
        functools.partial(precond_kernel, len(entries), acc is not None),
        out_shape=jax.ShapeDtypeStruct((depth, width), dtype),
        grid_spec=pltpu.PrefetchScalarGridSpec(num_scalar_prefetch=1, grid=(1,), in_specs=in_specs, out_specs=whole),
        compiler_params=pltpu.CompilerParams(vmem_limit_bytes=VMEM_LIMIT),
        cost_estimate=pl.CostEstimate(
            flops=2 * depth * depth * width * len(entries),
            bytes_accessed=depth * (depth + 2 * width) * 2 * len(entries),
            transcendentals=0,
        ),
    )(table, *operands)


def place_kernel(table, order, docs, *refs):
    del table
    out = refs[-1]
    rows = order.shape[1]
    put = jnp.where(order[...] == lax.broadcasted_iota(jnp.int32, (rows, rows), 0), 1.0, 0.0).astype(jnp.bfloat16)
    out[0] = dot(put, docs[0]).astype(out.dtype)


def place(table, order, docs, depth, after):
    modules, rows, width = docs.shape
    return pl.pallas_call(
        place_kernel,
        out_shape=jax.ShapeDtypeStruct(docs.shape, docs.dtype),
        grid_spec=pltpu.PrefetchScalarGridSpec(
            num_scalar_prefetch=1,
            grid=(modules, width // depth),
            in_specs=[pl.BlockSpec((1, rows), lambda m, i, t: (0, 0))]
            + [pl.BlockSpec((1, rows, depth), lambda m, i, t: (m, 0, t[i]))]
            + [pl.BlockSpec(memory_space=pl.ANY)] * len(after),
            out_specs=pl.BlockSpec((1, rows, depth), lambda m, i, t: (m, 0, i)),
        ),
        compiler_params=pltpu.CompilerParams(vmem_limit_bytes=VMEM_LIMIT),
        cost_estimate=pl.CostEstimate(flops=2 * docs.size * rows, bytes_accessed=4 * docs.size, transcendentals=0),
    )(table, order, docs, *after)


def per_device_plane(queries, inverse_fisher, documents, doc_order):
    fisher = inverse_fisher[0]
    modules, depth, width = fisher.shape
    n = width // depth
    ring = ring_order(n)
    up = [(ring[i], ring[(i + 1) % n]) for i in range(n)]
    down = [(b, a) for a, b in up]
    owners = np.zeros((n, n), np.int32)
    for i, d in enumerate(ring):
        owners[d] = [ring[(i - shift) % n] for shift in range(n)]
    table = jnp.asarray(owners)[lax.axis_index("doc")]
    docs = jnp.swapaxes(documents[0], 0, 1)

    def ring_gather(blocks, state, use):
        going = [[block, block] for block in blocks]
        fresh = [[(0, block)] for block in blocks]
        for step in range(1, n // 2 + 1):
            for m in range(modules):
                if step > 1:
                    going[m], state[m] = lax.optimization_barrier((going[m], state[m]))
                arrivals = []
                last = step == n // 2
                if not last or m % 2 == 0:
                    going[m][0] = lax.ppermute(going[m][0], "doc", up)
                    arrivals.append((step, going[m][0]))
                if not last or m % 2 == 1:
                    going[m][1] = lax.ppermute(going[m][1], "doc", down)
                    arrivals.append((n - step, going[m][1]))
                state[m] = use(m, state[m], fresh[m], False)
                fresh[m] = arrivals
        return [use(m, state[m], fresh[m], True) for m in range(modules)]

    third = []

    def add_query(m, acc, arrivals, last):
        third.append(arrivals[0][1])
        return add_precond(table, fisher, m, arrivals, acc, jnp.bfloat16 if last else jnp.float32)

    precond = ring_gather([queries[0, m] for m in range(modules)], [None] * modules, add_query)
    placed = place(table, doc_order, docs, depth, [third[2 * modules]])

    def add_score(m, score, arrivals, last):
        for shift, block in arrivals:
            part = dot(placed[m][:, shift * depth : (shift + 1) * depth], block)
            score = part if score is None else score + part
        return score

    score = sum(ring_gather(precond, [None] * modules, add_score))
    return score + lax.ppermute(score, "layer", [(0, 1), (1, 0)])


def per_device_any(queries, inverse_fisher, documents, doc_order):
    fisher = inverse_fisher[0]
    n_rows = documents.shape[1]
    put = (doc_order == lax.broadcasted_iota(jnp.int32, (n_rows, n_rows), 0)).astype(documents.dtype)
    placed = dot(put, documents[0].reshape(n_rows, -1)).astype(documents.dtype)
    full_queries = lax.all_gather(queries[0], "doc", axis=1, tiled=True)
    precond = jnp.einsum("mji,miq->mjq", fisher, full_queries, preferred_element_type=jnp.float32).astype(jnp.bfloat16)
    full_precond = lax.all_gather(precond, "doc", axis=1, tiled=True)
    score = dot(placed, full_precond.reshape(-1, full_precond.shape[2]))
    return lax.psum(score, "layer")


def solution(mesh):
    plane = mesh.shape["doc"] == 8 and mesh.shape["layer"] == 2
    in_specs = (
        P("layer", None, "doc", "groups"),
        P("layer", None, "doc", None),
        P("layer", ("groups", "doc"), None, None),
        P(("groups", "doc"), None),
    )
    return jax.shard_map(
        per_device_plane if plane else per_device_any,
        mesh=mesh,
        in_specs=in_specs,
        out_specs=P(("groups", "doc"), None),
        check_vma=False,
    )
```

time: 252 us -> 131 us (0.52)
  waiting for transfers between devices: 212 us -> 63.9 us
  starting transfers between devices: 0.08 us -> 29.7 us
  Pallas kernels: 0 us -> 21.7 us
  matrix products: 17.3 us -> 4.46 us
  between operations: 13.1 us -> 0.34 us
    all_gather x2 -> x0, waiting for transfers between devices: 195 us -> none  [the longest x1 104 us: per_device(): full_queries = lax.all_gather(query_slab, 'doc', axis=1, tiled=True)]
    ppermute x0 -> x29, waiting for transfers between devices: none -> 63.9 us  [the longest x14 38.9 us: ring_gather(): going[m][0] = lax.ppermute(going[m][0], 'doc', up)]
    ppermute x0 -> x29, starting transfers between devices: none -> 29.7 us  [the longest x14 24.1 us: ring_gather(): going[m][0] = lax.ppermute(going[m][0], 'doc', up)]
    pallas_call x0 -> x11, Pallas kernels: none -> 21.7 us  [the longest x10 17 us: add_precond(): pl.pallas_call(functools.partial(precond_kernel, len(entries), acc is not...]
    psum x1 -> x0, waiting for transfers between devices: 16.7 us -> none  [per_device(): total = lax.psum(layer_scores, 'layer')]
    dot_general x2 -> x16, matrix products: 17.3 us -> 4.46 us  [dot(): return jnp.dot(a, b, preferred_element_type=jnp.float32)]
    unnamed x3 -> x19, local copies, waits for them, and re-layouts: 6.4 us -> 7.79 us
  transfers between devices with their start and end apart: 3 -> 29, of which waited for: 3 -> 21; matrix products, arithmetic and copies ran while one was open for 3% -> 6% of each run, Pallas kernels for 0% -> 17%
where the time goes in v2:
time: 131 us
  waiting for transfers between devices  63.9 us (49%)
  starting transfers between devices  29.7 us (23%)
  Pallas kernels  21.7 us (17%)
  local copies, waits for them, and re-layouts  10.1 us (8%)
  matrix products  4.46 us (3%)
    ppermute x14, waiting for transfers between devices, ring_gather(): going[m][0] = lax.ppermute(going[m][0], 'doc', up)  38.9 us
    ppermute x14, starting transfers between devices, ring_gather(): going[m][0] = lax.ppermute(going[m][0], 'doc', up)  24.1 us
    ppermute x14, waiting for transfers between devices, ring_gather(): going[m][1] = lax.ppermute(going[m][1], 'doc', down)  23.4 us
    pallas_call x10, Pallas kernels, add_precond(): pl.pallas_call(functools.partial(precond_kernel, len(entries), acc is not...  17 us
    unnamed x19, local copies, waits for them, and re-layouts  7.79 us
    ppermute x14, starting transfers between devices, ring_gather(): going[m][1] = lax.ppermute(going[m][1], 'doc', down)  5.55 us
    pallas_call x1, Pallas kernels, place(): pl.pallas_call(place_kernel, out_shape=jax.ShapeDtypeStruct(docs.shape, d...  4.7 us
    dot_general x16, matrix products, dot(): return jnp.dot(a, b, preferred_element_type=jnp.float32)  4.46 us
  transfers between devices with their start and end apart: 29, of which 21 were waited for; matrix products, arithmetic and copies ran while one was open for 6% of the time, Pallas kernels for 17%

profile of v2, /device:TPU:0, one launch (start us, length us, event | category | flops | bytes accessed | tf_op | source)
XLA Modules:
  0.0 131.0 jit_solution(17840523836586185929)
XLA Ops:
  1.2 3.1 %collective-permute-start = (bf16[512,384]{1,0:T(8,128)(2,1)S(1)}, bf16[512,384]{1,0:T(8,128)(2,1)S(1)}, u32[]{:S(2)}, u32[]{:S(2)}) collective-permute-start(bf16[512,384]{1,0:T(8,128)(2,1)S(1)} %get-tuple-element.71.refs_1_), channel_id=1, source_target_pairs={{0,4},{4,8},{8,12},{12,14},{14,10},{10,6},{6,2},{2,0},{1,5},{5,9},... | collective-permute-start | bytes 1179656 | tf_op jit(solution)/shard_map/ppermute | solution.py:103
  4.3 2.0 %collective-permute-start.14 = (bf16[512,384]{1,0:T(8,128)(2,1)S(1)}, bf16[512,384]{1,0:T(8,128)(2,1)S(1)}, u32[]{:S(2)}, u32[]{:S(2)}) collective-permute-start(bf16[512,384]{1,0:T(8,128)(2,1)S(1)} %get-tuple-element.72.refs_1_), channel_id=1, source_target_pairs={{0,4},{4,8},{8,12},{12,14},{14,10},{10,6},{6,2},{2,0},{1,5},{5,9},... | collective-permute-start | bytes 1179656 | tf_op jit(solution)/shard_map/ppermute | solution.py:103
  7.0 3.4 %copy-done = bf16[1,2,512,4096]{3,2,1,0:T(8,128)(2,1)S(1)} copy-done((bf16[1,2,512,4096]{3,2,1,0:T(8,128)(2,1)S(1)}, bf16[1,2,512,4096]{3,2,1,0:T(8,128)(2,1)}, u32[]{:S(2)}) %copy-start) | copy-done | bytes 8388632
  12.3 1.8 %collective-permute-done.refs_2_ = bf16[512,384]{1,0:T(8,128)(2,1)S(1)} collective-permute-done((bf16[512,384]{1,0:T(8,128)(2,1)S(1)}, bf16[512,384]{1,0:T(8,128)(2,1)S(1)}, u32[]{:S(2)}, u32[]{:S(2)}) %collective-permute-start) | collective-permute-done | bytes 393248 | tf_op jit(solution)/shard_map/ppermute | solution.py:103
  14.1 2.3 %collective-permute-done.1.refs_3_ = bf16[512,384]{1,0:T(8,128)(2,1)} collective-permute-done((bf16[512,384]{1,0:T(8,128)(2,1)S(1)}, bf16[512,384]{1,0:T(8,128)(2,1)}, u32[]{:S(2)}, u32[]{:S(2)}) %collective-permute-start.1) | collective-permute-done | bytes 393248 | tf_op jit(solution)/shard_map/ppermute | solution.py:106
  18.4 4.1 %collective-permute-done.14.refs_2_ = bf16[512,384]{1,0:T(8,128)(2,1)S(1)} collective-permute-done((bf16[512,384]{1,0:T(8,128)(2,1)S(1)}, bf16[512,384]{1,0:T(8,128)(2,1)S(1)}, u32[]{:S(2)}, u32[]{:S(2)}) %collective-permute-start.14) | collective-permute-done | bytes 393248 | tf_op jit(solution)/shard_map/ppermute | solution.py:103
  22.6 2.2 %collective-permute-done.15.refs_3_ = bf16[512,384]{1,0:T(8,128)(2,1)S(1)} collective-permute-done((bf16[512,384]{1,0:T(8,128)(2,1)S(1)}, bf16[512,384]{1,0:T(8,128)(2,1)S(1)}, u32[]{:S(2)}, u32[]{:S(2)}) %collective-permute-start.15) | collective-permute-done | bytes 393248 | tf_op jit(solution)/shard_map/ppermute | solution.py:106
  26.8 2.2 %shard_map.56.refs_4_ = f32[512,384]{1,0:T(8,128)S(1)} custom-call(s32[8]{0:T(128)S(1)} %dynamic-slice_bitcast_fusion.table, bf16[2,512,4096]{2,1,0:T(8,128)(2,1)S(1)} %bitcast.34, bf16[2,512,4096]{2,1,0:T(8,128)(2,1)S(1)} %bitcast.35, bf16[512,384]{1,0:T(8,128)(2,1)S(1)} %collective-permute-done.refs_2_, bf16[512,384]{1,0:T(8,128)(2,1)} %collective-permute-done.1.refs_3_, ...), custom_call_target="tpu_custom_call" | custom-call | flops 402653184 | bytes 2621440 | tf_op jit(solution)/shard_map/pallas_call | solution.py:41
  31.0 2.3 %collective-permute-done.3.refs_3_ = bf16[512,384]{1,0:T(8,128)(2,1)} collective-permute-done((bf16[512,384]{1,0:T(8,128)(2,1)}, bf16[512,384]{1,0:T(8,128)(2,1)}, u32[]{:S(2)}, u32[]{:S(2)}) %collective-permute-start.3) | collective-permute-done | bytes 393248 | tf_op jit(solution)/shard_map/ppermute | solution.py:106
  35.3 4.2 %collective-permute-done.16.refs_2_ = bf16[512,384]{1,0:T(8,128)(2,1)} collective-permute-done((bf16[512,384]{1,0:T(8,128)(2,1)S(1)}, bf16[512,384]{1,0:T(8,128)(2,1)}, u32[]{:S(2)}, u32[]{:S(2)}) %collective-permute-start.16) | collective-permute-done | bytes 393248 | tf_op jit(solution)/shard_map/ppermute | solution.py:103
  39.5 2.2 %collective-permute-done.17.refs_3_ = bf16[512,384]{1,0:T(8,128)(2,1)} collective-permute-done((bf16[512,384]{1,0:T(8,128)(2,1)S(1)}, bf16[512,384]{1,0:T(8,128)(2,1)}, u32[]{:S(2)}, u32[]{:S(2)}) %collective-permute-start.17) | collective-permute-done | bytes 393248 | tf_op jit(solution)/shard_map/ppermute | solution.py:106
  43.7 2.5 %copy.8 = bf16[1,224,2,4096]{3,1,2,0:T(8,128)(2,1)S(1)} copy(bf16[1,224,2,4096]{3,2,1,0:T(2,128)(2,1)S(1)} %copy-done.6) | data formatting | bytes 7340032 | tf_op args[2]
  46.3 2.5 %shard_map.57.refs_4_ = f32[512,384]{1,0:T(8,128)S(1)} custom-call(s32[8]{0:T(128)S(1)} %dynamic-slice_bitcast_fusion.table, bf16[2,512,4096]{2,1,0:T(8,128)(2,1)S(1)} %bitcast.38, bf16[2,512,4096]{2,1,0:T(8,128)(2,1)S(1)} %bitcast.39, bf16[512,384]{1,0:T(8,128)(2,1)S(1)} %collective-permute-done.2.refs_2_.refs_0_, ...), custom_call_target="tpu_custom_call" | custom-call | flops 402653184 | bytes 2621440 | tf_op jit(solution)/shard_map/pallas_call | solution.py:41
  49.7 2.6 %shard_map.63.refs_4_ = f32[512,384]{1,0:T(8,128)S(1)} custom-call(s32[8]{0:T(128)S(1)} %dynamic-slice_bitcast_fusion.table, bf16[2,512,4096]{2,1,0:T(8,128)(2,1)S(1)} %bitcast.40, bf16[2,512,4096]{2,1,0:T(8,128)(2,1)S(1)} %bitcast.41, bf16[512,384]{1,0:T(8,128)(2,1)} %collective-permute-done.16.refs_2_, bf16[512,384]{1,0:T(8,128)(2,1)} %collective-permute-done.17.refs_3_, ...), custom_call_target="tpu_custom_call" | custom-call | flops 402653184 | bytes 2621440 | tf_op jit(solution)/shard_map/pallas_call | solution.py:41
  52.3 4.7 %shard_map.60 = bf16[2,224,4096]{2,1,0:T(8,128)(2,1)S(1)} custom-call(s32[8]{0:T(128)S(1)} %dynamic-slice_bitcast_fusion.table, s32[1,224]{1,0:T(1,128)S(1)} %copy-done.5, bf16[2,224,4096]{2,1,0:T(8,128)(2,1)S(1)} %bitcast.50, bf16[512,384]{1,0:T(8,128)(2,1)S(1)} %collective-permute-done.2.refs_2_.refs_0_), custom_call_target="tpu_custom_call" | custom-call | flops 822083584 | bytes 7340032 | tf_op jit(solution)/shard_map/pallas_call | solution.py:64
  57.0 1.6 %collective-permute-start.6 = (bf16[512,384]{1,0:T(8,128)(2,1)}, bf16[512,384]{1,0:T(8,128)(2,1)S(1)}, u32[]{:S(2)}, u32[]{:S(2)}) collective-permute-start(bf16[512,384]{1,0:T(8,128)(2,1)} %collective-permute-done.4.refs_2_), channel_id=1, source_target_pairs={{0,4},{4,8},{8,12},{12,14},{14,10},{10,6},{6,2},{2,0},{1,5},{5,9},... | collective-permute-start | bytes 1179656 | tf_op jit(solution)/shard_map/ppermute | solution.py:103
  59.7 2.2 %shard_map.58.refs_2_ = f32[512,384]{1,0:T(8,128)S(1)} custom-call(s32[8]{0:T(128)S(1)} %dynamic-slice_bitcast_fusion.table, bf16[2,512,4096]{2,1,0:T(8,128)(2,1)S(1)} %bitcast.44, bf16[2,512,4096]{2,1,0:T(8,128)(2,1)S(1)} %bitcast.45, bf16[512,384]{1,0:T(8,128)(2,1)} %collective-permute-done.4.refs_2_, bf16[512,384]{1,0:T(8,128)(2,1)S(1)} %collective-permute-done.5.refs_3_, ...), custom_call_target="tpu_custom_call" | custom-call | flops 402653184 | bytes 2621440 | tf_op jit(solution)/shard_map/pallas_call | solution.py:41
  62.9 2.2 %shard_map.64.refs_2_ = f32[512,384]{1,0:T(8,128)S(1)} custom-call(s32[8]{0:T(128)S(1)} %dynamic-slice_bitcast_fusion.table, bf16[2,512,4096]{2,1,0:T(8,128)(2,1)S(1)} %bitcast.46, bf16[2,512,4096]{2,1,0:T(8,128)(2,1)S(1)} %bitcast.47, bf16[512,384]{1,0:T(8,128)(2,1)S(1)} %copy-done.4, bf16[512,384]{1,0:T(8,128)(2,1)} %collective-permute-done.19.refs_3_, ...), custom_call_target="tpu_custom_call" | custom-call | flops 402653184 | bytes 2621440 | tf_op jit(solution)/shard_map/pallas_call | solution.py:41
  66.1 1.6 %collective-permute-start.7 = (bf16[512,384]{1,0:T(8,128)(2,1)S(1)}, bf16[512,384]{1,0:T(8,128)(2,1)S(1)}, u32[]{:S(2)}, u32[]{:S(2)}) collective-permute-start(bf16[512,384]{1,0:T(8,128)(2,1)S(1)} %shard_map.59), channel_id=1, source_target_pairs={{0,4},{4,8},{8,12},{12,14},{14,10},{10,6},{6,2},{2,0},{1,5},{5,9},... | collective-permute-start | bytes 1179656 | tf_op jit(solution)/shard_map/ppermute | solution.py:103
  69.2 1.6 %collective-permute-start.21 = (bf16[512,384]{1,0:T(8,128)(2,1)S(1)}, bf16[512,384]{1,0:T(8,128)(2,1)S(1)}, u32[]{:S(2)}, u32[]{:S(2)}) collective-permute-start(bf16[512,384]{1,0:T(8,128)(2,1)S(1)} %shard_map.65), channel_id=1, source_target_pairs={{0,4},{4,8},{8,12},{12,14},{14,10},{10,6},{6,2},{2,0},{1,5},{5,9},... | collective-permute-start | bytes 1179656 | tf_op jit(solution)/shard_map/ppermute | solution.py:103
  71.9 6.4 %collective-permute-done.7 = bf16[512,384]{1,0:T(8,128)(2,1)S(1)} collective-permute-done((bf16[512,384]{1,0:T(8,128)(2,1)S(1)}, bf16[512,384]{1,0:T(8,128)(2,1)S(1)}, u32[]{:S(2)}, u32[]{:S(2)}) %collective-permute-start.7) | collective-permute-done | bytes 393248 | tf_op jit(solution)/shard_map/ppermute | solution.py:103
  81.8 4.9 %collective-permute-done.21 = bf16[512,384]{1,0:T(8,128)(2,1)S(1)} collective-permute-done((bf16[512,384]{1,0:T(8,128)(2,1)S(1)}, bf16[512,384]{1,0:T(8,128)(2,1)S(1)}, u32[]{:S(2)}, u32[]{:S(2)}) %collective-permute-start.21) | collective-permute-done | bytes 393248 | tf_op jit(solution)/shard_map/ppermute | solution.py:103
  88.2 1.6 %collective-permute-start.23 = (bf16[512,384]{1,0:T(8,128)(2,1)S(1)}, bf16[512,384]{1,0:T(8,128)(2,1)S(1)}, u32[]{:S(2)}, u32[]{:S(2)}) collective-permute-start(bf16[512,384]{1,0:T(8,128)(2,1)S(1)} %collective-permute-done.21), channel_id=1, source_target_pairs={{0,4},{4,8},{8,12},{12,14},{14,10},{10,6},{6,2},{2,0},{1,5},{5,9},... | collective-permute-start | bytes 1179656 | tf_op jit(solution)/shard_map/ppermute | solution.py:103
  91.4 5.3 %collective-permute-done.10 = bf16[512,384]{1,0:T(8,128)(2,1)S(1)} collective-permute-done((bf16[512,384]{1,0:T(8,128)(2,1)S(1)}, bf16[512,384]{1,0:T(8,128)(2,1)S(1)}, u32[]{:S(2)}, u32[]{:S(2)}) %collective-permute-start.10) | collective-permute-done | bytes 393248 | tf_op jit(solution)/shard_map/ppermute | solution.py:106
  96.6 1.6 %collective-permute-start.11 = (bf16[512,384]{1,0:T(8,128)(2,1)S(1)}, bf16[512,384]{1,0:T(8,128)(2,1)S(1)}, u32[]{:S(2)}, u32[]{:S(2)}) collective-permute-start(bf16[512,384]{1,0:T(8,128)(2,1)S(1)} %collective-permute-done.9), channel_id=1, source_target_pairs={{0,4},{4,8},{8,12},{12,14},{14,10},{10,6},{6,2},{2,0},{1,5},{5,9},... | collective-permute-start | bytes 1179656 | tf_op jit(solution)/shard_map/ppermute | solution.py:103
  98.7 4.9 %collective-permute-done.23 = bf16[512,384]{1,0:T(8,128)(2,1)S(1)} collective-permute-done((bf16[512,384]{1,0:T(8,128)(2,1)S(1)}, bf16[512,384]{1,0:T(8,128)(2,1)S(1)}, u32[]{:S(2)}, u32[]{:S(2)}) %collective-permute-start.23) | collective-permute-done | bytes 393248 | tf_op jit(solution)/shard_map/ppermute | solution.py:103
  105.1 1.6 %collective-permute-start.25 = (bf16[512,384]{1,0:T(8,128)(2,1)S(1)}, bf16[512,384]{1,0:T(8,128)(2,1)S(1)}, u32[]{:S(2)}, u32[]{:S(2)}) collective-permute-start(bf16[512,384]{1,0:T(8,128)(2,1)S(1)} %collective-permute-done.23), channel_id=1, source_target_pairs={{0,4},{4,8},{8,12},{12,14},{14,10},{10,6},{6,2},{2,0},{1,5},{5,9},... | collective-permute-start | bytes 1179656 | tf_op jit(solution)/shard_map/ppermute | solution.py:103
  108.2 3.7 %collective-permute-done.11 = bf16[512,384]{1,0:T(8,128)(2,1)S(1)} collective-permute-done((bf16[512,384]{1,0:T(8,128)(2,1)S(1)}, bf16[512,384]{1,0:T(8,128)(2,1)S(1)}, u32[]{:S(2)}, u32[]{:S(2)}) %collective-permute-start.11) | collective-permute-done | bytes 393248 | tf_op jit(solution)/shard_map/ppermute | solution.py:103
  114.9 5.5 %collective-permute-done.25 = bf16[512,384]{1,0:T(8,128)(2,1)S(1)} collective-permute-done((bf16[512,384]{1,0:T(8,128)(2,1)S(1)}, bf16[512,384]{1,0:T(8,128)(2,1)S(1)}, u32[]{:S(2)}, u32[]{:S(2)}) %collective-permute-start.25) | collective-permute-done | bytes 393248 | tf_op jit(solution)/shard_map/ppermute | solution.py:103
  122.0 2.7 %collective-permute-done.13 = bf16[512,384]{1,0:T(8,128)(2,1)S(1)} collective-permute-done((bf16[512,384]{1,0:T(8,128)(2,1)S(1)}, bf16[512,384]{1,0:T(8,128)(2,1)S(1)}, u32[]{:S(2)}, u32[]{:S(2)}) %collective-permute-start.13) | collective-permute-done | bytes 393248 | tf_op jit(solution)/shard_map/ppermute | solution.py:103
  124.9 3.2 %collective-permute-done.27 = bf16[512,384]{1,0:T(8,128)(2,1)S(1)} collective-permute-done((bf16[512,384]{1,0:T(8,128)(2,1)S(1)}, bf16[512,384]{1,0:T(8,128)(2,1)S(1)}, u32[]{:S(2)}, u32[]{:S(2)}) %collective-permute-start.27) | collective-permute-done | bytes 393248 | tf_op jit(solution)/shard_map/ppermute | solution.py:106
  128.6 1.6 %collective-permute-done.28 = f32[224,384]{1,0:T(8,128)S(1)} collective-permute-done((f32[224,384]{1,0:T(8,128)S(1)}, f32[224,384]{1,0:T(8,128)S(1)}, u32[]{:S(2)}, u32[]{:S(2)}) %collective-permute-start.28) | collective-permute-done | bytes 344096 | tf_op jit(solution)/shard_map/ppermute | solution.py:128
  (77 shorter events, 36.3 us)
Async XLA Ops:
  1.2 12.9 %collective-permute-start = (bf16[512,384]{1,0:T(8,128)(2,1)S(1)}, bf16[512,384]{1,0:T(8,128)(2,1)S(1)}, u32[]{:S(2)}, u32[]{:S(2)}) collective-permute-start(bf16[512,384]{1,0:T(8,128)(2,1)S(1)} %get-tuple-element.71.refs_1_), channel_id=1, source_target_pairs={{0,4},{4,8},{8,12},{12,14},{14,10},{10,6},{6,2},{2,0},{1,5},{5,9},... | collective-permute-start | bytes 1179656 | tf_op jit(solution)/shard_map/ppermute | solution.py:103
  4.3 12.1 %collective-permute-start.1 = (bf16[512,384]{1,0:T(8,128)(2,1)S(1)}, bf16[512,384]{1,0:T(8,128)(2,1)}, u32[]{:S(2)}, u32[]{:S(2)}) collective-permute-start(bf16[512,384]{1,0:T(8,128)(2,1)S(1)} %get-tuple-element.71.refs_1_), channel_id=1, source_target_pairs={{4,0},{8,4},{12,8},{14,12},{10,14},{6,10},{2,6},{0,2},{5,1},{9,5},... | collective-permute-start | bytes 1179656 | tf_op jit(solution)/shard_map/ppermute | solution.py:106
  4.3 18.3 %collective-permute-start.14 = (bf16[512,384]{1,0:T(8,128)(2,1)S(1)}, bf16[512,384]{1,0:T(8,128)(2,1)S(1)}, u32[]{:S(2)}, u32[]{:S(2)}) collective-permute-start(bf16[512,384]{1,0:T(8,128)(2,1)S(1)} %get-tuple-element.72.refs_1_), channel_id=1, source_target_pairs={{0,4},{4,8},{8,12},{12,14},{14,10},{10,6},{6,2},{2,0},{1,5},{5,9},... | collective-permute-start | bytes 1179656 | tf_op jit(solution)/shard_map/ppermute | solution.py:103
  6.3 18.4 %collective-permute-start.15 = (bf16[512,384]{1,0:T(8,128)(2,1)S(1)}, bf16[512,384]{1,0:T(8,128)(2,1)S(1)}, u32[]{:S(2)}, u32[]{:S(2)}) collective-permute-start(bf16[512,384]{1,0:T(8,128)(2,1)S(1)} %get-tuple-element.72.refs_1_), channel_id=1, source_target_pairs={{4,0},{8,4},{12,8},{14,12},{10,14},{6,10},{2,6},{0,2},{5,1},{9,5},... | collective-permute-start | bytes 1179656 | tf_op jit(solution)/shard_map/ppermute | solution.py:106
  16.4 14.6 %collective-permute-start.2 = (bf16[512,384]{1,0:T(8,128)(2,1)S(1)}, bf16[512,384]{1,0:T(8,128)(2,1)S(1)}, u32[]{:S(2)}, u32[]{:S(2)}) collective-permute-start(bf16[512,384]{1,0:T(8,128)(2,1)S(1)} %collective-permute-done.refs_2_), channel_id=1, source_target_pairs={{0,4},{4,8},{8,12},{12,14},{14,10},{10,6},{6,2},{2,0},{1,5},{5,9},... | collective-permute-start | bytes 1179656 | tf_op jit(solution)/shard_map/ppermute | solution.py:103
  18.0 15.3 %collective-permute-start.3 = (bf16[512,384]{1,0:T(8,128)(2,1)}, bf16[512,384]{1,0:T(8,128)(2,1)}, u32[]{:S(2)}, u32[]{:S(2)}) collective-permute-start(bf16[512,384]{1,0:T(8,128)(2,1)} %collective-permute-done.1.refs_3_), channel_id=1, source_target_pairs={{4,0},{8,4},{12,8},{14,12},{10,14},{6,10},{2,6},{0,2},{5,1},{9,5},... | collective-permute-start | bytes 1179656 | tf_op jit(solution)/shard_map/ppermute | solution.py:106
  24.7 14.8 %collective-permute-start.16 = (bf16[512,384]{1,0:T(8,128)(2,1)S(1)}, bf16[512,384]{1,0:T(8,128)(2,1)}, u32[]{:S(2)}, u32[]{:S(2)}) collective-permute-start(bf16[512,384]{1,0:T(8,128)(2,1)S(1)} %collective-permute-done.14.refs_2_), channel_id=1, source_target_pairs={{0,4},{4,8},{8,12},{12,14},{14,10},{10,6},{6,2},{2,0},{1,5},{5,9},... | collective-permute-start | bytes 1179656 | tf_op jit(solution)/shard_map/ppermute | solution.py:103
  26.3 15.4 %collective-permute-start.17 = (bf16[512,384]{1,0:T(8,128)(2,1)S(1)}, bf16[512,384]{1,0:T(8,128)(2,1)}, u32[]{:S(2)}, u32[]{:S(2)}) collective-permute-start(bf16[512,384]{1,0:T(8,128)(2,1)S(1)} %collective-permute-done.15.refs_3_), channel_id=1, source_target_pairs={{4,0},{8,4},{12,8},{14,12},{10,14},{6,10},{2,6},{0,2},{5,1},{9,5},... | collective-permute-start | bytes 1179656 | tf_op jit(solution)/shard_map/ppermute | solution.py:106
  29.0 14.7 %copy-start.6 = (bf16[1,224,2,4096]{3,2,1,0:T(2,128)(2,1)S(1)}, bf16[1,224,2,4096]{3,2,1,0:T(2,128)(2,1)}, u32[]{:S(2)}) copy-start(bf16[1,224,2,4096]{3,2,1,0:T(2,128)(2,1)} %param.7) | copy-start | bytes 11010052
  33.3 23.8 %collective-permute-start.4 = (bf16[512,384]{1,0:T(8,128)(2,1)S(1)}, bf16[512,384]{1,0:T(8,128)(2,1)}, u32[]{:S(2)}, u32[]{:S(2)}) collective-permute-start(bf16[512,384]{1,0:T(8,128)(2,1)S(1)} %collective-permute-done.2.refs_2_.refs_0_), channel_id=1, source_target_pairs={{0,4},{4,8},{8,12},{12,14},{14,10},{10,6},{6,2},{2,0},{1,5},{5,9},... | collective-permute-start | bytes 1179656 | tf_op jit(solution)/shard_map/ppermute | solution.py:103
  34.8 22.2 %collective-permute-start.5 = (bf16[512,384]{1,0:T(8,128)(2,1)}, bf16[512,384]{1,0:T(8,128)(2,1)S(1)}, u32[]{:S(2)}, u32[]{:S(2)}) collective-permute-start(bf16[512,384]{1,0:T(8,128)(2,1)} %collective-permute-done.3.refs_3_), channel_id=1, source_target_pairs={{4,0},{8,4},{12,8},{14,12},{10,14},{6,10},{2,6},{0,2},{5,1},{9,5},... | collective-permute-start | bytes 1179656 | tf_op jit(solution)/shard_map/ppermute | solution.py:106
  41.7 16.9 %collective-permute-start.18 = (bf16[512,384]{1,0:T(8,128)(2,1)}, bf16[512,384]{1,0:T(8,128)(2,1)S(1)}, u32[]{:S(2)}, u32[]{:S(2)}) collective-permute-start(bf16[512,384]{1,0:T(8,128)(2,1)} %collective-permute-done.16.refs_2_), channel_id=1, source_target_pairs={{0,4},{4,8},{8,12},{12,14},{14,10},{10,6},{6,2},{2,0},{1,5},{5,9},... | collective-permute-start | bytes 1179656 | tf_op jit(solution)/shard_map/ppermute | solution.py:103
  43.3 15.4 %collective-permute-start.19 = (bf16[512,384]{1,0:T(8,128)(2,1)}, bf16[512,384]{1,0:T(8,128)(2,1)}, u32[]{:S(2)}, u32[]{:S(2)}) collective-permute-start(bf16[512,384]{1,0:T(8,128)(2,1)} %collective-permute-done.17.refs_3_), channel_id=1, source_target_pairs={{4,0},{8,4},{12,8},{14,12},{10,14},{6,10},{2,6},{0,2},{5,1},{9,5},... | collective-permute-start | bytes 1179656 | tf_op jit(solution)/shard_map/ppermute | solution.py:106
  46.2 13.4 %slice-start = ((s8[8388608]{0:T(1024)(128)(4,1)}), s8[4194304]{0:T(1024)(128)(4,1)S(1)}, s32[]{:S(2)}) async-start(s8[8388608]{0:T(1024)(128)(4,1)} %bitcast.42), calls=%async_computation | async-start | bytes 8388608
  49.7 10.0 %slice-start.1 = ((s8[8388608]{0:T(1024)(128)(4,1)}), s8[4194304]{0:T(1024)(128)(4,1)S(1)}, s32[]{:S(2)}) async-start(s8[8388608]{0:T(1024)(128)(4,1)} %bitcast.42), calls=%async_computation.1 | async-start | bytes 8388608
  57.0 8.1 %collective-permute-start.6 = (bf16[512,384]{1,0:T(8,128)(2,1)}, bf16[512,384]{1,0:T(8,128)(2,1)S(1)}, u32[]{:S(2)}, u32[]{:S(2)}) collective-permute-start(bf16[512,384]{1,0:T(8,128)(2,1)} %collective-permute-done.4.refs_2_), channel_id=1, source_target_pairs={{0,4},{4,8},{8,12},{12,14},{14,10},{10,6},{6,2},{2,0},{1,5},{5,9},... | collective-permute-start | bytes 1179656 | tf_op jit(solution)/shard_map/ppermute | solution.py:103
  58.7 9.6 %collective-permute-start.20 = (bf16[512,384]{1,0:T(8,128)(2,1)}, bf16[512,384]{1,0:T(8,128)(2,1)S(1)}, u32[]{:S(2)}, u32[]{:S(2)}) collective-permute-start(bf16[512,384]{1,0:T(8,128)(2,1)} %collective-permute-done.19.refs_3_), channel_id=1, source_target_pairs={{4,0},{8,4},{12,8},{14,12},{10,14},{6,10},{2,6},{0,2},{5,1},{9,5},... | collective-permute-start | bytes 1179656 | tf_op jit(solution)/shard_map/ppermute | solution.py:106
  66.1 12.1 %collective-permute-start.7 = (bf16[512,384]{1,0:T(8,128)(2,1)S(1)}, bf16[512,384]{1,0:T(8,128)(2,1)S(1)}, u32[]{:S(2)}, u32[]{:S(2)}) collective-permute-start(bf16[512,384]{1,0:T(8,128)(2,1)S(1)} %shard_map.59), channel_id=1, source_target_pairs={{0,4},{4,8},{8,12},{12,14},{14,10},{10,6},{6,2},{2,0},{1,5},{5,9},... | collective-permute-start | bytes 1179656 | tf_op jit(solution)/shard_map/ppermute | solution.py:103
  67.7 12.1 %collective-permute-start.8 = (bf16[512,384]{1,0:T(8,128)(2,1)S(1)}, bf16[512,384]{1,0:T(8,128)(2,1)S(1)}, u32[]{:S(2)}, u32[]{:S(2)}) collective-permute-start(bf16[512,384]{1,0:T(8,128)(2,1)S(1)} %shard_map.59), channel_id=1, source_target_pairs={{4,0},{8,4},{12,8},{14,12},{10,14},{6,10},{2,6},{0,2},{5,1},{9,5},... | collective-permute-start | bytes 1179656 | tf_op jit(solution)/shard_map/ppermute | solution.py:106
  69.2 17.5 %collective-permute-start.21 = (bf16[512,384]{1,0:T(8,128)(2,1)S(1)}, bf16[512,384]{1,0:T(8,128)(2,1)S(1)}, u32[]{:S(2)}, u32[]{:S(2)}) collective-permute-start(bf16[512,384]{1,0:T(8,128)(2,1)S(1)} %shard_map.65), channel_id=1, source_target_pairs={{0,4},{4,8},{8,12},{12,14},{14,10},{10,6},{6,2},{2,0},{1,5},{5,9},... | collective-permute-start | bytes 1179656 | tf_op jit(solution)/shard_map/ppermute | solution.py:103
  70.8 17.4 %collective-permute-start.22 = (bf16[512,384]{1,0:T(8,128)(2,1)S(1)}, bf16[512,384]{1,0:T(8,128)(2,1)S(1)}, u32[]{:S(2)}, u32[]{:S(2)}) collective-permute-start(bf16[512,384]{1,0:T(8,128)(2,1)S(1)} %shard_map.65), channel_id=1, source_target_pairs={{4,0},{8,4},{12,8},{14,12},{10,14},{6,10},{2,6},{0,2},{5,1},{9,5},... | collective-permute-start | bytes 1179656 | tf_op jit(solution)/shard_map/ppermute | solution.py:106
  79.8 16.9 %collective-permute-start.10 = (bf16[512,384]{1,0:T(8,128)(2,1)S(1)}, bf16[512,384]{1,0:T(8,128)(2,1)S(1)}, u32[]{:S(2)}, u32[]{:S(2)}) collective-permute-start(bf16[512,384]{1,0:T(8,128)(2,1)S(1)} %collective-permute-done.8), channel_id=1, source_target_pairs={{4,0},{8,4},{12,8},{14,12},{10,14},{6,10},{2,6},{0,2},{5,1},{9,5},... | collective-permute-start | bytes 1179656 | tf_op jit(solution)/shard_map/ppermute | solution.py:106
  80.3 16.4 %collective-permute-start.9 = (bf16[512,384]{1,0:T(8,128)(2,1)S(1)}, bf16[512,384]{1,0:T(8,128)(2,1)S(1)}, u32[]{:S(2)}, u32[]{:S(2)}) collective-permute-start(bf16[512,384]{1,0:T(8,128)(2,1)S(1)} %collective-permute-done.7), channel_id=1, source_target_pairs={{0,4},{4,8},{8,12},{12,14},{14,10},{10,6},{6,2},{2,0},{1,5},{5,9},... | collective-permute-start | bytes 1179656 | tf_op jit(solution)/shard_map/ppermute | solution.py:103
  88.2 15.3 %collective-permute-start.23 = (bf16[512,384]{1,0:T(8,128)(2,1)S(1)}, bf16[512,384]{1,0:T(8,128)(2,1)S(1)}, u32[]{:S(2)}, u32[]{:S(2)}) collective-permute-start(bf16[512,384]{1,0:T(8,128)(2,1)S(1)} %collective-permute-done.21), channel_id=1, source_target_pairs={{0,4},{4,8},{8,12},{12,14},{14,10},{10,6},{6,2},{2,0},{1,5},{5,9},... | collective-permute-start | bytes 1179656 | tf_op jit(solution)/shard_map/ppermute | solution.py:103
  89.8 15.3 %collective-permute-start.24 = (bf16[512,384]{1,0:T(8,128)(2,1)S(1)}, bf16[512,384]{1,0:T(8,128)(2,1)S(1)}, u32[]{:S(2)}, u32[]{:S(2)}) collective-permute-start(bf16[512,384]{1,0:T(8,128)(2,1)S(1)} %collective-permute-done.22), channel_id=1, source_target_pairs={{4,0},{8,4},{12,8},{14,12},{10,14},{6,10},{2,6},{0,2},{5,1},{9,5},... | collective-permute-start | bytes 1179656 | tf_op jit(solution)/shard_map/ppermute | solution.py:106
  96.6 15.3 %collective-permute-start.11 = (bf16[512,384]{1,0:T(8,128)(2,1)S(1)}, bf16[512,384]{1,0:T(8,128)(2,1)S(1)}, u32[]{:S(2)}, u32[]{:S(2)}) collective-permute-start(bf16[512,384]{1,0:T(8,128)(2,1)S(1)} %collective-permute-done.9), channel_id=1, source_target_pairs={{0,4},{4,8},{8,12},{12,14},{14,10},{10,6},{6,2},{2,0},{1,5},{5,9},... | collective-permute-start | bytes 1179656 | tf_op jit(solution)/shard_map/ppermute | solution.py:103
  98.2 15.1 %collective-permute-start.12 = (bf16[512,384]{1,0:T(8,128)(2,1)S(1)}, bf16[512,384]{1,0:T(8,128)(2,1)S(1)}, u32[]{:S(2)}, u32[]{:S(2)}) collective-permute-start(bf16[512,384]{1,0:T(8,128)(2,1)S(1)} %collective-permute-done.10), channel_id=1, source_target_pairs={{4,0},{8,4},{12,8},{14,12},{10,14},{6,10},{2,6},{0,2},{5,1},{9,5},... | collective-permute-start | bytes 1179656 | tf_op jit(solution)/shard_map/ppermute | solution.py:106
  105.1 15.3 %collective-permute-start.25 = (bf16[512,384]{1,0:T(8,128)(2,1)S(1)}, bf16[512,384]{1,0:T(8,128)(2,1)S(1)}, u32[]{:S(2)}, u32[]{:S(2)}) collective-permute-start(bf16[512,384]{1,0:T(8,128)(2,1)S(1)} %collective-permute-done.23), channel_id=1, source_target_pairs={{0,4},{4,8},{8,12},{12,14},{14,10},{10,6},{6,2},{2,0},{1,5},{5,9},... | collective-permute-start | bytes 1179656 | tf_op jit(solution)/shard_map/ppermute | solution.py:103
  106.7 13.7 %collective-permute-start.26 = (bf16[512,384]{1,0:T(8,128)(2,1)S(1)}, bf16[512,384]{1,0:T(8,128)(2,1)S(1)}, u32[]{:S(2)}, u32[]{:S(2)}) collective-permute-start(bf16[512,384]{1,0:T(8,128)(2,1)S(1)} %collective-permute-done.24), channel_id=1, source_target_pairs={{4,0},{8,4},{12,8},{14,12},{10,14},{6,10},{2,6},{0,2},{5,1},{9,5},... | collective-permute-start | bytes 1179656 | tf_op jit(solution)/shard_map/ppermute | solution.py:106
  113.3 11.3 %collective-permute-start.13 = (bf16[512,384]{1,0:T(8,128)(2,1)S(1)}, bf16[512,384]{1,0:T(8,128)(2,1)S(1)}, u32[]{:S(2)}, u32[]{:S(2)}) collective-permute-start(bf16[512,384]{1,0:T(8,128)(2,1)S(1)} %collective-permute-done.11), channel_id=1, source_target_pairs={{0,4},{4,8},{8,12},{12,14},{14,10},{10,6},{6,2},{2,0},{1,5},{5,9},... | collective-permute-start | bytes 1179656 | tf_op jit(solution)/shard_map/ppermute | solution.py:103
  120.4 7.8 %collective-permute-start.27 = (bf16[512,384]{1,0:T(8,128)(2,1)S(1)}, bf16[512,384]{1,0:T(8,128)(2,1)S(1)}, u32[]{:S(2)}, u32[]{:S(2)}) collective-permute-start(bf16[512,384]{1,0:T(8,128)(2,1)S(1)} %collective-permute-done.26), channel_id=1, source_target_pairs={{4,0},{8,4},{12,8},{14,12},{10,14},{6,10},{2,6},{0,2},{5,1},{9,5},... | collective-permute-start | bytes 1179656 | tf_op jit(solution)/shard_map/ppermute | solution.py:106
  128.5 1.7 %collective-permute-start.28 = (f32[224,384]{1,0:T(8,128)S(1)}, f32[224,384]{1,0:T(8,128)S(1)}, u32[]{:S(2)}, u32[]{:S(2)}) collective-permute-start(f32[224,384]{1,0:T(8,128)S(1)} %add_add_fusion), channel_id=1, source_target_pairs={{0,1},{1,0},{2,3},{3,2},{4,5},{5,4},{6,7},{7,6},{8,9},{9,8},{10,11... | collective-permute-start | bytes 1032200 | tf_op jit(solution)/shard_map/ppermute | solution.py:128
  (6 other events, 11.5 us)

commit v3 on v2

--- a/solution.py
+++ b/solution.py
@@ -8,7 +8,7 @@
 from jax.experimental.pallas import tpu as pltpu
 from jax.sharding import PartitionSpec as P
 
-VMEM_LIMIT = 40 * 1024 * 1024
+VMEM_LIMIT = 16 * 1024 * 1024
 
 
 def dot(a, b):
@@ -51,30 +51,30 @@
     )(table, *operands)
 
 
-def place_kernel(table, order, docs, *refs):
+def place_kernel(table, order, docs, out):
     del table
-    out = refs[-1]
     rows = order.shape[1]
     put = jnp.where(order[...] == lax.broadcasted_iota(jnp.int32, (rows, rows), 0), 1.0, 0.0).astype(jnp.bfloat16)
-    out[0] = dot(put, docs[0]).astype(out.dtype)
+    out[...] = dot(put, docs[0]).astype(out.dtype)
 
 
-def place(table, order, docs, depth, after):
-    modules, rows, width = docs.shape
+def place(table, order, docs, depth, m):
+    _, rows, width = docs.shape
     return pl.pallas_call(
         place_kernel,
-        out_shape=jax.ShapeDtypeStruct(docs.shape, docs.dtype),
+        out_shape=jax.ShapeDtypeStruct((rows, width), docs.dtype),
         grid_spec=pltpu.PrefetchScalarGridSpec(
             num_scalar_prefetch=1,
-            grid=(modules, width // depth),
-            in_specs=[pl.BlockSpec((1, rows), lambda m, i, t: (0, 0))]
-            + [pl.BlockSpec((1, rows, depth), lambda m, i, t: (m, 0, t[i]))]
-            + [pl.BlockSpec(memory_space=pl.ANY)] * len(after),
-            out_specs=pl.BlockSpec((1, rows, depth), lambda m, i, t: (m, 0, i)),
+            grid=(width // depth,),
+            in_specs=[
+                pl.BlockSpec((1, rows), lambda i, t: (0, 0)),
+                pl.BlockSpec((1, rows, depth), lambda i, t: (m, 0, t[i])),
+            ],
+            out_specs=pl.BlockSpec((rows, depth), lambda i, t: (0, i)),
         ),
         compiler_params=pltpu.CompilerParams(vmem_limit_bytes=VMEM_LIMIT),
-        cost_estimate=pl.CostEstimate(flops=2 * docs.size * rows, bytes_accessed=4 * docs.size, transcendentals=0),
-    )(table, order, docs, *after)
+        cost_estimate=pl.CostEstimate(flops=2 * rows * rows * width, bytes_accessed=4 * rows * width, transcendentals=0),
+    )(table, order, docs)
 
 
 def per_device_plane(queries, inverse_fisher, documents, doc_order):
@@ -90,13 +90,13 @@
     table = jnp.asarray(owners)[lax.axis_index("doc")]
     docs = jnp.swapaxes(documents[0], 0, 1)
 
-    def ring_gather(blocks, state, use):
+    def ring_gather(blocks, state, use, waits):
         going = [[block, block] for block in blocks]
         fresh = [[(0, block)] for block in blocks]
         for step in range(1, n // 2 + 1):
             for m in range(modules):
                 if step > 1:
-                    going[m], state[m] = lax.optimization_barrier((going[m], state[m]))
+                    going[m], state[m], _ = lax.optimization_barrier((going[m], state[m], waits.get((step, m), ())))
                 arrivals = []
                 last = step == n // 2
                 if not last or m % 2 == 0:
@@ -109,14 +109,15 @@
                 fresh[m] = arrivals
         return [use(m, state[m], fresh[m], True) for m in range(modules)]
 
-    third = []
-
     def add_query(m, acc, arrivals, last):
-        third.append(arrivals[0][1])
         return add_precond(table, fisher, m, arrivals, acc, jnp.bfloat16 if last else jnp.float32)
 
-    precond = ring_gather([queries[0, m] for m in range(modules)], [None] * modules, add_query)
-    placed = place(table, doc_order, docs, depth, [third[2 * modules]])
+    blocks = [queries[0, 0]]
+    for m in range(1, modules):
+        blocks.append(lax.optimization_barrier((queries, blocks[-1]))[0][0, m])
+    placed = [place(table, doc_order, docs, depth, m) for m in range(modules)]
+    waits = {(2, modules - 1): docs, (3, 0): placed[0], (3, modules - 1): placed[1:]}
+    precond = ring_gather(blocks, [None] * modules, add_query, waits)
 
     def add_score(m, score, arrivals, last):
         for shift, block in arrivals:
@@ -124,7 +125,7 @@
             score = part if score is None else score + part
         return score
 
-    score = sum(ring_gather(precond, [None] * modules, add_score))
+    score = sum(ring_gather(precond, [None] * modules, add_score, {}))
     return score + lax.ppermute(score, "layer", [(0, 1), (1, 0)])
 
 

time: 131 us -> 130 us (level)
  Pallas kernels: 21.7 us -> 16.6 us
  starting transfers between devices: 29.7 us -> 31.9 us
  waiting for transfers between devices: 63.9 us -> 65.3 us
    pallas_call x10, Pallas kernels: 17 us -> 11.4 us  [add_precond(): pl.pallas_call(functools.partial(precond_kernel, len(entries), acc is not...]
    ppermute x14, waiting for transfers between devices: 38.9 us -> 41.7 us  [ring_gather(): going[m][0] = lax.ppermute(going[m][0], 'doc', up)]
    ppermute x14, waiting for transfers between devices: 23.4 us -> 21.9 us  [ring_gather(): going[m][1] = lax.ppermute(going[m][1], 'doc', down)]
    pallas_call x1 -> x2, Pallas kernels: 4.7 us -> 5.19 us  [place(): pl.pallas_call(place_kernel, out_shape=jax.ShapeDtypeStruct((rows, width)...]
    unnamed x19 -> x7, local copies, waits for them, and re-layouts: 7.79 us -> 7.96 us
  transfers between devices with their start and end apart: 29 -> 29, of which waited for: 21 -> 23; matrix products, arithmetic and copies ran while one was open for 6% -> 8% of each run, Pallas kernels for 17% -> 13%
where the time goes in v3:
time: 130 us
  waiting for transfers between devices  65.3 us (50%)
  starting transfers between devices  31.9 us (25%)
  Pallas kernels  16.6 us (13%)
  local copies, waits for them, and re-layouts  10.7 us (8%)
  matrix products  4.47 us (3%)
    ppermute x14, waiting for transfers between devices, ring_gather(): going[m][0] = lax.ppermute(going[m][0], 'doc', up)  41.7 us
    ppermute x14, starting transfers between devices, ring_gather(): going[m][0] = lax.ppermute(going[m][0], 'doc', up)  25 us
    ppermute x14, waiting for transfers between devices, ring_gather(): going[m][1] = lax.ppermute(going[m][1], 'doc', down)  21.9 us
    pallas_call x10, Pallas kernels, add_precond(): pl.pallas_call(functools.partial(precond_kernel, len(entries), acc is not...  11.4 us
    unnamed x7, local copies, waits for them, and re-layouts  7.96 us
    ppermute x14, starting transfers between devices, ring_gather(): going[m][1] = lax.ppermute(going[m][1], 'doc', down)  6.84 us
    pallas_call x2, Pallas kernels, place(): pl.pallas_call(place_kernel, out_shape=jax.ShapeDtypeStruct((rows, width)...  5.19 us
    dot_general x16, matrix products, dot(): return jnp.dot(a, b, preferred_element_type=jnp.float32)  4.47 us
  transfers between devices with their start and end apart: 29, of which 23 were waited for; matrix products, arithmetic and copies ran while one was open for 8% of the time, Pallas kernels for 13%

profile of v3, /device:TPU:0, one launch (start us, length us, event | category | flops | bytes accessed | tf_op | source)
XLA Modules:
  0.0 130.0 jit_solution(11341019838726527027)
XLA Ops:
  1.0 3.1 %collective-permute-start = (bf16[512,384]{1,0:T(8,128)(2,1)S(1)}, bf16[512,384]{1,0:T(8,128)(2,1)S(1)}, u32[]{:S(2)}, u32[]{:S(2)}) collective-permute-start(bf16[512,384]{1,0:T(8,128)(2,1)S(1)} %slice_bitcast_fusion.1.refs_1_), channel_id=1, source_target_pairs={{0,4},{4,8},{8,12},{12,14},{14,10},{10,6},{6,2},{2,0},{1,5},{5,9},... | collective-permute-start | bytes 1179656 | tf_op jit(solution)/shard_map/ppermute | solution.py:103
  5.2 2.1 %collective-permute-start.14 = (bf16[512,384]{1,0:T(8,128)(2,1)S(1)}, bf16[512,384]{1,0:T(8,128)(2,1)S(1)}, u32[]{:S(2)}, u32[]{:S(2)}) collective-permute-start(bf16[512,384]{1,0:T(8,128)(2,1)S(1)} %slice_bitcast_fusion.refs_1_), channel_id=1, source_target_pairs={{0,4},{4,8},{8,12},{12,14},{14,10},{10,6},{6,2},{2,0},{1,5},{5,9},... | collective-permute-start | bytes 1179656 | tf_op jit(solution)/shard_map/ppermute | solution.py:103
  7.9 3.4 %copy-done = bf16[1,2,512,4096]{3,2,1,0:T(8,128)(2,1)S(1)} copy-done((bf16[1,2,512,4096]{3,2,1,0:T(8,128)(2,1)S(1)}, bf16[1,2,512,4096]{3,2,1,0:T(8,128)(2,1)}, u32[]{:S(2)}) %copy-start) | copy-done | bytes 8388632
  12.3 1.7 %collective-permute-done.refs_2_ = bf16[512,384]{1,0:T(8,128)(2,1)S(1)} collective-permute-done((bf16[512,384]{1,0:T(8,128)(2,1)S(1)}, bf16[512,384]{1,0:T(8,128)(2,1)S(1)}, u32[]{:S(2)}, u32[]{:S(2)}) %collective-permute-start) | collective-permute-done | bytes 393248 | tf_op jit(solution)/shard_map/ppermute | solution.py:103
  14.0 2.2 %collective-permute-done.1.refs_3_ = bf16[512,384]{1,0:T(8,128)(2,1)S(1)} collective-permute-done((bf16[512,384]{1,0:T(8,128)(2,1)S(1)}, bf16[512,384]{1,0:T(8,128)(2,1)S(1)}, u32[]{:S(2)}, u32[]{:S(2)}) %collective-permute-start.1) | collective-permute-done | bytes 393248 | tf_op jit(solution)/shard_map/ppermute | solution.py:106
  18.2 4.6 %copy.8 = bf16[1,224,2,4096]{3,1,2,0:T(8,128)(2,1)S(1)} copy(bf16[1,224,2,4096]{3,2,1,0:T(2,128)(2,1)} %param.7) | data formatting | bytes 7340032 | tf_op args[2]
  26.6 2.6 %shard_map.57 = bf16[224,4096]{1,0:T(8,128)(2,1)S(1)} custom-call(s32[8]{0:T(128)S(1)} %dynamic-slice_bitcast_fusion.table, s32[1,224]{1,0:T(1,128)S(1)} %copy-done.2, bf16[2,224,4096]{2,1,0:T(8,128)(2,1)S(1)} %bitcast.44), custom_call_target="tpu_custom_call" | custom-call | flops 411041792 | bytes 3670016 | tf_op jit(solution)/shard_map/pallas_call | solution.py:63
  29.2 2.6 %shard_map.63 = bf16[224,4096]{1,0:T(8,128)(2,1)S(1)} custom-call(s32[8]{0:T(128)S(1)} %dynamic-slice_bitcast_fusion.table, s32[1,224]{1,0:T(1,128)S(1)} %copy-done.2, bf16[2,224,4096]{2,1,0:T(8,128)(2,1)S(1)} %bitcast.45), custom_call_target="tpu_custom_call" | custom-call | flops 411041792 | bytes 3670016 | tf_op jit(solution)/shard_map/pallas_call | solution.py:63
  33.1 1.6 %collective-permute-start.4 = (bf16[512,384]{1,0:T(8,128)(2,1)S(1)}, bf16[512,384]{1,0:T(8,128)(2,1)S(1)}, u32[]{:S(2)}, u32[]{:S(2)}) collective-permute-start(bf16[512,384]{1,0:T(8,128)(2,1)S(1)} %collective-permute-done.2.refs_2_), channel_id=1, source_target_pairs={{0,4},{4,8},{8,12},{12,14},{14,10},{10,6},{6,2},{2,0},{1,5},{5,9},... | collective-permute-start | bytes 1179656 | tf_op jit(solution)/shard_map/ppermute | solution.py:103
  36.4 2.8 %collective-permute-done.16.refs_2_ = bf16[512,384]{1,0:T(8,128)(2,1)S(1)} collective-permute-done((bf16[512,384]{1,0:T(8,128)(2,1)S(1)}, bf16[512,384]{1,0:T(8,128)(2,1)S(1)}, u32[]{:S(2)}, u32[]{:S(2)}) %collective-permute-start.16) | collective-permute-done | bytes 393248 | tf_op jit(solution)/shard_map/ppermute | solution.py:103
  39.3 2.2 %collective-permute-done.17.refs_3_ = bf16[512,384]{1,0:T(8,128)(2,1)S(1)} collective-permute-done((bf16[512,384]{1,0:T(8,128)(2,1)S(1)}, bf16[512,384]{1,0:T(8,128)(2,1)S(1)}, u32[]{:S(2)}, u32[]{:S(2)}) %collective-permute-start.17) | collective-permute-done | bytes 393248 | tf_op jit(solution)/shard_map/ppermute | solution.py:106
  44.7 3.0 %collective-permute-done.4.refs_2_ = bf16[512,384]{1,0:T(8,128)(2,1)S(1)} collective-permute-done((bf16[512,384]{1,0:T(8,128)(2,1)S(1)}, bf16[512,384]{1,0:T(8,128)(2,1)S(1)}, u32[]{:S(2)}, u32[]{:S(2)}) %collective-permute-start.4) | collective-permute-done | bytes 393248 | tf_op jit(solution)/shard_map/ppermute | solution.py:103
  47.7 2.2 %collective-permute-done.5.refs_3_ = bf16[512,384]{1,0:T(8,128)(2,1)S(1)} collective-permute-done((bf16[512,384]{1,0:T(8,128)(2,1)S(1)}, bf16[512,384]{1,0:T(8,128)(2,1)S(1)}, u32[]{:S(2)}, u32[]{:S(2)}) %collective-permute-start.5) | collective-permute-done | bytes 393248 | tf_op jit(solution)/shard_map/ppermute | solution.py:106
  52.7 3.4 %collective-permute-done.18.refs_2_ = bf16[512,384]{1,0:T(8,128)(2,1)S(1)} collective-permute-done((bf16[512,384]{1,0:T(8,128)(2,1)S(1)}, bf16[512,384]{1,0:T(8,128)(2,1)S(1)}, u32[]{:S(2)}, u32[]{:S(2)}) %collective-permute-start.18) | collective-permute-done | bytes 393248 | tf_op jit(solution)/shard_map/ppermute | solution.py:103
  60.7 3.0 %collective-permute-done.6.refs_1_ = bf16[512,384]{1,0:T(8,128)(2,1)S(1)} collective-permute-done((bf16[512,384]{1,0:T(8,128)(2,1)S(1)}, bf16[512,384]{1,0:T(8,128)(2,1)S(1)}, u32[]{:S(2)}, u32[]{:S(2)}) %collective-permute-start.6) | collective-permute-done | bytes 393248 | tf_op jit(solution)/shard_map/ppermute | solution.py:103
  64.7 1.9 %collective-permute-start.7 = (bf16[512,384]{1,0:T(8,128)(2,1)S(1)}, bf16[512,384]{1,0:T(8,128)(2,1)S(1)}, u32[]{:S(2)}, u32[]{:S(2)}) collective-permute-start(bf16[512,384]{1,0:T(8,128)(2,1)S(1)} %shard_map.60), channel_id=1, source_target_pairs={{0,4},{4,8},{8,12},{12,14},{14,10},{10,6},{6,2},{2,0},{1,5},{5,9},... | collective-permute-start | bytes 1179656 | tf_op jit(solution)/shard_map/ppermute | solution.py:103
  67.8 1.9 %collective-permute-start.21 = (bf16[512,384]{1,0:T(8,128)(2,1)S(1)}, bf16[512,384]{1,0:T(8,128)(2,1)S(1)}, u32[]{:S(2)}, u32[]{:S(2)}) collective-permute-start(bf16[512,384]{1,0:T(8,128)(2,1)S(1)} %shard_map.66), channel_id=1, source_target_pairs={{0,4},{4,8},{8,12},{12,14},{14,10},{10,6},{6,2},{2,0},{1,5},{5,9},... | collective-permute-start | bytes 1179656 | tf_op jit(solution)/shard_map/ppermute | solution.py:103
  70.4 6.4 %collective-permute-done.7 = bf16[512,384]{1,0:T(8,128)(2,1)S(1)} collective-permute-done((bf16[512,384]{1,0:T(8,128)(2,1)S(1)}, bf16[512,384]{1,0:T(8,128)(2,1)S(1)}, u32[]{:S(2)}, u32[]{:S(2)}) %collective-permute-start.7) | collective-permute-done | bytes 393248 | tf_op jit(solution)/shard_map/ppermute | solution.py:103
  76.8 1.8 %collective-permute-done.8 = bf16[512,384]{1,0:T(8,128)(2,1)S(1)} collective-permute-done((bf16[512,384]{1,0:T(8,128)(2,1)S(1)}, bf16[512,384]{1,0:T(8,128)(2,1)S(1)}, u32[]{:S(2)}, u32[]{:S(2)}) %collective-permute-start.8) | collective-permute-done | bytes 393248 | tf_op jit(solution)/shard_map/ppermute | solution.py:106
  78.8 1.8 %collective-permute-start.9 = (bf16[512,384]{1,0:T(8,128)(2,1)S(1)}, bf16[512,384]{1,0:T(8,128)(2,1)S(1)}, u32[]{:S(2)}, u32[]{:S(2)}) collective-permute-start(bf16[512,384]{1,0:T(8,128)(2,1)S(1)} %collective-permute-done.7), channel_id=1, source_target_pairs={{0,4},{4,8},{8,12},{12,14},{14,10},{10,6},{6,2},{2,0},{1,5},{5,9},... | collective-permute-start | bytes 1179656 | tf_op jit(solution)/shard_map/ppermute | solution.py:103
  80.6 4.6 %collective-permute-done.21 = bf16[512,384]{1,0:T(8,128)(2,1)S(1)} collective-permute-done((bf16[512,384]{1,0:T(8,128)(2,1)S(1)}, bf16[512,384]{1,0:T(8,128)(2,1)S(1)}, u32[]{:S(2)}, u32[]{:S(2)}) %collective-permute-start.21) | collective-permute-done | bytes 393248 | tf_op jit(solution)/shard_map/ppermute | solution.py:103
  85.2 1.8 %collective-permute-done.22 = bf16[512,384]{1,0:T(8,128)(2,1)S(1)} collective-permute-done((bf16[512,384]{1,0:T(8,128)(2,1)S(1)}, bf16[512,384]{1,0:T(8,128)(2,1)S(1)}, u32[]{:S(2)}, u32[]{:S(2)}) %collective-permute-start.22) | collective-permute-done | bytes 393248 | tf_op jit(solution)/shard_map/ppermute | solution.py:106
  90.2 5.3 %collective-permute-done.10 = bf16[512,384]{1,0:T(8,128)(2,1)S(1)} collective-permute-done((bf16[512,384]{1,0:T(8,128)(2,1)S(1)}, bf16[512,384]{1,0:T(8,128)(2,1)S(1)}, u32[]{:S(2)}, u32[]{:S(2)}) %collective-permute-start.10) | collective-permute-done | bytes 393248 | tf_op jit(solution)/shard_map/ppermute | solution.py:106
  95.5 1.6 %collective-permute-start.11 = (bf16[512,384]{1,0:T(8,128)(2,1)S(1)}, bf16[512,384]{1,0:T(8,128)(2,1)S(1)}, u32[]{:S(2)}, u32[]{:S(2)}) collective-permute-start(bf16[512,384]{1,0:T(8,128)(2,1)S(1)} %collective-permute-done.9), channel_id=1, source_target_pairs={{0,4},{4,8},{8,12},{12,14},{14,10},{10,6},{6,2},{2,0},{1,5},{5,9},... | collective-permute-start | bytes 1179656 | tf_op jit(solution)/shard_map/ppermute | solution.py:103
  97.5 4.6 %collective-permute-done.23 = bf16[512,384]{1,0:T(8,128)(2,1)S(1)} collective-permute-done((bf16[512,384]{1,0:T(8,128)(2,1)S(1)}, bf16[512,384]{1,0:T(8,128)(2,1)S(1)}, u32[]{:S(2)}, u32[]{:S(2)}) %collective-permute-start.23) | collective-permute-done | bytes 393248 | tf_op jit(solution)/shard_map/ppermute | solution.py:103
  102.1 1.8 %collective-permute-done.24 = bf16[512,384]{1,0:T(8,128)(2,1)S(1)} collective-permute-done((bf16[512,384]{1,0:T(8,128)(2,1)S(1)}, bf16[512,384]{1,0:T(8,128)(2,1)S(1)}, u32[]{:S(2)}, u32[]{:S(2)}) %collective-permute-start.24) | collective-permute-done | bytes 393248 | tf_op jit(solution)/shard_map/ppermute | solution.py:106
  107.1 3.4 %collective-permute-done.11 = bf16[512,384]{1,0:T(8,128)(2,1)S(1)} collective-permute-done((bf16[512,384]{1,0:T(8,128)(2,1)S(1)}, bf16[512,384]{1,0:T(8,128)(2,1)S(1)}, u32[]{:S(2)}, u32[]{:S(2)}) %collective-permute-start.11) | collective-permute-done | bytes 393248 | tf_op jit(solution)/shard_map/ppermute | solution.py:103
  110.5 1.8 %collective-permute-done.12 = bf16[512,384]{1,0:T(8,128)(2,1)S(1)} collective-permute-done((bf16[512,384]{1,0:T(8,128)(2,1)S(1)}, bf16[512,384]{1,0:T(8,128)(2,1)S(1)}, u32[]{:S(2)}, u32[]{:S(2)}) %collective-permute-start.12) | collective-permute-done | bytes 393248 | tf_op jit(solution)/shard_map/ppermute | solution.py:106
  113.9 5.0 %collective-permute-done.25 = bf16[512,384]{1,0:T(8,128)(2,1)S(1)} collective-permute-done((bf16[512,384]{1,0:T(8,128)(2,1)S(1)}, bf16[512,384]{1,0:T(8,128)(2,1)S(1)}, u32[]{:S(2)}, u32[]{:S(2)}) %collective-permute-start.25) | collective-permute-done | bytes 393248 | tf_op jit(solution)/shard_map/ppermute | solution.py:103
  118.9 1.7 %collective-permute-start.27 = (bf16[512,384]{1,0:T(8,128)(2,1)S(1)}, bf16[512,384]{1,0:T(8,128)(2,1)S(1)}, u32[]{:S(2)}, u32[]{:S(2)}) collective-permute-start(bf16[512,384]{1,0:T(8,128)(2,1)S(1)} %collective-permute-done.26), channel_id=1, source_target_pairs={{4,0},{8,4},{12,8},{14,12},{10,14},{6,10},{2,6},{0,2},{5,1},{9,5},... | collective-permute-start | bytes 1179656 | tf_op jit(solution)/shard_map/ppermute | solution.py:106
  121.8 3.8 %collective-permute-done.13 = bf16[512,384]{1,0:T(8,128)(2,1)S(1)} collective-permute-done((bf16[512,384]{1,0:T(8,128)(2,1)S(1)}, bf16[512,384]{1,0:T(8,128)(2,1)S(1)}, u32[]{:S(2)}, u32[]{:S(2)}) %collective-permute-start.13) | collective-permute-done | bytes 393248 | tf_op jit(solution)/shard_map/ppermute | solution.py:103
  127.6 1.6 %collective-permute-done.28 = f32[224,384]{1,0:T(8,128)S(1)} collective-permute-done((f32[224,384]{1,0:T(8,128)S(1)}, f32[224,384]{1,0:T(8,128)S(1)}, u32[]{:S(2)}, u32[]{:S(2)}) %collective-permute-start.28) | collective-permute-done | bytes 344096 | tf_op jit(solution)/shard_map/ppermute | solution.py:129
  (65 shorter events, 38.4 us)
Async XLA Ops:
  1.0 12.9 %collective-permute-start = (bf16[512,384]{1,0:T(8,128)(2,1)S(1)}, bf16[512,384]{1,0:T(8,128)(2,1)S(1)}, u32[]{:S(2)}, u32[]{:S(2)}) collective-permute-start(bf16[512,384]{1,0:T(8,128)(2,1)S(1)} %slice_bitcast_fusion.1.refs_1_), channel_id=1, source_target_pairs={{0,4},{4,8},{8,12},{12,14},{14,10},{10,6},{6,2},{2,0},{1,5},{5,9},... | collective-permute-start | bytes 1179656 | tf_op jit(solution)/shard_map/ppermute | solution.py:103
  4.1 12.0 %collective-permute-start.1 = (bf16[512,384]{1,0:T(8,128)(2,1)S(1)}, bf16[512,384]{1,0:T(8,128)(2,1)S(1)}, u32[]{:S(2)}, u32[]{:S(2)}) collective-permute-start(bf16[512,384]{1,0:T(8,128)(2,1)S(1)} %slice_bitcast_fusion.1.refs_1_), channel_id=1, source_target_pairs={{4,0},{8,4},{12,8},{14,12},{10,14},{6,10},{2,6},{0,2},{5,1},{9,5},... | collective-permute-start | bytes 1179656 | tf_op jit(solution)/shard_map/ppermute | solution.py:106
  5.2 18.6 %collective-permute-start.14 = (bf16[512,384]{1,0:T(8,128)(2,1)S(1)}, bf16[512,384]{1,0:T(8,128)(2,1)S(1)}, u32[]{:S(2)}, u32[]{:S(2)}) collective-permute-start(bf16[512,384]{1,0:T(8,128)(2,1)S(1)} %slice_bitcast_fusion.refs_1_), channel_id=1, source_target_pairs={{0,4},{4,8},{8,12},{12,14},{14,10},{10,6},{6,2},{2,0},{1,5},{5,9},... | collective-permute-start | bytes 1179656 | tf_op jit(solution)/shard_map/ppermute | solution.py:103
  7.2 17.3 %collective-permute-start.15 = (bf16[512,384]{1,0:T(8,128)(2,1)S(1)}, bf16[512,384]{1,0:T(8,128)(2,1)S(1)}, u32[]{:S(2)}, u32[]{:S(2)}) collective-permute-start(bf16[512,384]{1,0:T(8,128)(2,1)S(1)} %slice_bitcast_fusion.refs_1_), channel_id=1, source_target_pairs={{4,0},{8,4},{12,8},{14,12},{10,14},{6,10},{2,6},{0,2},{5,1},{9,5},... | collective-permute-start | bytes 1179656 | tf_op jit(solution)/shard_map/ppermute | solution.py:106
  7.9 3.4 %copy-start = (bf16[1,2,512,4096]{3,2,1,0:T(8,128)(2,1)S(1)}, bf16[1,2,512,4096]{3,2,1,0:T(8,128)(2,1)}, u32[]{:S(2)}) copy-start(bf16[1,2,512,4096]{3,2,1,0:T(8,128)(2,1)} %param.6) | copy-start | bytes 25165828
  11.3 11.4 %copy-start.1 = (bf16[1,2,512,4096]{3,2,1,0:T(8,128)(2,1)S(1)}, bf16[1,2,512,4096]{3,2,1,0:T(8,128)(2,1)}, u32[]{:S(2)}) copy-start(bf16[1,2,512,4096]{3,2,1,0:T(8,128)(2,1)} %param.6) | copy-start | bytes 25165828
  16.2 16.9 %collective-permute-start.2 = (bf16[512,384]{1,0:T(8,128)(2,1)S(1)}, bf16[512,384]{1,0:T(8,128)(2,1)S(1)}, u32[]{:S(2)}, u32[]{:S(2)}) collective-permute-start(bf16[512,384]{1,0:T(8,128)(2,1)S(1)} %collective-permute-done.refs_2_), channel_id=1, source_target_pairs={{0,4},{4,8},{8,12},{12,14},{14,10},{10,6},{6,2},{2,0},{1,5},{5,9},... | collective-permute-start | bytes 1179656 | tf_op jit(solution)/shard_map/ppermute | solution.py:103
  17.7 15.4 %collective-permute-start.3 = (bf16[512,384]{1,0:T(8,128)(2,1)S(1)}, bf16[512,384]{1,0:T(8,128)(2,1)S(1)}, u32[]{:S(2)}, u32[]{:S(2)}) collective-permute-start(bf16[512,384]{1,0:T(8,128)(2,1)S(1)} %collective-permute-done.1.refs_3_), channel_id=1, source_target_pairs={{4,0},{8,4},{12,8},{14,12},{10,14},{6,10},{2,6},{0,2},{5,1},{9,5},... | collective-permute-start | bytes 1179656 | tf_op jit(solution)/shard_map/ppermute | solution.py:106
  22.8 3.8 %copy-start.2 = (s32[1,224]{1,0:T(1,128)S(1)}, s32[1,224]{1,0:T(1,128)}, u32[]{:S(2)}) copy-start(s32[1,224]{1,0:T(1,128)} %order.3) | copy-start | bytes 2692
  24.6 14.7 %collective-permute-start.16 = (bf16[512,384]{1,0:T(8,128)(2,1)S(1)}, bf16[512,384]{1,0:T(8,128)(2,1)S(1)}, u32[]{:S(2)}, u32[]{:S(2)}) collective-permute-start(bf16[512,384]{1,0:T(8,128)(2,1)S(1)} %collective-permute-done.14.refs_2_), channel_id=1, source_target_pairs={{0,4},{4,8},{8,12},{12,14},{14,10},{10,6},{6,2},{2,0},{1,5},{5,9},... | collective-permute-start | bytes 1179656 | tf_op jit(solution)/shard_map/ppermute | solution.py:103
  26.2 15.3 %collective-permute-start.17 = (bf16[512,384]{1,0:T(8,128)(2,1)S(1)}, bf16[512,384]{1,0:T(8,128)(2,1)S(1)}, u32[]{:S(2)}, u32[]{:S(2)}) collective-permute-start(bf16[512,384]{1,0:T(8,128)(2,1)S(1)} %collective-permute-done.15.refs_3_), channel_id=1, source_target_pairs={{4,0},{8,4},{12,8},{14,12},{10,14},{6,10},{2,6},{0,2},{5,1},{9,5},... | collective-permute-start | bytes 1179656 | tf_op jit(solution)/shard_map/ppermute | solution.py:106
  33.1 14.6 %collective-permute-start.4 = (bf16[512,384]{1,0:T(8,128)(2,1)S(1)}, bf16[512,384]{1,0:T(8,128)(2,1)S(1)}, u32[]{:S(2)}, u32[]{:S(2)}) collective-permute-start(bf16[512,384]{1,0:T(8,128)(2,1)S(1)} %collective-permute-done.2.refs_2_), channel_id=1, source_target_pairs={{0,4},{4,8},{8,12},{12,14},{14,10},{10,6},{6,2},{2,0},{1,5},{5,9},... | collective-permute-start | bytes 1179656 | tf_op jit(solution)/shard_map/ppermute | solution.py:103
  34.7 15.1 %collective-permute-start.5 = (bf16[512,384]{1,0:T(8,128)(2,1)S(1)}, bf16[512,384]{1,0:T(8,128)(2,1)S(1)}, u32[]{:S(2)}, u32[]{:S(2)}) collective-permute-start(bf16[512,384]{1,0:T(8,128)(2,1)S(1)} %collective-permute-done.3.refs_3_), channel_id=1, source_target_pairs={{4,0},{8,4},{12,8},{14,12},{10,14},{6,10},{2,6},{0,2},{5,1},{9,5},... | collective-permute-start | bytes 1179656 | tf_op jit(solution)/shard_map/ppermute | solution.py:106
  41.4 14.7 %collective-permute-start.18 = (bf16[512,384]{1,0:T(8,128)(2,1)S(1)}, bf16[512,384]{1,0:T(8,128)(2,1)S(1)}, u32[]{:S(2)}, u32[]{:S(2)}) collective-permute-start(bf16[512,384]{1,0:T(8,128)(2,1)S(1)} %collective-permute-done.16.refs_2_), channel_id=1, source_target_pairs={{0,4},{4,8},{8,12},{12,14},{14,10},{10,6},{6,2},{2,0},{1,5},{5,9},... | collective-permute-start | bytes 1179656 | tf_op jit(solution)/shard_map/ppermute | solution.py:103
  43.0 13.8 %collective-permute-start.19 = (bf16[512,384]{1,0:T(8,128)(2,1)S(1)}, bf16[512,384]{1,0:T(8,128)(2,1)S(1)}, u32[]{:S(2)}, u32[]{:S(2)}) collective-permute-start(bf16[512,384]{1,0:T(8,128)(2,1)S(1)} %collective-permute-done.17.refs_3_), channel_id=1, source_target_pairs={{4,0},{8,4},{12,8},{14,12},{10,14},{6,10},{2,6},{0,2},{5,1},{9,5},... | collective-permute-start | bytes 1179656 | tf_op jit(solution)/shard_map/ppermute | solution.py:106
  49.9 13.8 %collective-permute-start.6 = (bf16[512,384]{1,0:T(8,128)(2,1)S(1)}, bf16[512,384]{1,0:T(8,128)(2,1)S(1)}, u32[]{:S(2)}, u32[]{:S(2)}) collective-permute-start(bf16[512,384]{1,0:T(8,128)(2,1)S(1)} %collective-permute-done.4.refs_2_), channel_id=1, source_target_pairs={{0,4},{4,8},{8,12},{12,14},{14,10},{10,6},{6,2},{2,0},{1,5},{5,9},... | collective-permute-start | bytes 1179656 | tf_op jit(solution)/shard_map/ppermute | solution.py:103
  56.8 9.9 %collective-permute-start.20 = (bf16[512,384]{1,0:T(8,128)(2,1)S(1)}, bf16[512,384]{1,0:T(8,128)(2,1)S(1)}, u32[]{:S(2)}, u32[]{:S(2)}) collective-permute-start(bf16[512,384]{1,0:T(8,128)(2,1)S(1)} %collective-permute-done.19.refs_3_), channel_id=1, source_target_pairs={{4,0},{8,4},{12,8},{14,12},{10,14},{6,10},{2,6},{0,2},{5,1},{9,5},... | collective-permute-start | bytes 1179656 | tf_op jit(solution)/shard_map/ppermute | solution.py:106
  64.7 12.1 %collective-permute-start.7 = (bf16[512,384]{1,0:T(8,128)(2,1)S(1)}, bf16[512,384]{1,0:T(8,128)(2,1)S(1)}, u32[]{:S(2)}, u32[]{:S(2)}) collective-permute-start(bf16[512,384]{1,0:T(8,128)(2,1)S(1)} %shard_map.60), channel_id=1, source_target_pairs={{0,4},{4,8},{8,12},{12,14},{14,10},{10,6},{6,2},{2,0},{1,5},{5,9},... | collective-permute-start | bytes 1179656 | tf_op jit(solution)/shard_map/ppermute | solution.py:103
  66.6 12.1 %collective-permute-start.8 = (bf16[512,384]{1,0:T(8,128)(2,1)S(1)}, bf16[512,384]{1,0:T(8,128)(2,1)S(1)}, u32[]{:S(2)}, u32[]{:S(2)}) collective-permute-start(bf16[512,384]{1,0:T(8,128)(2,1)S(1)} %shard_map.60), channel_id=1, source_target_pairs={{4,0},{8,4},{12,8},{14,12},{10,14},{6,10},{2,6},{0,2},{5,1},{9,5},... | collective-permute-start | bytes 1179656 | tf_op jit(solution)/shard_map/ppermute | solution.py:106
  67.8 17.5 %collective-permute-start.21 = (bf16[512,384]{1,0:T(8,128)(2,1)S(1)}, bf16[512,384]{1,0:T(8,128)(2,1)S(1)}, u32[]{:S(2)}, u32[]{:S(2)}) collective-permute-start(bf16[512,384]{1,0:T(8,128)(2,1)S(1)} %shard_map.66), channel_id=1, source_target_pairs={{0,4},{4,8},{8,12},{12,14},{14,10},{10,6},{6,2},{2,0},{1,5},{5,9},... | collective-permute-start | bytes 1179656 | tf_op jit(solution)/shard_map/ppermute | solution.py:103
  69.6 17.4 %collective-permute-start.22 = (bf16[512,384]{1,0:T(8,128)(2,1)S(1)}, bf16[512,384]{1,0:T(8,128)(2,1)S(1)}, u32[]{:S(2)}, u32[]{:S(2)}) collective-permute-start(bf16[512,384]{1,0:T(8,128)(2,1)S(1)} %shard_map.66), channel_id=1, source_target_pairs={{4,0},{8,4},{12,8},{14,12},{10,14},{6,10},{2,6},{0,2},{5,1},{9,5},... | collective-permute-start | bytes 1179656 | tf_op jit(solution)/shard_map/ppermute | solution.py:106
  78.6 16.9 %collective-permute-start.10 = (bf16[512,384]{1,0:T(8,128)(2,1)S(1)}, bf16[512,384]{1,0:T(8,128)(2,1)S(1)}, u32[]{:S(2)}, u32[]{:S(2)}) collective-permute-start(bf16[512,384]{1,0:T(8,128)(2,1)S(1)} %collective-permute-done.8), channel_id=1, source_target_pairs={{4,0},{8,4},{12,8},{14,12},{10,14},{6,10},{2,6},{0,2},{5,1},{9,5},... | collective-permute-start | bytes 1179656 | tf_op jit(solution)/shard_map/ppermute | solution.py:106
  78.8 16.7 %collective-permute-start.9 = (bf16[512,384]{1,0:T(8,128)(2,1)S(1)}, bf16[512,384]{1,0:T(8,128)(2,1)S(1)}, u32[]{:S(2)}, u32[]{:S(2)}) collective-permute-start(bf16[512,384]{1,0:T(8,128)(2,1)S(1)} %collective-permute-done.7), channel_id=1, source_target_pairs={{0,4},{4,8},{8,12},{12,14},{14,10},{10,6},{6,2},{2,0},{1,5},{5,9},... | collective-permute-start | bytes 1179656 | tf_op jit(solution)/shard_map/ppermute | solution.py:103
  87.0 15.0 %collective-permute-start.23 = (bf16[512,384]{1,0:T(8,128)(2,1)S(1)}, bf16[512,384]{1,0:T(8,128)(2,1)S(1)}, u32[]{:S(2)}, u32[]{:S(2)}) collective-permute-start(bf16[512,384]{1,0:T(8,128)(2,1)S(1)} %collective-permute-done.21), channel_id=1, source_target_pairs={{0,4},{4,8},{8,12},{12,14},{14,10},{10,6},{6,2},{2,0},{1,5},{5,9},... | collective-permute-start | bytes 1179656 | tf_op jit(solution)/shard_map/ppermute | solution.py:103
  88.6 15.3 %collective-permute-start.24 = (bf16[512,384]{1,0:T(8,128)(2,1)S(1)}, bf16[512,384]{1,0:T(8,128)(2,1)S(1)}, u32[]{:S(2)}, u32[]{:S(2)}) collective-permute-start(bf16[512,384]{1,0:T(8,128)(2,1)S(1)} %collective-permute-done.22), channel_id=1, source_target_pairs={{4,0},{8,4},{12,8},{14,12},{10,14},{6,10},{2,6},{0,2},{5,1},{9,5},... | collective-permute-start | bytes 1179656 | tf_op jit(solution)/shard_map/ppermute | solution.py:106
  95.5 15.0 %collective-permute-start.11 = (bf16[512,384]{1,0:T(8,128)(2,1)S(1)}, bf16[512,384]{1,0:T(8,128)(2,1)S(1)}, u32[]{:S(2)}, u32[]{:S(2)}) collective-permute-start(bf16[512,384]{1,0:T(8,128)(2,1)S(1)} %collective-permute-done.9), channel_id=1, source_target_pairs={{0,4},{4,8},{8,12},{12,14},{14,10},{10,6},{6,2},{2,0},{1,5},{5,9},... | collective-permute-start | bytes 1179656 | tf_op jit(solution)/shard_map/ppermute | solution.py:103
  97.1 15.3 %collective-permute-start.12 = (bf16[512,384]{1,0:T(8,128)(2,1)S(1)}, bf16[512,384]{1,0:T(8,128)(2,1)S(1)}, u32[]{:S(2)}, u32[]{:S(2)}) collective-permute-start(bf16[512,384]{1,0:T(8,128)(2,1)S(1)} %collective-permute-done.10), channel_id=1, source_target_pairs={{4,0},{8,4},{12,8},{14,12},{10,14},{6,10},{2,6},{0,2},{5,1},{9,5},... | collective-permute-start | bytes 1179656 | tf_op jit(solution)/shard_map/ppermute | solution.py:106
  103.9 15.0 %collective-permute-start.25 = (bf16[512,384]{1,0:T(8,128)(2,1)S(1)}, bf16[512,384]{1,0:T(8,128)(2,1)S(1)}, u32[]{:S(2)}, u32[]{:S(2)}) collective-permute-start(bf16[512,384]{1,0:T(8,128)(2,1)S(1)} %collective-permute-done.23), channel_id=1, source_target_pairs={{0,4},{4,8},{8,12},{12,14},{14,10},{10,6},{6,2},{2,0},{1,5},{5,9},... | collective-permute-start | bytes 1179656 | tf_op jit(solution)/shard_map/ppermute | solution.py:103
  105.5 13.5 %collective-permute-start.26 = (bf16[512,384]{1,0:T(8,128)(2,1)S(1)}, bf16[512,384]{1,0:T(8,128)(2,1)S(1)}, u32[]{:S(2)}, u32[]{:S(2)}) collective-permute-start(bf16[512,384]{1,0:T(8,128)(2,1)S(1)} %collective-permute-done.24), channel_id=1, source_target_pairs={{4,0},{8,4},{12,8},{14,12},{10,14},{6,10},{2,6},{0,2},{5,1},{9,5},... | collective-permute-start | bytes 1179656 | tf_op jit(solution)/shard_map/ppermute | solution.py:106
  112.3 13.3 %collective-permute-start.13 = (bf16[512,384]{1,0:T(8,128)(2,1)S(1)}, bf16[512,384]{1,0:T(8,128)(2,1)S(1)}, u32[]{:S(2)}, u32[]{:S(2)}) collective-permute-start(bf16[512,384]{1,0:T(8,128)(2,1)S(1)} %collective-permute-done.11), channel_id=1, source_target_pairs={{0,4},{4,8},{8,12},{12,14},{14,10},{10,6},{6,2},{2,0},{1,5},{5,9},... | collective-permute-start | bytes 1179656 | tf_op jit(solution)/shard_map/ppermute | solution.py:103
  118.9 8.3 %collective-permute-start.27 = (bf16[512,384]{1,0:T(8,128)(2,1)S(1)}, bf16[512,384]{1,0:T(8,128)(2,1)S(1)}, u32[]{:S(2)}, u32[]{:S(2)}) collective-permute-start(bf16[512,384]{1,0:T(8,128)(2,1)S(1)} %collective-permute-done.26), channel_id=1, source_target_pairs={{4,0},{8,4},{12,8},{14,12},{10,14},{6,10},{2,6},{0,2},{5,1},{9,5},... | collective-permute-start | bytes 1179656 | tf_op jit(solution)/shard_map/ppermute | solution.py:106
  127.5 1.7 %collective-permute-start.28 = (f32[224,384]{1,0:T(8,128)S(1)}, f32[224,384]{1,0:T(8,128)S(1)}, u32[]{:S(2)}, u32[]{:S(2)}) collective-permute-start(f32[224,384]{1,0:T(8,128)S(1)} %add_add_fusion), channel_id=1, source_target_pairs={{0,1},{1,0},{2,3},{3,2},{4,5},{5,4},{6,7},{7,6},{8,9},{9,8},{10,11... | collective-permute-start | bytes 1032200 | tf_op jit(solution)/shard_map/ppermute | solution.py:129

commit v4 on v3

--- a/solution.py
+++ b/solution.py
@@ -33,11 +33,14 @@
 
 def add_precond(table, fisher, m, entries, acc, dtype):
     _, depth, _ = fisher.shape
-    width = entries[0][1].shape[1]
+    width = entries[0][2].shape[1]
     whole = pl.BlockSpec((depth, width), lambda i, t: (0, 0))
-    in_specs = [pl.BlockSpec((1, depth, depth), lambda i, t, k=k: (m, 0, t[k])) for k, _ in entries]
-    in_specs += [whole] * (len(entries) + (acc is not None))
-    operands = [fisher] * len(entries) + [a for _, a in entries] + ([acc] if acc is not None else [])
+    in_specs = [
+        pl.BlockSpec((1, depth, b.shape[0]), lambda i, t, k=k, h=h, parts=depth // b.shape[0]: (m, 0, t[k] * parts + h))
+        for k, h, b in entries
+    ]
+    in_specs += [pl.BlockSpec(b.shape, lambda i, t: (0, 0)) for _, _, b in entries] + [whole] * (acc is not None)
+    operands = [fisher] * len(entries) + [b for _, _, b in entries] + ([acc] if acc is not None else [])
     return pl.pallas_call(
         functools.partial(precond_kernel, len(entries), acc is not None),
         out_shape=jax.ShapeDtypeStruct((depth, width), dtype),
@@ -92,22 +95,29 @@
 
     def ring_gather(blocks, state, use, waits):
         going = [[block, block] for block in blocks]
-        fresh = [[(0, block)] for block in blocks]
+        fresh = [[(0, 0, block)] for block in blocks]
+        final = []
         for step in range(1, n // 2 + 1):
             for m in range(modules):
                 if step > 1:
                     going[m], state[m], _ = lax.optimization_barrier((going[m], state[m], waits.get((step, m), ())))
-                arrivals = []
-                last = step == n // 2
-                if not last or m % 2 == 0:
-                    going[m][0] = lax.ppermute(going[m][0], "doc", up)
-                    arrivals.append((step, going[m][0]))
-                if not last or m % 2 == 1:
-                    going[m][1] = lax.ppermute(going[m][1], "doc", down)
-                    arrivals.append((n - step, going[m][1]))
-                state[m] = use(m, state[m], fresh[m], False)
-                fresh[m] = arrivals
-        return [use(m, state[m], fresh[m], True) for m in range(modules)]
+                ways = going[m]
+                if step == n // 2:
+                    half = ways[0].shape[0] // 2
+                    ways = [ways[0][:half], ways[1][half:]]
+                going[m] = [lax.ppermute(ways[0], "doc", up), lax.ppermute(ways[1], "doc", down)]
+                arrivals = [(step, 0, going[m][0]), (n - step, step // (n // 2), going[m][1])]
+                if step < n // 2:
+                    state[m] = use(m, state[m], fresh[m], False)
+                    fresh[m] = arrivals
+                else:
+                    final.append(arrivals)
+        for m in range(modules):
+            if m > 0:
+                blocks, _ = lax.optimization_barrier(([block for _, _, block in fresh[m]], state[m - 1]))
+                fresh[m] = [(shift, half, block) for (shift, half, _), block in zip(fresh[m], blocks)]
+            state[m] = use(m, use(m, state[m], fresh[m], False), final[m], True)
+        return state
 
     def add_query(m, acc, arrivals, last):
         return add_precond(table, fisher, m, arrivals, acc, jnp.bfloat16 if last else jnp.float32)
@@ -120,8 +130,10 @@
     precond = ring_gather(blocks, [None] * modules, add_query, waits)
 
     def add_score(m, score, arrivals, last):
-        for shift, block in arrivals:
-            part = dot(placed[m][:, shift * depth : (shift + 1) * depth], block)
+        for shift, half, block in arrivals:
+            rows = block.shape[0]
+            start = shift * depth + half * rows
+            part = dot(placed[m][:, start : start + rows], block)
             score = part if score is None else score + part
         return score
 

time: 130 us -> 130 us (level)
  waiting for transfers between devices: 65.3 us -> 62 us
  starting transfers between devices: 31.9 us -> 34.1 us
    ppermute x28 -> x32, waiting for transfers between devices: 63.7 us -> 60.4 us  [the longest x16 36.3 us: ring_gather(): lax.ppermute(ways[0], 'doc', up)]
    ppermute x28 -> x32, starting transfers between devices: 31.8 us -> 34 us  [the longest x16 27.5 us: ring_gather(): lax.ppermute(ways[0], 'doc', up)]
    dot_general x16 -> x18, matrix products: 4.47 us -> 4.71 us  [dot(): return jnp.dot(a, b, preferred_element_type=jnp.float32)]
  transfers between devices with their start and end apart: 29 -> 33, of which waited for: 23 -> 28; matrix products, arithmetic and copies ran while one was open for 8% -> 8% of each run, Pallas kernels for 13% -> 13%
where the time goes in v4:
time: 130 us; the launch traced here: 129 us
  waiting for transfers between devices  62 us (48%)
  starting transfers between devices  34.1 us (26%)
  Pallas kernels  16.6 us (13%)
  local copies, waits for them, and re-layouts  10.9 us (8%)
  matrix products  4.71 us (4%)
    ppermute x16, waiting for transfers between devices, ring_gather(): lax.ppermute(ways[0], 'doc', up)  36.3 us
    ppermute x16, starting transfers between devices, ring_gather(): lax.ppermute(ways[0], 'doc', up)  27.5 us
    ppermute x16, waiting for transfers between devices, ring_gather(): lax.ppermute(ways[1], 'doc', down)  24.1 us
    pallas_call x10, Pallas kernels, add_precond(): pl.pallas_call(functools.partial(precond_kernel, len(entries), acc is not...  11.4 us
    unnamed x7, local copies, waits for them, and re-layouts  7.96 us
    ppermute x16, starting transfers between devices, ring_gather(): lax.ppermute(ways[1], 'doc', down)  6.5 us
    pallas_call x2, Pallas kernels, place(): pl.pallas_call(place_kernel, out_shape=jax.ShapeDtypeStruct((rows, width)...  5.2 us
    dot_general x18, matrix products, dot(): return jnp.dot(a, b, preferred_element_type=jnp.float32)  4.71 us
  transfers between devices with their start and end apart: 33, of which 28 were waited for; matrix products, arithmetic and copies ran while one was open for 8% of the time, Pallas kernels for 13%

profile of v4, /device:TPU:0, one launch (start us, length us, event | category | flops | bytes accessed | tf_op | source)
XLA Modules:
  0.0 129.4 jit_solution(5859167626308540937)
XLA Ops:
  1.0 3.1 %collective-permute-start = (bf16[512,384]{1,0:T(8,128)(2,1)S(1)}, bf16[512,384]{1,0:T(8,128)(2,1)S(1)}, u32[]{:S(2)}, u32[]{:S(2)}) collective-permute-start(bf16[512,384]{1,0:T(8,128)(2,1)S(1)} %slice_bitcast_fusion.1.refs_1_), channel_id=1, source_target_pairs={{0,4},{4,8},{8,12},{12,14},{14,10},{10,6},{6,2},{2,0},{1,5},{5,9},... | collective-permute-start | bytes 1179656 | tf_op jit(solution)/shard_map/ppermute | solution.py:108
  5.2 2.1 %collective-permute-start.16 = (bf16[512,384]{1,0:T(8,128)(2,1)S(1)}, bf16[512,384]{1,0:T(8,128)(2,1)S(1)}, u32[]{:S(2)}, u32[]{:S(2)}) collective-permute-start(bf16[512,384]{1,0:T(8,128)(2,1)S(1)} %slice_bitcast_fusion.refs_1_), channel_id=1, source_target_pairs={{0,4},{4,8},{8,12},{12,14},{14,10},{10,6},{6,2},{2,0},{1,5},{5,9},... | collective-permute-start | bytes 1179656 | tf_op jit(solution)/shard_map/ppermute | solution.py:108
  7.9 3.4 %copy-done = bf16[1,2,512,4096]{3,2,1,0:T(8,128)(2,1)S(1)} copy-done((bf16[1,2,512,4096]{3,2,1,0:T(8,128)(2,1)S(1)}, bf16[1,2,512,4096]{3,2,1,0:T(8,128)(2,1)}, u32[]{:S(2)}) %copy-start) | copy-done | bytes 8388632
  12.3 1.7 %collective-permute-done.refs_2_ = bf16[512,384]{1,0:T(8,128)(2,1)S(1)} collective-permute-done((bf16[512,384]{1,0:T(8,128)(2,1)S(1)}, bf16[512,384]{1,0:T(8,128)(2,1)S(1)}, u32[]{:S(2)}, u32[]{:S(2)}) %collective-permute-start) | collective-permute-done | bytes 393248 | tf_op jit(solution)/shard_map/ppermute | solution.py:108
  14.0 2.2 %collective-permute-done.1.refs_3_ = bf16[512,384]{1,0:T(8,128)(2,1)S(1)} collective-permute-done((bf16[512,384]{1,0:T(8,128)(2,1)S(1)}, bf16[512,384]{1,0:T(8,128)(2,1)S(1)}, u32[]{:S(2)}, u32[]{:S(2)}) %collective-permute-start.1) | collective-permute-done | bytes 393248 | tf_op jit(solution)/shard_map/ppermute | solution.py:108
  16.2 1.6 %collective-permute-start.2 = (bf16[512,384]{1,0:T(8,128)(2,1)S(1)}, bf16[512,384]{1,0:T(8,128)(2,1)S(1)}, u32[]{:S(2)}, u32[]{:S(2)}) collective-permute-start(bf16[512,384]{1,0:T(8,128)(2,1)S(1)} %collective-permute-done.refs_2_), channel_id=1, source_target_pairs={{0,4},{4,8},{8,12},{12,14},{14,10},{10,6},{6,2},{2,0},{1,5},{5,9},... | collective-permute-start | bytes 1179656 | tf_op jit(solution)/shard_map/ppermute | solution.py:108
  18.2 4.6 %copy.8 = bf16[1,224,2,4096]{3,1,2,0:T(8,128)(2,1)S(1)} copy(bf16[1,224,2,4096]{3,2,1,0:T(2,128)(2,1)} %param.7) | data formatting | bytes 7340032 | tf_op args[2]
  24.6 1.6 %collective-permute-start.18 = (bf16[512,384]{1,0:T(8,128)(2,1)S(1)}, bf16[512,384]{1,0:T(8,128)(2,1)S(1)}, u32[]{:S(2)}, u32[]{:S(2)}) collective-permute-start(bf16[512,384]{1,0:T(8,128)(2,1)S(1)} %collective-permute-done.16.refs_2_), channel_id=1, source_target_pairs={{0,4},{4,8},{8,12},{12,14},{14,10},{10,6},{6,2},{2,0},{1,5},{5,9},... | collective-permute-start | bytes 1179656 | tf_op jit(solution)/shard_map/ppermute | solution.py:108
  26.6 2.6 %shard_map.57 = bf16[224,4096]{1,0:T(8,128)(2,1)S(1)} custom-call(s32[8]{0:T(128)S(1)} %dynamic-slice_bitcast_fusion.table, s32[1,224]{1,0:T(1,128)S(1)} %copy-done.2, bf16[2,224,4096]{2,1,0:T(8,128)(2,1)S(1)} %bitcast.48), custom_call_target="tpu_custom_call" | custom-call | flops 411041792 | bytes 3670016 | tf_op jit(solution)/shard_map/pallas_call | solution.py:66
  30.8 2.2 %collective-permute-done.3.refs_3_ = bf16[512,384]{1,0:T(8,128)(2,1)S(1)} collective-permute-done((bf16[512,384]{1,0:T(8,128)(2,1)S(1)}, bf16[512,384]{1,0:T(8,128)(2,1)S(1)}, u32[]{:S(2)}, u32[]{:S(2)}) %collective-permute-start.3) | collective-permute-done | bytes 393248 | tf_op jit(solution)/shard_map/ppermute | solution.py:108
  33.0 1.6 %collective-permute-start.4 = (bf16[512,384]{1,0:T(8,128)(2,1)S(1)}, bf16[512,384]{1,0:T(8,128)(2,1)S(1)}, u32[]{:S(2)}, u32[]{:S(2)}) collective-permute-start(bf16[512,384]{1,0:T(8,128)(2,1)S(1)} %collective-permute-done.2.refs_2_), channel_id=1, source_target_pairs={{0,4},{4,8},{8,12},{12,14},{14,10},{10,6},{6,2},{2,0},{1,5},{5,9},... | collective-permute-start | bytes 1179656 | tf_op jit(solution)/shard_map/ppermute | solution.py:108
  35.0 2.6 %shard_map.63 = bf16[224,4096]{1,0:T(8,128)(2,1)S(1)} custom-call(s32[8]{0:T(128)S(1)} %dynamic-slice_bitcast_fusion.table, s32[1,224]{1,0:T(1,128)S(1)} %copy-done.2, bf16[2,224,4096]{2,1,0:T(8,128)(2,1)S(1)} %bitcast.49), custom_call_target="tpu_custom_call" | custom-call | flops 411041792 | bytes 3670016 | tf_op jit(solution)/shard_map/pallas_call | solution.py:66
  39.3 2.2 %collective-permute-done.19.refs_3_ = bf16[512,384]{1,0:T(8,128)(2,1)S(1)} collective-permute-done((bf16[512,384]{1,0:T(8,128)(2,1)S(1)}, bf16[512,384]{1,0:T(8,128)(2,1)S(1)}, u32[]{:S(2)}, u32[]{:S(2)}) %collective-permute-start.19) | collective-permute-done | bytes 393248 | tf_op jit(solution)/shard_map/ppermute | solution.py:108
  44.7 3.0 %collective-permute-done.4.refs_2_ = bf16[512,384]{1,0:T(8,128)(2,1)S(1)} collective-permute-done((bf16[512,384]{1,0:T(8,128)(2,1)S(1)}, bf16[512,384]{1,0:T(8,128)(2,1)S(1)}, u32[]{:S(2)}, u32[]{:S(2)}) %collective-permute-start.4) | collective-permute-done | bytes 393248 | tf_op jit(solution)/shard_map/ppermute | solution.py:108
  47.7 2.2 %collective-permute-done.5.refs_3_ = bf16[512,384]{1,0:T(8,128)(2,1)S(1)} collective-permute-done((bf16[512,384]{1,0:T(8,128)(2,1)S(1)}, bf16[512,384]{1,0:T(8,128)(2,1)S(1)}, u32[]{:S(2)}, u32[]{:S(2)}) %collective-permute-start.5) | collective-permute-done | bytes 393248 | tf_op jit(solution)/shard_map/ppermute | solution.py:108
  49.9 1.6 %collective-permute-start.6 = (bf16[256,384]{1,0:T(8,128)(2,1)S(1)}, bf16[256,384]{1,0:T(8,128)(2,1)S(1)}, u32[]{:S(2)}, u32[]{:S(2)}) collective-permute-start(bf16[256,384]{1,0:T(8,128)(2,1)S(1)} %slice.85), channel_id=1, source_target_pairs={{0,4},{4,8},{8,12},{12,14},{14,10},{10,6},{6,2},{2,0},{1,5},{5,9},... | collective-permute-start | bytes 589832 | tf_op jit(solution)/shard_map/ppermute | solution.py:108
  53.3 2.8 %collective-permute-done.20.refs_2_ = bf16[512,384]{1,0:T(8,128)(2,1)S(1)} collective-permute-done((bf16[512,384]{1,0:T(8,128)(2,1)S(1)}, bf16[512,384]{1,0:T(8,128)(2,1)S(1)}, u32[]{:S(2)}, u32[]{:S(2)}) %collective-permute-start.20) | collective-permute-done | bytes 393248 | tf_op jit(solution)/shard_map/ppermute | solution.py:108
  56.1 2.2 %collective-permute-done.21.refs_3_ = bf16[512,384]{1,0:T(8,128)(2,1)S(1)} collective-permute-done((bf16[512,384]{1,0:T(8,128)(2,1)S(1)}, bf16[512,384]{1,0:T(8,128)(2,1)S(1)}, u32[]{:S(2)}, u32[]{:S(2)}) %collective-permute-start.21) | collective-permute-done | bytes 393248 | tf_op jit(solution)/shard_map/ppermute | solution.py:108
  58.3 1.6 %collective-permute-start.22 = (bf16[256,384]{1,0:T(8,128)(2,1)S(1)}, bf16[256,384]{1,0:T(8,128)(2,1)S(1)}, u32[]{:S(2)}, u32[]{:S(2)}) collective-permute-start(bf16[256,384]{1,0:T(8,128)(2,1)S(1)} %slice.99), channel_id=1, source_target_pairs={{0,4},{4,8},{8,12},{12,14},{14,10},{10,6},{6,2},{2,0},{1,5},{5,9},... | collective-permute-start | bytes 589832 | tf_op jit(solution)/shard_map/ppermute | solution.py:108
  63.5 1.6 %collective-permute-start.8 = (bf16[512,384]{1,0:T(8,128)(2,1)S(1)}, bf16[512,384]{1,0:T(8,128)(2,1)S(1)}, u32[]{:S(2)}, u32[]{:S(2)}) collective-permute-start(bf16[512,384]{1,0:T(8,128)(2,1)S(1)} %shard_map.60), channel_id=1, source_target_pairs={{0,4},{4,8},{8,12},{12,14},{14,10},{10,6},{6,2},{2,0},{1,5},{5,9},... | collective-permute-start | bytes 1179656 | tf_op jit(solution)/shard_map/ppermute | solution.py:108
  67.8 1.6 %collective-permute-start.24 = (bf16[512,384]{1,0:T(8,128)(2,1)S(1)}, bf16[512,384]{1,0:T(8,128)(2,1)S(1)}, u32[]{:S(2)}, u32[]{:S(2)}) collective-permute-start(bf16[512,384]{1,0:T(8,128)(2,1)S(1)} %shard_map.66), channel_id=1, source_target_pairs={{0,4},{4,8},{8,12},{12,14},{14,10},{10,6},{6,2},{2,0},{1,5},{5,9},... | collective-permute-start | bytes 1179656 | tf_op jit(solution)/shard_map/ppermute | solution.py:108
  70.5 5.1 %collective-permute-done.8 = bf16[512,384]{1,0:T(8,128)(2,1)S(1)} collective-permute-done((bf16[512,384]{1,0:T(8,128)(2,1)S(1)}, bf16[512,384]{1,0:T(8,128)(2,1)S(1)}, u32[]{:S(2)}, u32[]{:S(2)}) %collective-permute-start.8) | collective-permute-done | bytes 393248 | tf_op jit(solution)/shard_map/ppermute | solution.py:108
  79.2 4.8 %collective-permute-done.24 = bf16[512,384]{1,0:T(8,128)(2,1)S(1)} collective-permute-done((bf16[512,384]{1,0:T(8,128)(2,1)S(1)}, bf16[512,384]{1,0:T(8,128)(2,1)S(1)}, u32[]{:S(2)}, u32[]{:S(2)}) %collective-permute-start.24) | collective-permute-done | bytes 393248 | tf_op jit(solution)/shard_map/ppermute | solution.py:108
  88.8 3.7 %collective-permute-done.10 = bf16[512,384]{1,0:T(8,128)(2,1)S(1)} collective-permute-done((bf16[512,384]{1,0:T(8,128)(2,1)S(1)}, bf16[512,384]{1,0:T(8,128)(2,1)S(1)}, u32[]{:S(2)}, u32[]{:S(2)}) %collective-permute-start.10) | collective-permute-done | bytes 393248 | tf_op jit(solution)/shard_map/ppermute | solution.py:108
  96.0 4.8 %collective-permute-done.26 = bf16[512,384]{1,0:T(8,128)(2,1)S(1)} collective-permute-done((bf16[512,384]{1,0:T(8,128)(2,1)S(1)}, bf16[512,384]{1,0:T(8,128)(2,1)S(1)}, u32[]{:S(2)}, u32[]{:S(2)}) %collective-permute-start.26) | collective-permute-done | bytes 393248 | tf_op jit(solution)/shard_map/ppermute | solution.py:108
  105.6 3.7 %collective-permute-done.12 = bf16[512,384]{1,0:T(8,128)(2,1)S(1)} collective-permute-done((bf16[512,384]{1,0:T(8,128)(2,1)S(1)}, bf16[512,384]{1,0:T(8,128)(2,1)S(1)}, u32[]{:S(2)}, u32[]{:S(2)}) %collective-permute-start.12) | collective-permute-done | bytes 393248 | tf_op jit(solution)/shard_map/ppermute | solution.py:108
  110.9 1.6 %collective-permute-start.14 = (bf16[256,384]{1,0:T(8,128)(2,1)S(1)}, bf16[256,384]{1,0:T(8,128)(2,1)S(1)}, u32[]{:S(2)}, u32[]{:S(2)}) collective-permute-start(bf16[256,384]{1,0:T(8,128)(2,1)S(1)} %slice.95), channel_id=1, source_target_pairs={{0,4},{4,8},{8,12},{12,14},{14,10},{10,6},{6,2},{2,0},{1,5},{5,9},... | collective-permute-start | bytes 589832 | tf_op jit(solution)/shard_map/ppermute | solution.py:108
  113.0 4.3 %collective-permute-done.28 = bf16[512,384]{1,0:T(8,128)(2,1)S(1)} collective-permute-done((bf16[512,384]{1,0:T(8,128)(2,1)S(1)}, bf16[512,384]{1,0:T(8,128)(2,1)S(1)}, u32[]{:S(2)}, u32[]{:S(2)}) %collective-permute-start.28) | collective-permute-done | bytes 393248 | tf_op jit(solution)/shard_map/ppermute | solution.py:108
  117.4 1.9 %collective-permute-done.29 = bf16[512,384]{1,0:T(8,128)(2,1)S(1)} collective-permute-done((bf16[512,384]{1,0:T(8,128)(2,1)S(1)}, bf16[512,384]{1,0:T(8,128)(2,1)S(1)}, u32[]{:S(2)}, u32[]{:S(2)}) %collective-permute-start.29) | collective-permute-done | bytes 393248 | tf_op jit(solution)/shard_map/ppermute | solution.py:108
  119.3 1.6 %collective-permute-start.30 = (bf16[256,384]{1,0:T(8,128)(2,1)S(1)}, bf16[256,384]{1,0:T(8,128)(2,1)S(1)}, u32[]{:S(2)}, u32[]{:S(2)}) collective-permute-start(bf16[256,384]{1,0:T(8,128)(2,1)S(1)} %slice.109), channel_id=1, source_target_pairs={{0,4},{4,8},{8,12},{12,14},{14,10},{10,6},{6,2},{2,0},{1,5},{5,9},... | collective-permute-start | bytes 589832 | tf_op jit(solution)/shard_map/ppermute | solution.py:108
  123.3 1.7 %collective-permute-done.30 = bf16[256,384]{1,0:T(8,128)(2,1)S(1)} collective-permute-done((bf16[256,384]{1,0:T(8,128)(2,1)S(1)}, bf16[256,384]{1,0:T(8,128)(2,1)S(1)}, u32[]{:S(2)}, u32[]{:S(2)}) %collective-permute-start.30) | collective-permute-done | bytes 196640 | tf_op jit(solution)/shard_map/ppermute | solution.py:108
  127.0 1.6 %collective-permute-done.32 = f32[224,384]{1,0:T(8,128)S(1)} collective-permute-done((f32[224,384]{1,0:T(8,128)S(1)}, f32[224,384]{1,0:T(8,128)S(1)}, u32[]{:S(2)}, u32[]{:S(2)}) %collective-permute-start.32) | collective-permute-done | bytes 344096 | tf_op jit(solution)/shard_map/ppermute | solution.py:141
  (83 shorter events, 46.2 us)
Async XLA Ops:
  1.0 12.9 %collective-permute-start = (bf16[512,384]{1,0:T(8,128)(2,1)S(1)}, bf16[512,384]{1,0:T(8,128)(2,1)S(1)}, u32[]{:S(2)}, u32[]{:S(2)}) collective-permute-start(bf16[512,384]{1,0:T(8,128)(2,1)S(1)} %slice_bitcast_fusion.1.refs_1_), channel_id=1, source_target_pairs={{0,4},{4,8},{8,12},{12,14},{14,10},{10,6},{6,2},{2,0},{1,5},{5,9},... | collective-permute-start | bytes 1179656 | tf_op jit(solution)/shard_map/ppermute | solution.py:108
  4.1 12.0 %collective-permute-start.1 = (bf16[512,384]{1,0:T(8,128)(2,1)S(1)}, bf16[512,384]{1,0:T(8,128)(2,1)S(1)}, u32[]{:S(2)}, u32[]{:S(2)}) collective-permute-start(bf16[512,384]{1,0:T(8,128)(2,1)S(1)} %slice_bitcast_fusion.1.refs_1_), channel_id=1, source_target_pairs={{4,0},{8,4},{12,8},{14,12},{10,14},{6,10},{2,6},{0,2},{5,1},{9,5},... | collective-permute-start | bytes 1179656 | tf_op jit(solution)/shard_map/ppermute | solution.py:108
  5.2 18.6 %collective-permute-start.16 = (bf16[512,384]{1,0:T(8,128)(2,1)S(1)}, bf16[512,384]{1,0:T(8,128)(2,1)S(1)}, u32[]{:S(2)}, u32[]{:S(2)}) collective-permute-start(bf16[512,384]{1,0:T(8,128)(2,1)S(1)} %slice_bitcast_fusion.refs_1_), channel_id=1, source_target_pairs={{0,4},{4,8},{8,12},{12,14},{14,10},{10,6},{6,2},{2,0},{1,5},{5,9},... | collective-permute-start | bytes 1179656 | tf_op jit(solution)/shard_map/ppermute | solution.py:108
  7.2 17.3 %collective-permute-start.17 = (bf16[512,384]{1,0:T(8,128)(2,1)S(1)}, bf16[512,384]{1,0:T(8,128)(2,1)S(1)}, u32[]{:S(2)}, u32[]{:S(2)}) collective-permute-start(bf16[512,384]{1,0:T(8,128)(2,1)S(1)} %slice_bitcast_fusion.refs_1_), channel_id=1, source_target_pairs={{4,0},{8,4},{12,8},{14,12},{10,14},{6,10},{2,6},{0,2},{5,1},{9,5},... | collective-permute-start | bytes 1179656 | tf_op jit(solution)/shard_map/ppermute | solution.py:108
  16.2 14.7 %collective-permute-start.2 = (bf16[512,384]{1,0:T(8,128)(2,1)S(1)}, bf16[512,384]{1,0:T(8,128)(2,1)S(1)}, u32[]{:S(2)}, u32[]{:S(2)}) collective-permute-start(bf16[512,384]{1,0:T(8,128)(2,1)S(1)} %collective-permute-done.refs_2_), channel_id=1, source_target_pairs={{0,4},{4,8},{8,12},{12,14},{14,10},{10,6},{6,2},{2,0},{1,5},{5,9},... | collective-permute-start | bytes 1179656 | tf_op jit(solution)/shard_map/ppermute | solution.py:108
  17.7 15.3 %collective-permute-start.3 = (bf16[512,384]{1,0:T(8,128)(2,1)S(1)}, bf16[512,384]{1,0:T(8,128)(2,1)S(1)}, u32[]{:S(2)}, u32[]{:S(2)}) collective-permute-start(bf16[512,384]{1,0:T(8,128)(2,1)S(1)} %collective-permute-done.1.refs_3_), channel_id=1, source_target_pairs={{4,0},{8,4},{12,8},{14,12},{10,14},{6,10},{2,6},{0,2},{5,1},{9,5},... | collective-permute-start | bytes 1179656 | tf_op jit(solution)/shard_map/ppermute | solution.py:108
  24.6 14.7 %collective-permute-start.18 = (bf16[512,384]{1,0:T(8,128)(2,1)S(1)}, bf16[512,384]{1,0:T(8,128)(2,1)S(1)}, u32[]{:S(2)}, u32[]{:S(2)}) collective-permute-start(bf16[512,384]{1,0:T(8,128)(2,1)S(1)} %collective-permute-done.16.refs_2_), channel_id=1, source_target_pairs={{0,4},{4,8},{8,12},{12,14},{14,10},{10,6},{6,2},{2,0},{1,5},{5,9},... | collective-permute-start | bytes 1179656 | tf_op jit(solution)/shard_map/ppermute | solution.py:108
  26.2 15.3 %collective-permute-start.19 = (bf16[512,384]{1,0:T(8,128)(2,1)S(1)}, bf16[512,384]{1,0:T(8,128)(2,1)S(1)}, u32[]{:S(2)}, u32[]{:S(2)}) collective-permute-start(bf16[512,384]{1,0:T(8,128)(2,1)S(1)} %collective-permute-done.17.refs_3_), channel_id=1, source_target_pairs={{4,0},{8,4},{12,8},{14,12},{10,14},{6,10},{2,6},{0,2},{5,1},{9,5},... | collective-permute-start | bytes 1179656 | tf_op jit(solution)/shard_map/ppermute | solution.py:108
  33.0 14.7 %collective-permute-start.4 = (bf16[512,384]{1,0:T(8,128)(2,1)S(1)}, bf16[512,384]{1,0:T(8,128)(2,1)S(1)}, u32[]{:S(2)}, u32[]{:S(2)}) collective-permute-start(bf16[512,384]{1,0:T(8,128)(2,1)S(1)} %collective-permute-done.2.refs_2_), channel_id=1, source_target_pairs={{0,4},{4,8},{8,12},{12,14},{14,10},{10,6},{6,2},{2,0},{1,5},{5,9},... | collective-permute-start | bytes 1179656 | tf_op jit(solution)/shard_map/ppermute | solution.py:108
  34.6 15.3 %collective-permute-start.5 = (bf16[512,384]{1,0:T(8,128)(2,1)S(1)}, bf16[512,384]{1,0:T(8,128)(2,1)S(1)}, u32[]{:S(2)}, u32[]{:S(2)}) collective-permute-start(bf16[512,384]{1,0:T(8,128)(2,1)S(1)} %collective-permute-done.3.refs_3_), channel_id=1, source_target_pairs={{4,0},{8,4},{12,8},{14,12},{10,14},{6,10},{2,6},{0,2},{5,1},{9,5},... | collective-permute-start | bytes 1179656 | tf_op jit(solution)/shard_map/ppermute | solution.py:108
  41.4 14.7 %collective-permute-start.20 = (bf16[512,384]{1,0:T(8,128)(2,1)S(1)}, bf16[512,384]{1,0:T(8,128)(2,1)S(1)}, u32[]{:S(2)}, u32[]{:S(2)}) collective-permute-start(bf16[512,384]{1,0:T(8,128)(2,1)S(1)} %collective-permute-done.18.refs_2_), channel_id=1, source_target_pairs={{0,4},{4,8},{8,12},{12,14},{14,10},{10,6},{6,2},{2,0},{1,5},{5,9},... | collective-permute-start | bytes 1179656 | tf_op jit(solution)/shard_map/ppermute | solution.py:108
  43.0 15.3 %collective-permute-start.21 = (bf16[512,384]{1,0:T(8,128)(2,1)S(1)}, bf16[512,384]{1,0:T(8,128)(2,1)S(1)}, u32[]{:S(2)}, u32[]{:S(2)}) collective-permute-start(bf16[512,384]{1,0:T(8,128)(2,1)S(1)} %collective-permute-done.19.refs_3_), channel_id=1, source_target_pairs={{4,0},{8,4},{12,8},{14,12},{10,14},{6,10},{2,6},{0,2},{5,1},{9,5},... | collective-permute-start | bytes 1179656 | tf_op jit(solution)/shard_map/ppermute | solution.py:108
  49.9 11.8 %collective-permute-start.6 = (bf16[256,384]{1,0:T(8,128)(2,1)S(1)}, bf16[256,384]{1,0:T(8,128)(2,1)S(1)}, u32[]{:S(2)}, u32[]{:S(2)}) collective-permute-start(bf16[256,384]{1,0:T(8,128)(2,1)S(1)} %slice.85), channel_id=1, source_target_pairs={{0,4},{4,8},{8,12},{12,14},{14,10},{10,6},{6,2},{2,0},{1,5},{5,9},... | collective-permute-start | bytes 589832 | tf_op jit(solution)/shard_map/ppermute | solution.py:108
  51.5 11.0 %collective-permute-start.7 = (bf16[256,384]{1,0:T(8,128)(2,1)S(1)}, bf16[256,384]{1,0:T(8,128)(2,1)S(1)}, u32[]{:S(2)}, u32[]{:S(2)}) collective-permute-start(bf16[256,384]{1,0:T(8,128)(2,1)S(1)} %slice.86), channel_id=1, source_target_pairs={{4,0},{8,4},{12,8},{14,12},{10,14},{6,10},{2,6},{0,2},{5,1},{9,5},... | collective-permute-start | bytes 589832 | tf_op jit(solution)/shard_map/ppermute | solution.py:108
  58.3 8.5 %collective-permute-start.22 = (bf16[256,384]{1,0:T(8,128)(2,1)S(1)}, bf16[256,384]{1,0:T(8,128)(2,1)S(1)}, u32[]{:S(2)}, u32[]{:S(2)}) collective-permute-start(bf16[256,384]{1,0:T(8,128)(2,1)S(1)} %slice.99), channel_id=1, source_target_pairs={{0,4},{4,8},{8,12},{12,14},{14,10},{10,6},{6,2},{2,0},{1,5},{5,9},... | collective-permute-start | bytes 589832 | tf_op jit(solution)/shard_map/ppermute | solution.py:108
  60.0 6.9 %collective-permute-start.23 = (bf16[256,384]{1,0:T(8,128)(2,1)S(1)}, bf16[256,384]{1,0:T(8,128)(2,1)S(1)}, u32[]{:S(2)}, u32[]{:S(2)}) collective-permute-start(bf16[256,384]{1,0:T(8,128)(2,1)S(1)} %slice.100), channel_id=1, source_target_pairs={{4,0},{8,4},{12,8},{14,12},{10,14},{6,10},{2,6},{0,2},{5,1},{9,5},... | collective-permute-start | bytes 589832 | tf_op jit(solution)/shard_map/ppermute | solution.py:108
  63.5 12.1 %collective-permute-start.8 = (bf16[512,384]{1,0:T(8,128)(2,1)S(1)}, bf16[512,384]{1,0:T(8,128)(2,1)S(1)}, u32[]{:S(2)}, u32[]{:S(2)}) collective-permute-start(bf16[512,384]{1,0:T(8,128)(2,1)S(1)} %shard_map.60), channel_id=1, source_target_pairs={{0,4},{4,8},{8,12},{12,14},{14,10},{10,6},{6,2},{2,0},{1,5},{5,9},... | collective-permute-start | bytes 1179656 | tf_op jit(solution)/shard_map/ppermute | solution.py:108
  65.1 12.1 %collective-permute-start.9 = (bf16[512,384]{1,0:T(8,128)(2,1)S(1)}, bf16[512,384]{1,0:T(8,128)(2,1)S(1)}, u32[]{:S(2)}, u32[]{:S(2)}) collective-permute-start(bf16[512,384]{1,0:T(8,128)(2,1)S(1)} %shard_map.60), channel_id=1, source_target_pairs={{4,0},{8,4},{12,8},{14,12},{10,14},{6,10},{2,6},{0,2},{5,1},{9,5},... | collective-permute-start | bytes 1179656 | tf_op jit(solution)/shard_map/ppermute | solution.py:108
  67.8 16.2 %collective-permute-start.24 = (bf16[512,384]{1,0:T(8,128)(2,1)S(1)}, bf16[512,384]{1,0:T(8,128)(2,1)S(1)}, u32[]{:S(2)}, u32[]{:S(2)}) collective-permute-start(bf16[512,384]{1,0:T(8,128)(2,1)S(1)} %shard_map.66), channel_id=1, source_target_pairs={{0,4},{4,8},{8,12},{12,14},{14,10},{10,6},{6,2},{2,0},{1,5},{5,9},... | collective-permute-start | bytes 1179656 | tf_op jit(solution)/shard_map/ppermute | solution.py:108
  69.4 16.1 %collective-permute-start.25 = (bf16[512,384]{1,0:T(8,128)(2,1)S(1)}, bf16[512,384]{1,0:T(8,128)(2,1)S(1)}, u32[]{:S(2)}, u32[]{:S(2)}) collective-permute-start(bf16[512,384]{1,0:T(8,128)(2,1)S(1)} %shard_map.66), channel_id=1, source_target_pairs={{4,0},{8,4},{12,8},{14,12},{10,14},{6,10},{2,6},{0,2},{5,1},{9,5},... | collective-permute-start | bytes 1179656 | tf_op jit(solution)/shard_map/ppermute | solution.py:108
  77.2 15.3 %collective-permute-start.10 = (bf16[512,384]{1,0:T(8,128)(2,1)S(1)}, bf16[512,384]{1,0:T(8,128)(2,1)S(1)}, u32[]{:S(2)}, u32[]{:S(2)}) collective-permute-start(bf16[512,384]{1,0:T(8,128)(2,1)S(1)} %collective-permute-done.8), channel_id=1, source_target_pairs={{0,4},{4,8},{8,12},{12,14},{14,10},{10,6},{6,2},{2,0},{1,5},{5,9},... | collective-permute-start | bytes 1179656 | tf_op jit(solution)/shard_map/ppermute | solution.py:108
  78.7 15.3 %collective-permute-start.11 = (bf16[512,384]{1,0:T(8,128)(2,1)S(1)}, bf16[512,384]{1,0:T(8,128)(2,1)S(1)}, u32[]{:S(2)}, u32[]{:S(2)}) collective-permute-start(bf16[512,384]{1,0:T(8,128)(2,1)S(1)} %collective-permute-done.9), channel_id=1, source_target_pairs={{4,0},{8,4},{12,8},{14,12},{10,14},{6,10},{2,6},{0,2},{5,1},{9,5},... | collective-permute-start | bytes 1179656 | tf_op jit(solution)/shard_map/ppermute | solution.py:108
  85.6 15.3 %collective-permute-start.26 = (bf16[512,384]{1,0:T(8,128)(2,1)S(1)}, bf16[512,384]{1,0:T(8,128)(2,1)S(1)}, u32[]{:S(2)}, u32[]{:S(2)}) collective-permute-start(bf16[512,384]{1,0:T(8,128)(2,1)S(1)} %collective-permute-done.24), channel_id=1, source_target_pairs={{0,4},{4,8},{8,12},{12,14},{14,10},{10,6},{6,2},{2,0},{1,5},{5,9},... | collective-permute-start | bytes 1179656 | tf_op jit(solution)/shard_map/ppermute | solution.py:108
  87.2 15.3 %collective-permute-start.27 = (bf16[512,384]{1,0:T(8,128)(2,1)S(1)}, bf16[512,384]{1,0:T(8,128)(2,1)S(1)}, u32[]{:S(2)}, u32[]{:S(2)}) collective-permute-start(bf16[512,384]{1,0:T(8,128)(2,1)S(1)} %collective-permute-done.25), channel_id=1, source_target_pairs={{4,0},{8,4},{12,8},{14,12},{10,14},{6,10},{2,6},{0,2},{5,1},{9,5},... | collective-permute-start | bytes 1179656 | tf_op jit(solution)/shard_map/ppermute | solution.py:108
  94.0 15.3 %collective-permute-start.12 = (bf16[512,384]{1,0:T(8,128)(2,1)S(1)}, bf16[512,384]{1,0:T(8,128)(2,1)S(1)}, u32[]{:S(2)}, u32[]{:S(2)}) collective-permute-start(bf16[512,384]{1,0:T(8,128)(2,1)S(1)} %collective-permute-done.10), channel_id=1, source_target_pairs={{0,4},{4,8},{8,12},{12,14},{14,10},{10,6},{6,2},{2,0},{1,5},{5,9},... | collective-permute-start | bytes 1179656 | tf_op jit(solution)/shard_map/ppermute | solution.py:108
  95.6 15.3 %collective-permute-start.13 = (bf16[512,384]{1,0:T(8,128)(2,1)S(1)}, bf16[512,384]{1,0:T(8,128)(2,1)S(1)}, u32[]{:S(2)}, u32[]{:S(2)}) collective-permute-start(bf16[512,384]{1,0:T(8,128)(2,1)S(1)} %collective-permute-done.11), channel_id=1, source_target_pairs={{4,0},{8,4},{12,8},{14,12},{10,14},{6,10},{2,6},{0,2},{5,1},{9,5},... | collective-permute-start | bytes 1179656 | tf_op jit(solution)/shard_map/ppermute | solution.py:108
  102.4 14.9 %collective-permute-start.28 = (bf16[512,384]{1,0:T(8,128)(2,1)S(1)}, bf16[512,384]{1,0:T(8,128)(2,1)S(1)}, u32[]{:S(2)}, u32[]{:S(2)}) collective-permute-start(bf16[512,384]{1,0:T(8,128)(2,1)S(1)} %collective-permute-done.26), channel_id=1, source_target_pairs={{0,4},{4,8},{8,12},{12,14},{14,10},{10,6},{6,2},{2,0},{1,5},{5,9},... | collective-permute-start | bytes 1179656 | tf_op jit(solution)/shard_map/ppermute | solution.py:108
  104.0 15.3 %collective-permute-start.29 = (bf16[512,384]{1,0:T(8,128)(2,1)S(1)}, bf16[512,384]{1,0:T(8,128)(2,1)S(1)}, u32[]{:S(2)}, u32[]{:S(2)}) collective-permute-start(bf16[512,384]{1,0:T(8,128)(2,1)S(1)} %collective-permute-done.27), channel_id=1, source_target_pairs={{4,0},{8,4},{12,8},{14,12},{10,14},{6,10},{2,6},{0,2},{5,1},{9,5},... | collective-permute-start | bytes 1179656 | tf_op jit(solution)/shard_map/ppermute | solution.py:108
  110.9 11.1 %collective-permute-start.14 = (bf16[256,384]{1,0:T(8,128)(2,1)S(1)}, bf16[256,384]{1,0:T(8,128)(2,1)S(1)}, u32[]{:S(2)}, u32[]{:S(2)}) collective-permute-start(bf16[256,384]{1,0:T(8,128)(2,1)S(1)} %slice.95), channel_id=1, source_target_pairs={{0,4},{4,8},{8,12},{12,14},{14,10},{10,6},{6,2},{2,0},{1,5},{5,9},... | collective-permute-start | bytes 589832 | tf_op jit(solution)/shard_map/ppermute | solution.py:108
  112.5 10.0 %collective-permute-start.15 = (bf16[256,384]{1,0:T(8,128)(2,1)S(1)}, bf16[256,384]{1,0:T(8,128)(2,1)S(1)}, u32[]{:S(2)}, u32[]{:S(2)}) collective-permute-start(bf16[256,384]{1,0:T(8,128)(2,1)S(1)} %slice.97), channel_id=1, source_target_pairs={{4,0},{8,4},{12,8},{14,12},{10,14},{6,10},{2,6},{0,2},{5,1},{9,5},... | collective-permute-start | bytes 589832 | tf_op jit(solution)/shard_map/ppermute | solution.py:108
  119.3 5.7 %collective-permute-start.30 = (bf16[256,384]{1,0:T(8,128)(2,1)S(1)}, bf16[256,384]{1,0:T(8,128)(2,1)S(1)}, u32[]{:S(2)}, u32[]{:S(2)}) collective-permute-start(bf16[256,384]{1,0:T(8,128)(2,1)S(1)} %slice.109), channel_id=1, source_target_pairs={{0,4},{4,8},{8,12},{12,14},{14,10},{10,6},{6,2},{2,0},{1,5},{5,9},... | collective-permute-start | bytes 589832 | tf_op jit(solution)/shard_map/ppermute | solution.py:108
  121.0 5.7 %collective-permute-start.31 = (bf16[256,384]{1,0:T(8,128)(2,1)S(1)}, bf16[256,384]{1,0:T(8,128)(2,1)S(1)}, u32[]{:S(2)}, u32[]{:S(2)}) collective-permute-start(bf16[256,384]{1,0:T(8,128)(2,1)S(1)} %slice.111), channel_id=1, source_target_pairs={{4,0},{8,4},{12,8},{14,12},{10,14},{6,10},{2,6},{0,2},{5,1},{9,5},... | collective-permute-start | bytes 589832 | tf_op jit(solution)/shard_map/ppermute | solution.py:108
  (4 other events, 20.4 us)

commit v5 on v4

--- a/solution.py
+++ b/solution.py
@@ -100,7 +100,9 @@
         for step in range(1, n // 2 + 1):
             for m in range(modules):
                 if step > 1:
-                    going[m], state[m], _ = lax.optimization_barrier((going[m], state[m], waits.get((step, m), ())))
+                    ways = going[m] if step < n // 2 else going[m][:1]
+                    ways, state[m], _ = lax.optimization_barrier((ways, state[m], waits.get((step, m), ())))
+                    going[m] = ways + going[m][len(ways) :]
                 ways = going[m]
                 if step == n // 2:
                     half = ways[0].shape[0] // 2

time: 130 us -> 128 us (0.985)
  waiting for transfers between devices: 62 us -> 60.2 us
    ppermute x16, waiting for transfers between devices: 24.1 us -> 19 us  [ring_gather(): lax.ppermute(ways[1], 'doc', down)]
    ppermute x16, waiting for transfers between devices: 36.3 us -> 39.5 us  [ring_gather(): lax.ppermute(ways[0], 'doc', up)]
    ppermute x16, starting transfers between devices: 27.5 us -> 29.1 us  [ring_gather(): lax.ppermute(ways[0], 'doc', up)]
  transfers between devices with their start and end apart: 33 -> 33, of which waited for: 28 -> 26; matrix products, arithmetic and copies ran while one was open for 8% -> 9% of each run, Pallas kernels for 13% -> 13%
where the time goes in v5:
time: 128 us
  waiting for transfers between devices  60.2 us (47%)
  starting transfers between devices  34.4 us (27%)
  Pallas kernels  16.6 us (13%)
  local copies, waits for them, and re-layouts  10.9 us (9%)
  matrix products  4.71 us (4%)
    ppermute x16, waiting for transfers between devices, ring_gather(): lax.ppermute(ways[0], 'doc', up)  39.5 us
    ppermute x16, starting transfers between devices, ring_gather(): lax.ppermute(ways[0], 'doc', up)  29.1 us
    ppermute x16, waiting for transfers between devices, ring_gather(): lax.ppermute(ways[1], 'doc', down)  19 us
    pallas_call x10, Pallas kernels, add_precond(): pl.pallas_call(functools.partial(precond_kernel, len(entries), acc is not...  11.4 us
    unnamed x7, local copies, waits for them, and re-layouts  7.96 us
    ppermute x16, starting transfers between devices, ring_gather(): lax.ppermute(ways[1], 'doc', down)  5.21 us
    pallas_call x2, Pallas kernels, place(): pl.pallas_call(place_kernel, out_shape=jax.ShapeDtypeStruct((rows, width)...  5.2 us
    dot_general x18, matrix products, dot(): return jnp.dot(a, b, preferred_element_type=jnp.float32)  4.71 us
  transfers between devices with their start and end apart: 33, of which 26 were waited for; matrix products, arithmetic and copies ran while one was open for 9% of the time, Pallas kernels for 13%

profile of v5, /device:TPU:0, one launch (start us, length us, event | category | flops | bytes accessed | tf_op | source)
XLA Modules:
  0.0 127.8 jit_solution(1897172082747127930)
XLA Ops:
  1.0 3.1 %collective-permute-start = (bf16[512,384]{1,0:T(8,128)(2,1)S(1)}, bf16[512,384]{1,0:T(8,128)(2,1)S(1)}, u32[]{:S(2)}, u32[]{:S(2)}) collective-permute-start(bf16[512,384]{1,0:T(8,128)(2,1)S(1)} %slice_bitcast_fusion.1.refs_1_), channel_id=1, source_target_pairs={{0,4},{4,8},{8,12},{12,14},{14,10},{10,6},{6,2},{2,0},{1,5},{5,9},... | collective-permute-start | bytes 1179656 | tf_op jit(solution)/shard_map/ppermute | solution.py:110
  5.2 2.1 %collective-permute-start.16 = (bf16[512,384]{1,0:T(8,128)(2,1)S(1)}, bf16[512,384]{1,0:T(8,128)(2,1)S(1)}, u32[]{:S(2)}, u32[]{:S(2)}) collective-permute-start(bf16[512,384]{1,0:T(8,128)(2,1)S(1)} %slice_bitcast_fusion.refs_1_), channel_id=1, source_target_pairs={{0,4},{4,8},{8,12},{12,14},{14,10},{10,6},{6,2},{2,0},{1,5},{5,9},... | collective-permute-start | bytes 1179656 | tf_op jit(solution)/shard_map/ppermute | solution.py:110
  7.9 3.4 %copy-done = bf16[1,2,512,4096]{3,2,1,0:T(8,128)(2,1)S(1)} copy-done((bf16[1,2,512,4096]{3,2,1,0:T(8,128)(2,1)S(1)}, bf16[1,2,512,4096]{3,2,1,0:T(8,128)(2,1)}, u32[]{:S(2)}) %copy-start) | copy-done | bytes 8388632
  12.3 1.7 %collective-permute-done.refs_2_ = bf16[512,384]{1,0:T(8,128)(2,1)S(1)} collective-permute-done((bf16[512,384]{1,0:T(8,128)(2,1)S(1)}, bf16[512,384]{1,0:T(8,128)(2,1)S(1)}, u32[]{:S(2)}, u32[]{:S(2)}) %collective-permute-start) | collective-permute-done | bytes 393248 | tf_op jit(solution)/shard_map/ppermute | solution.py:110
  14.0 2.2 %collective-permute-done.1.refs_3_ = bf16[512,384]{1,0:T(8,128)(2,1)S(1)} collective-permute-done((bf16[512,384]{1,0:T(8,128)(2,1)S(1)}, bf16[512,384]{1,0:T(8,128)(2,1)S(1)}, u32[]{:S(2)}, u32[]{:S(2)}) %collective-permute-start.1) | collective-permute-done | bytes 393248 | tf_op jit(solution)/shard_map/ppermute | solution.py:110
  16.2 1.6 %collective-permute-start.2 = (bf16[512,384]{1,0:T(8,128)(2,1)S(1)}, bf16[512,384]{1,0:T(8,128)(2,1)S(1)}, u32[]{:S(2)}, u32[]{:S(2)}) collective-permute-start(bf16[512,384]{1,0:T(8,128)(2,1)S(1)} %collective-permute-done.refs_2_), channel_id=1, source_target_pairs={{0,4},{4,8},{8,12},{12,14},{14,10},{10,6},{6,2},{2,0},{1,5},{5,9},... | collective-permute-start | bytes 1179656 | tf_op jit(solution)/shard_map/ppermute | solution.py:110
  18.2 4.6 %copy.8 = bf16[1,224,2,4096]{3,1,2,0:T(8,128)(2,1)S(1)} copy(bf16[1,224,2,4096]{3,2,1,0:T(2,128)(2,1)} %param.7) | data formatting | bytes 7340032 | tf_op args[2]
  26.6 2.6 %shard_map.57 = bf16[224,4096]{1,0:T(8,128)(2,1)S(1)} custom-call(s32[8]{0:T(128)S(1)} %dynamic-slice_bitcast_fusion.table, s32[1,224]{1,0:T(1,128)S(1)} %copy-done.2, bf16[2,224,4096]{2,1,0:T(8,128)(2,1)S(1)} %bitcast.48), custom_call_target="tpu_custom_call" | custom-call | flops 411041792 | bytes 3670016 | tf_op jit(solution)/shard_map/pallas_call | solution.py:66
  30.8 2.2 %collective-permute-done.3.refs_3_ = bf16[512,384]{1,0:T(8,128)(2,1)S(1)} collective-permute-done((bf16[512,384]{1,0:T(8,128)(2,1)S(1)}, bf16[512,384]{1,0:T(8,128)(2,1)S(1)}, u32[]{:S(2)}, u32[]{:S(2)}) %collective-permute-start.3) | collective-permute-done | bytes 393248 | tf_op jit(solution)/shard_map/ppermute | solution.py:110
  35.0 2.6 %shard_map.63 = bf16[224,4096]{1,0:T(8,128)(2,1)S(1)} custom-call(s32[8]{0:T(128)S(1)} %dynamic-slice_bitcast_fusion.table, s32[1,224]{1,0:T(1,128)S(1)} %copy-done.2, bf16[2,224,4096]{2,1,0:T(8,128)(2,1)S(1)} %bitcast.49), custom_call_target="tpu_custom_call" | custom-call | flops 411041792 | bytes 3670016 | tf_op jit(solution)/shard_map/pallas_call | solution.py:66
  39.3 2.2 %collective-permute-done.19.refs_3_ = bf16[512,384]{1,0:T(8,128)(2,1)S(1)} collective-permute-done((bf16[512,384]{1,0:T(8,128)(2,1)S(1)}, bf16[512,384]{1,0:T(8,128)(2,1)S(1)}, u32[]{:S(2)}, u32[]{:S(2)}) %collective-permute-start.19) | collective-permute-done | bytes 393248 | tf_op jit(solution)/shard_map/ppermute | solution.py:110
  44.7 3.0 %collective-permute-done.4.refs_2_ = bf16[512,384]{1,0:T(8,128)(2,1)S(1)} collective-permute-done((bf16[512,384]{1,0:T(8,128)(2,1)S(1)}, bf16[512,384]{1,0:T(8,128)(2,1)S(1)}, u32[]{:S(2)}, u32[]{:S(2)}) %collective-permute-start.4) | collective-permute-done | bytes 393248 | tf_op jit(solution)/shard_map/ppermute | solution.py:110
  47.7 2.2 %collective-permute-start.5 = (bf16[256,384]{1,0:T(8,128)(2,1)S(1)}, bf16[256,384]{1,0:T(8,128)(2,1)S(1)}, u32[]{:S(2)}, u32[]{:S(2)}) collective-permute-start(bf16[256,384]{1,0:T(8,128)(2,1)S(1)} %slice.85), channel_id=1, source_target_pairs={{0,4},{4,8},{8,12},{12,14},{14,10},{10,6},{6,2},{2,0},{1,5},{5,9},... | collective-permute-start | bytes 589832 | tf_op jit(solution)/shard_map/ppermute | solution.py:110
  51.2 4.9 %collective-permute-done.20.refs_2_ = bf16[512,384]{1,0:T(8,128)(2,1)S(1)} collective-permute-done((bf16[512,384]{1,0:T(8,128)(2,1)S(1)}, bf16[512,384]{1,0:T(8,128)(2,1)S(1)}, u32[]{:S(2)}, u32[]{:S(2)}) %collective-permute-start.20) | collective-permute-done | bytes 393248 | tf_op jit(solution)/shard_map/ppermute | solution.py:110
  56.1 2.2 %collective-permute-start.21 = (bf16[256,384]{1,0:T(8,128)(2,1)S(1)}, bf16[256,384]{1,0:T(8,128)(2,1)S(1)}, u32[]{:S(2)}, u32[]{:S(2)}) collective-permute-start(bf16[256,384]{1,0:T(8,128)(2,1)S(1)} %slice.99), channel_id=1, source_target_pairs={{0,4},{4,8},{8,12},{12,14},{14,10},{10,6},{6,2},{2,0},{1,5},{5,9},... | collective-permute-start | bytes 589832 | tf_op jit(solution)/shard_map/ppermute | solution.py:110
  60.3 2.2 %collective-permute-done.7.refs_3_ = bf16[256,384]{1,0:T(8,128)(2,1)S(1)} collective-permute-done((bf16[256,384]{1,0:T(8,128)(2,1)S(1)}, bf16[256,384]{1,0:T(8,128)(2,1)S(1)}, u32[]{:S(2)}, u32[]{:S(2)}) %collective-permute-start.7) | collective-permute-done | bytes 196640 | tf_op jit(solution)/shard_map/ppermute | solution.py:110
  63.5 1.6 %collective-permute-start.8 = (bf16[512,384]{1,0:T(8,128)(2,1)S(1)}, bf16[512,384]{1,0:T(8,128)(2,1)S(1)}, u32[]{:S(2)}, u32[]{:S(2)}) collective-permute-start(bf16[512,384]{1,0:T(8,128)(2,1)S(1)} %shard_map.60), channel_id=1, source_target_pairs={{0,4},{4,8},{8,12},{12,14},{14,10},{10,6},{6,2},{2,0},{1,5},{5,9},... | collective-permute-start | bytes 1179656 | tf_op jit(solution)/shard_map/ppermute | solution.py:110
  67.8 1.6 %collective-permute-start.24 = (bf16[512,384]{1,0:T(8,128)(2,1)S(1)}, bf16[512,384]{1,0:T(8,128)(2,1)S(1)}, u32[]{:S(2)}, u32[]{:S(2)}) collective-permute-start(bf16[512,384]{1,0:T(8,128)(2,1)S(1)} %shard_map.66), channel_id=1, source_target_pairs={{0,4},{4,8},{8,12},{12,14},{14,10},{10,6},{6,2},{2,0},{1,5},{5,9},... | collective-permute-start | bytes 1179656 | tf_op jit(solution)/shard_map/ppermute | solution.py:110
  70.5 5.1 %collective-permute-done.8 = bf16[512,384]{1,0:T(8,128)(2,1)S(1)} collective-permute-done((bf16[512,384]{1,0:T(8,128)(2,1)S(1)}, bf16[512,384]{1,0:T(8,128)(2,1)S(1)}, u32[]{:S(2)}, u32[]{:S(2)}) %collective-permute-start.8) | collective-permute-done | bytes 393248 | tf_op jit(solution)/shard_map/ppermute | solution.py:110
  75.6 1.6 %collective-permute-done.9 = bf16[512,384]{1,0:T(8,128)(2,1)S(1)} collective-permute-done((bf16[512,384]{1,0:T(8,128)(2,1)S(1)}, bf16[512,384]{1,0:T(8,128)(2,1)S(1)}, u32[]{:S(2)}, u32[]{:S(2)}) %collective-permute-start.9) | collective-permute-done | bytes 393248 | tf_op jit(solution)/shard_map/ppermute | solution.py:110
  79.2 4.8 %collective-permute-done.24 = bf16[512,384]{1,0:T(8,128)(2,1)S(1)} collective-permute-done((bf16[512,384]{1,0:T(8,128)(2,1)S(1)}, bf16[512,384]{1,0:T(8,128)(2,1)S(1)}, u32[]{:S(2)}, u32[]{:S(2)}) %collective-permute-start.24) | collective-permute-done | bytes 393248 | tf_op jit(solution)/shard_map/ppermute | solution.py:110
  84.0 1.6 %collective-permute-done.25 = bf16[512,384]{1,0:T(8,128)(2,1)S(1)} collective-permute-done((bf16[512,384]{1,0:T(8,128)(2,1)S(1)}, bf16[512,384]{1,0:T(8,128)(2,1)S(1)}, u32[]{:S(2)}, u32[]{:S(2)}) %collective-permute-start.25) | collective-permute-done | bytes 393248 | tf_op jit(solution)/shard_map/ppermute | solution.py:110
  88.8 3.7 %collective-permute-done.10 = bf16[512,384]{1,0:T(8,128)(2,1)S(1)} collective-permute-done((bf16[512,384]{1,0:T(8,128)(2,1)S(1)}, bf16[512,384]{1,0:T(8,128)(2,1)S(1)}, u32[]{:S(2)}, u32[]{:S(2)}) %collective-permute-start.10) | collective-permute-done | bytes 393248 | tf_op jit(solution)/shard_map/ppermute | solution.py:110
  92.4 1.6 %collective-permute-done.11 = bf16[512,384]{1,0:T(8,128)(2,1)S(1)} collective-permute-done((bf16[512,384]{1,0:T(8,128)(2,1)S(1)}, bf16[512,384]{1,0:T(8,128)(2,1)S(1)}, u32[]{:S(2)}, u32[]{:S(2)}) %collective-permute-start.11) | collective-permute-done | bytes 393248 | tf_op jit(solution)/shard_map/ppermute | solution.py:110
  96.0 4.8 %collective-permute-done.26 = bf16[512,384]{1,0:T(8,128)(2,1)S(1)} collective-permute-done((bf16[512,384]{1,0:T(8,128)(2,1)S(1)}, bf16[512,384]{1,0:T(8,128)(2,1)S(1)}, u32[]{:S(2)}, u32[]{:S(2)}) %collective-permute-start.26) | collective-permute-done | bytes 393248 | tf_op jit(solution)/shard_map/ppermute | solution.py:110
  100.9 1.6 %collective-permute-done.27 = bf16[512,384]{1,0:T(8,128)(2,1)S(1)} collective-permute-done((bf16[512,384]{1,0:T(8,128)(2,1)S(1)}, bf16[512,384]{1,0:T(8,128)(2,1)S(1)}, u32[]{:S(2)}, u32[]{:S(2)}) %collective-permute-start.27) | collective-permute-done | bytes 393248 | tf_op jit(solution)/shard_map/ppermute | solution.py:110
  105.6 3.7 %collective-permute-done.12 = bf16[512,384]{1,0:T(8,128)(2,1)S(1)} collective-permute-done((bf16[512,384]{1,0:T(8,128)(2,1)S(1)}, bf16[512,384]{1,0:T(8,128)(2,1)S(1)}, u32[]{:S(2)}, u32[]{:S(2)}) %collective-permute-start.12) | collective-permute-done | bytes 393248 | tf_op jit(solution)/shard_map/ppermute | solution.py:110
  109.3 1.6 %collective-permute-start.14 = (bf16[256,384]{1,0:T(8,128)(2,1)S(1)}, bf16[256,384]{1,0:T(8,128)(2,1)S(1)}, u32[]{:S(2)}, u32[]{:S(2)}) collective-permute-start(bf16[256,384]{1,0:T(8,128)(2,1)S(1)} %slice.95), channel_id=1, source_target_pairs={{0,4},{4,8},{8,12},{12,14},{14,10},{10,6},{6,2},{2,0},{1,5},{5,9},... | collective-permute-start | bytes 589832 | tf_op jit(solution)/shard_map/ppermute | solution.py:110
  111.5 5.8 %collective-permute-done.28 = bf16[512,384]{1,0:T(8,128)(2,1)S(1)} collective-permute-done((bf16[512,384]{1,0:T(8,128)(2,1)S(1)}, bf16[512,384]{1,0:T(8,128)(2,1)S(1)}, u32[]{:S(2)}, u32[]{:S(2)}) %collective-permute-start.28) | collective-permute-done | bytes 393248 | tf_op jit(solution)/shard_map/ppermute | solution.py:110
  117.3 2.0 %collective-permute-start.30 = (bf16[256,384]{1,0:T(8,128)(2,1)S(1)}, bf16[256,384]{1,0:T(8,128)(2,1)S(1)}, u32[]{:S(2)}, u32[]{:S(2)}) collective-permute-start(bf16[256,384]{1,0:T(8,128)(2,1)S(1)} %slice.109), channel_id=1, source_target_pairs={{0,4},{4,8},{8,12},{12,14},{14,10},{10,6},{6,2},{2,0},{1,5},{5,9},... | collective-permute-start | bytes 589832 | tf_op jit(solution)/shard_map/ppermute | solution.py:110
  123.3 1.9 %collective-permute-done.31 = bf16[256,384]{1,0:T(8,128)(2,1)S(1)} collective-permute-done((bf16[256,384]{1,0:T(8,128)(2,1)S(1)}, bf16[256,384]{1,0:T(8,128)(2,1)S(1)}, u32[]{:S(2)}, u32[]{:S(2)}) %collective-permute-start.31) | collective-permute-done | bytes 196640 | tf_op jit(solution)/shard_map/ppermute | solution.py:110
  125.4 1.6 %collective-permute-done.32 = f32[224,384]{1,0:T(8,128)S(1)} collective-permute-done((f32[224,384]{1,0:T(8,128)S(1)}, f32[224,384]{1,0:T(8,128)S(1)}, u32[]{:S(2)}, u32[]{:S(2)}) %collective-permute-start.32) | collective-permute-done | bytes 344096 | tf_op jit(solution)/shard_map/ppermute | solution.py:143
  (83 shorter events, 40.3 us)
Async XLA Ops:
  1.0 12.9 %collective-permute-start = (bf16[512,384]{1,0:T(8,128)(2,1)S(1)}, bf16[512,384]{1,0:T(8,128)(2,1)S(1)}, u32[]{:S(2)}, u32[]{:S(2)}) collective-permute-start(bf16[512,384]{1,0:T(8,128)(2,1)S(1)} %slice_bitcast_fusion.1.refs_1_), channel_id=1, source_target_pairs={{0,4},{4,8},{8,12},{12,14},{14,10},{10,6},{6,2},{2,0},{1,5},{5,9},... | collective-permute-start | bytes 1179656 | tf_op jit(solution)/shard_map/ppermute | solution.py:110
  4.1 12.0 %collective-permute-start.1 = (bf16[512,384]{1,0:T(8,128)(2,1)S(1)}, bf16[512,384]{1,0:T(8,128)(2,1)S(1)}, u32[]{:S(2)}, u32[]{:S(2)}) collective-permute-start(bf16[512,384]{1,0:T(8,128)(2,1)S(1)} %slice_bitcast_fusion.1.refs_1_), channel_id=1, source_target_pairs={{4,0},{8,4},{12,8},{14,12},{10,14},{6,10},{2,6},{0,2},{5,1},{9,5},... | collective-permute-start | bytes 1179656 | tf_op jit(solution)/shard_map/ppermute | solution.py:110
  5.2 18.6 %collective-permute-start.16 = (bf16[512,384]{1,0:T(8,128)(2,1)S(1)}, bf16[512,384]{1,0:T(8,128)(2,1)S(1)}, u32[]{:S(2)}, u32[]{:S(2)}) collective-permute-start(bf16[512,384]{1,0:T(8,128)(2,1)S(1)} %slice_bitcast_fusion.refs_1_), channel_id=1, source_target_pairs={{0,4},{4,8},{8,12},{12,14},{14,10},{10,6},{6,2},{2,0},{1,5},{5,9},... | collective-permute-start | bytes 1179656 | tf_op jit(solution)/shard_map/ppermute | solution.py:110
  7.2 17.3 %collective-permute-start.17 = (bf16[512,384]{1,0:T(8,128)(2,1)S(1)}, bf16[512,384]{1,0:T(8,128)(2,1)S(1)}, u32[]{:S(2)}, u32[]{:S(2)}) collective-permute-start(bf16[512,384]{1,0:T(8,128)(2,1)S(1)} %slice_bitcast_fusion.refs_1_), channel_id=1, source_target_pairs={{4,0},{8,4},{12,8},{14,12},{10,14},{6,10},{2,6},{0,2},{5,1},{9,5},... | collective-permute-start | bytes 1179656 | tf_op jit(solution)/shard_map/ppermute | solution.py:110
  16.2 14.7 %collective-permute-start.2 = (bf16[512,384]{1,0:T(8,128)(2,1)S(1)}, bf16[512,384]{1,0:T(8,128)(2,1)S(1)}, u32[]{:S(2)}, u32[]{:S(2)}) collective-permute-start(bf16[512,384]{1,0:T(8,128)(2,1)S(1)} %collective-permute-done.refs_2_), channel_id=1, source_target_pairs={{0,4},{4,8},{8,12},{12,14},{14,10},{10,6},{6,2},{2,0},{1,5},{5,9},... | collective-permute-start | bytes 1179656 | tf_op jit(solution)/shard_map/ppermute | solution.py:110
  17.7 15.3 %collective-permute-start.3 = (bf16[512,384]{1,0:T(8,128)(2,1)S(1)}, bf16[512,384]{1,0:T(8,128)(2,1)S(1)}, u32[]{:S(2)}, u32[]{:S(2)}) collective-permute-start(bf16[512,384]{1,0:T(8,128)(2,1)S(1)} %collective-permute-done.1.refs_3_), channel_id=1, source_target_pairs={{4,0},{8,4},{12,8},{14,12},{10,14},{6,10},{2,6},{0,2},{5,1},{9,5},... | collective-permute-start | bytes 1179656 | tf_op jit(solution)/shard_map/ppermute | solution.py:110
  24.6 14.7 %collective-permute-start.18 = (bf16[512,384]{1,0:T(8,128)(2,1)S(1)}, bf16[512,384]{1,0:T(8,128)(2,1)S(1)}, u32[]{:S(2)}, u32[]{:S(2)}) collective-permute-start(bf16[512,384]{1,0:T(8,128)(2,1)S(1)} %collective-permute-done.16.refs_2_), channel_id=1, source_target_pairs={{0,4},{4,8},{8,12},{12,14},{14,10},{10,6},{6,2},{2,0},{1,5},{5,9},... | collective-permute-start | bytes 1179656 | tf_op jit(solution)/shard_map/ppermute | solution.py:110
  26.2 15.3 %collective-permute-start.19 = (bf16[512,384]{1,0:T(8,128)(2,1)S(1)}, bf16[512,384]{1,0:T(8,128)(2,1)S(1)}, u32[]{:S(2)}, u32[]{:S(2)}) collective-permute-start(bf16[512,384]{1,0:T(8,128)(2,1)S(1)} %collective-permute-done.17.refs_3_), channel_id=1, source_target_pairs={{4,0},{8,4},{12,8},{14,12},{10,14},{6,10},{2,6},{0,2},{5,1},{9,5},... | collective-permute-start | bytes 1179656 | tf_op jit(solution)/shard_map/ppermute | solution.py:110
  33.0 14.7 %collective-permute-start.4 = (bf16[512,384]{1,0:T(8,128)(2,1)S(1)}, bf16[512,384]{1,0:T(8,128)(2,1)S(1)}, u32[]{:S(2)}, u32[]{:S(2)}) collective-permute-start(bf16[512,384]{1,0:T(8,128)(2,1)S(1)} %collective-permute-done.2.refs_2_), channel_id=1, source_target_pairs={{0,4},{4,8},{8,12},{12,14},{14,10},{10,6},{6,2},{2,0},{1,5},{5,9},... | collective-permute-start | bytes 1179656 | tf_op jit(solution)/shard_map/ppermute | solution.py:110
  34.6 15.3 %collective-permute-start.6 = (bf16[512,384]{1,0:T(8,128)(2,1)S(1)}, bf16[512,384]{1,0:T(8,128)(2,1)S(1)}, u32[]{:S(2)}, u32[]{:S(2)}) collective-permute-start(bf16[512,384]{1,0:T(8,128)(2,1)S(1)} %collective-permute-done.3.refs_3_), channel_id=1, source_target_pairs={{4,0},{8,4},{12,8},{14,12},{10,14},{6,10},{2,6},{0,2},{5,1},{9,5},... | collective-permute-start | bytes 1179656 | tf_op jit(solution)/shard_map/ppermute | solution.py:110
  41.4 14.7 %collective-permute-start.20 = (bf16[512,384]{1,0:T(8,128)(2,1)S(1)}, bf16[512,384]{1,0:T(8,128)(2,1)S(1)}, u32[]{:S(2)}, u32[]{:S(2)}) collective-permute-start(bf16[512,384]{1,0:T(8,128)(2,1)S(1)} %collective-permute-done.18.refs_2_), channel_id=1, source_target_pairs={{0,4},{4,8},{8,12},{12,14},{14,10},{10,6},{6,2},{2,0},{1,5},{5,9},... | collective-permute-start | bytes 1179656 | tf_op jit(solution)/shard_map/ppermute | solution.py:110
  43.0 15.3 %collective-permute-start.22 = (bf16[512,384]{1,0:T(8,128)(2,1)S(1)}, bf16[512,384]{1,0:T(8,128)(2,1)S(1)}, u32[]{:S(2)}, u32[]{:S(2)}) collective-permute-start(bf16[512,384]{1,0:T(8,128)(2,1)S(1)} %collective-permute-done.19.refs_3_), channel_id=1, source_target_pairs={{4,0},{8,4},{12,8},{14,12},{10,14},{6,10},{2,6},{0,2},{5,1},{9,5},... | collective-permute-start | bytes 1179656 | tf_op jit(solution)/shard_map/ppermute | solution.py:110
  47.7 12.6 %collective-permute-start.5 = (bf16[256,384]{1,0:T(8,128)(2,1)S(1)}, bf16[256,384]{1,0:T(8,128)(2,1)S(1)}, u32[]{:S(2)}, u32[]{:S(2)}) collective-permute-start(bf16[256,384]{1,0:T(8,128)(2,1)S(1)} %slice.85), channel_id=1, source_target_pairs={{0,4},{4,8},{8,12},{12,14},{14,10},{10,6},{6,2},{2,0},{1,5},{5,9},... | collective-permute-start | bytes 589832 | tf_op jit(solution)/shard_map/ppermute | solution.py:110
  49.9 12.6 %collective-permute-start.7 = (bf16[256,384]{1,0:T(8,128)(2,1)S(1)}, bf16[256,384]{1,0:T(8,128)(2,1)S(1)}, u32[]{:S(2)}, u32[]{:S(2)}) collective-permute-start(bf16[256,384]{1,0:T(8,128)(2,1)S(1)} %slice.112), channel_id=1, source_target_pairs={{4,0},{8,4},{12,8},{14,12},{10,14},{6,10},{2,6},{0,2},{5,1},{9,5},... | collective-permute-start | bytes 589832 | tf_op jit(solution)/shard_map/ppermute | solution.py:110
  56.1 10.7 %collective-permute-start.21 = (bf16[256,384]{1,0:T(8,128)(2,1)S(1)}, bf16[256,384]{1,0:T(8,128)(2,1)S(1)}, u32[]{:S(2)}, u32[]{:S(2)}) collective-permute-start(bf16[256,384]{1,0:T(8,128)(2,1)S(1)} %slice.99), channel_id=1, source_target_pairs={{0,4},{4,8},{8,12},{12,14},{14,10},{10,6},{6,2},{2,0},{1,5},{5,9},... | collective-permute-start | bytes 589832 | tf_op jit(solution)/shard_map/ppermute | solution.py:110
  58.4 8.5 %collective-permute-start.23 = (bf16[256,384]{1,0:T(8,128)(2,1)S(1)}, bf16[256,384]{1,0:T(8,128)(2,1)S(1)}, u32[]{:S(2)}, u32[]{:S(2)}) collective-permute-start(bf16[256,384]{1,0:T(8,128)(2,1)S(1)} %slice.123), channel_id=1, source_target_pairs={{4,0},{8,4},{12,8},{14,12},{10,14},{6,10},{2,6},{0,2},{5,1},{9,5},... | collective-permute-start | bytes 589832 | tf_op jit(solution)/shard_map/ppermute | solution.py:110
  63.5 12.1 %collective-permute-start.8 = (bf16[512,384]{1,0:T(8,128)(2,1)S(1)}, bf16[512,384]{1,0:T(8,128)(2,1)S(1)}, u32[]{:S(2)}, u32[]{:S(2)}) collective-permute-start(bf16[512,384]{1,0:T(8,128)(2,1)S(1)} %shard_map.60), channel_id=1, source_target_pairs={{0,4},{4,8},{8,12},{12,14},{14,10},{10,6},{6,2},{2,0},{1,5},{5,9},... | collective-permute-start | bytes 1179656 | tf_op jit(solution)/shard_map/ppermute | solution.py:110
  65.1 12.1 %collective-permute-start.9 = (bf16[512,384]{1,0:T(8,128)(2,1)S(1)}, bf16[512,384]{1,0:T(8,128)(2,1)S(1)}, u32[]{:S(2)}, u32[]{:S(2)}) collective-permute-start(bf16[512,384]{1,0:T(8,128)(2,1)S(1)} %shard_map.60), channel_id=1, source_target_pairs={{4,0},{8,4},{12,8},{14,12},{10,14},{6,10},{2,6},{0,2},{5,1},{9,5},... | collective-permute-start | bytes 1179656 | tf_op jit(solution)/shard_map/ppermute | solution.py:110
  67.8 16.2 %collective-permute-start.24 = (bf16[512,384]{1,0:T(8,128)(2,1)S(1)}, bf16[512,384]{1,0:T(8,128)(2,1)S(1)}, u32[]{:S(2)}, u32[]{:S(2)}) collective-permute-start(bf16[512,384]{1,0:T(8,128)(2,1)S(1)} %shard_map.66), channel_id=1, source_target_pairs={{0,4},{4,8},{8,12},{12,14},{14,10},{10,6},{6,2},{2,0},{1,5},{5,9},... | collective-permute-start | bytes 1179656 | tf_op jit(solution)/shard_map/ppermute | solution.py:110
  69.4 16.1 %collective-permute-start.25 = (bf16[512,384]{1,0:T(8,128)(2,1)S(1)}, bf16[512,384]{1,0:T(8,128)(2,1)S(1)}, u32[]{:S(2)}, u32[]{:S(2)}) collective-permute-start(bf16[512,384]{1,0:T(8,128)(2,1)S(1)} %shard_map.66), channel_id=1, source_target_pairs={{4,0},{8,4},{12,8},{14,12},{10,14},{6,10},{2,6},{0,2},{5,1},{9,5},... | collective-permute-start | bytes 1179656 | tf_op jit(solution)/shard_map/ppermute | solution.py:110
  77.2 15.3 %collective-permute-start.10 = (bf16[512,384]{1,0:T(8,128)(2,1)S(1)}, bf16[512,384]{1,0:T(8,128)(2,1)S(1)}, u32[]{:S(2)}, u32[]{:S(2)}) collective-permute-start(bf16[512,384]{1,0:T(8,128)(2,1)S(1)} %collective-permute-done.8), channel_id=1, source_target_pairs={{0,4},{4,8},{8,12},{12,14},{14,10},{10,6},{6,2},{2,0},{1,5},{5,9},... | collective-permute-start | bytes 1179656 | tf_op jit(solution)/shard_map/ppermute | solution.py:110
  78.7 15.3 %collective-permute-start.11 = (bf16[512,384]{1,0:T(8,128)(2,1)S(1)}, bf16[512,384]{1,0:T(8,128)(2,1)S(1)}, u32[]{:S(2)}, u32[]{:S(2)}) collective-permute-start(bf16[512,384]{1,0:T(8,128)(2,1)S(1)} %collective-permute-done.9), channel_id=1, source_target_pairs={{4,0},{8,4},{12,8},{14,12},{10,14},{6,10},{2,6},{0,2},{5,1},{9,5},... | collective-permute-start | bytes 1179656 | tf_op jit(solution)/shard_map/ppermute | solution.py:110
  85.6 15.3 %collective-permute-start.26 = (bf16[512,384]{1,0:T(8,128)(2,1)S(1)}, bf16[512,384]{1,0:T(8,128)(2,1)S(1)}, u32[]{:S(2)}, u32[]{:S(2)}) collective-permute-start(bf16[512,384]{1,0:T(8,128)(2,1)S(1)} %collective-permute-done.24), channel_id=1, source_target_pairs={{0,4},{4,8},{8,12},{12,14},{14,10},{10,6},{6,2},{2,0},{1,5},{5,9},... | collective-permute-start | bytes 1179656 | tf_op jit(solution)/shard_map/ppermute | solution.py:110
  87.2 15.3 %collective-permute-start.27 = (bf16[512,384]{1,0:T(8,128)(2,1)S(1)}, bf16[512,384]{1,0:T(8,128)(2,1)S(1)}, u32[]{:S(2)}, u32[]{:S(2)}) collective-permute-start(bf16[512,384]{1,0:T(8,128)(2,1)S(1)} %collective-permute-done.25), channel_id=1, source_target_pairs={{4,0},{8,4},{12,8},{14,12},{10,14},{6,10},{2,6},{0,2},{5,1},{9,5},... | collective-permute-start | bytes 1179656 | tf_op jit(solution)/shard_map/ppermute | solution.py:110
  94.0 15.3 %collective-permute-start.12 = (bf16[512,384]{1,0:T(8,128)(2,1)S(1)}, bf16[512,384]{1,0:T(8,128)(2,1)S(1)}, u32[]{:S(2)}, u32[]{:S(2)}) collective-permute-start(bf16[512,384]{1,0:T(8,128)(2,1)S(1)} %collective-permute-done.10), channel_id=1, source_target_pairs={{0,4},{4,8},{8,12},{12,14},{14,10},{10,6},{6,2},{2,0},{1,5},{5,9},... | collective-permute-start | bytes 1179656 | tf_op jit(solution)/shard_map/ppermute | solution.py:110
  95.6 15.4 %collective-permute-start.13 = (bf16[512,384]{1,0:T(8,128)(2,1)S(1)}, bf16[512,384]{1,0:T(8,128)(2,1)S(1)}, u32[]{:S(2)}, u32[]{:S(2)}) collective-permute-start(bf16[512,384]{1,0:T(8,128)(2,1)S(1)} %collective-permute-done.11), channel_id=1, source_target_pairs={{4,0},{8,4},{12,8},{14,12},{10,14},{6,10},{2,6},{0,2},{5,1},{9,5},... | collective-permute-start | bytes 1179656 | tf_op jit(solution)/shard_map/ppermute | solution.py:110
  102.4 14.9 %collective-permute-start.28 = (bf16[512,384]{1,0:T(8,128)(2,1)S(1)}, bf16[512,384]{1,0:T(8,128)(2,1)S(1)}, u32[]{:S(2)}, u32[]{:S(2)}) collective-permute-start(bf16[512,384]{1,0:T(8,128)(2,1)S(1)} %collective-permute-done.26), channel_id=1, source_target_pairs={{0,4},{4,8},{8,12},{12,14},{14,10},{10,6},{6,2},{2,0},{1,5},{5,9},... | collective-permute-start | bytes 1179656 | tf_op jit(solution)/shard_map/ppermute | solution.py:110
  104.0 15.4 %collective-permute-start.29 = (bf16[512,384]{1,0:T(8,128)(2,1)S(1)}, bf16[512,384]{1,0:T(8,128)(2,1)S(1)}, u32[]{:S(2)}, u32[]{:S(2)}) collective-permute-start(bf16[512,384]{1,0:T(8,128)(2,1)S(1)} %collective-permute-done.27), channel_id=1, source_target_pairs={{4,0},{8,4},{12,8},{14,12},{10,14},{6,10},{2,6},{0,2},{5,1},{9,5},... | collective-permute-start | bytes 1179656 | tf_op jit(solution)/shard_map/ppermute | solution.py:110
  109.3 11.3 %collective-permute-start.14 = (bf16[256,384]{1,0:T(8,128)(2,1)S(1)}, bf16[256,384]{1,0:T(8,128)(2,1)S(1)}, u32[]{:S(2)}, u32[]{:S(2)}) collective-permute-start(bf16[256,384]{1,0:T(8,128)(2,1)S(1)} %slice.95), channel_id=1, source_target_pairs={{0,4},{4,8},{8,12},{12,14},{14,10},{10,6},{6,2},{2,0},{1,5},{5,9},... | collective-permute-start | bytes 589832 | tf_op jit(solution)/shard_map/ppermute | solution.py:110
  111.0 11.2 %collective-permute-start.15 = (bf16[256,384]{1,0:T(8,128)(2,1)S(1)}, bf16[256,384]{1,0:T(8,128)(2,1)S(1)}, u32[]{:S(2)}, u32[]{:S(2)}) collective-permute-start(bf16[256,384]{1,0:T(8,128)(2,1)S(1)} %slice.122), channel_id=1, source_target_pairs={{4,0},{8,4},{12,8},{14,12},{10,14},{6,10},{2,6},{0,2},{5,1},{9,5},... | collective-permute-start | bytes 589832 | tf_op jit(solution)/shard_map/ppermute | solution.py:110
  117.3 5.7 %collective-permute-start.30 = (bf16[256,384]{1,0:T(8,128)(2,1)S(1)}, bf16[256,384]{1,0:T(8,128)(2,1)S(1)}, u32[]{:S(2)}, u32[]{:S(2)}) collective-permute-start(bf16[256,384]{1,0:T(8,128)(2,1)S(1)} %slice.109), channel_id=1, source_target_pairs={{0,4},{4,8},{8,12},{12,14},{14,10},{10,6},{6,2},{2,0},{1,5},{5,9},... | collective-permute-start | bytes 589832 | tf_op jit(solution)/shard_map/ppermute | solution.py:110
  119.4 5.7 %collective-permute-start.31 = (bf16[256,384]{1,0:T(8,128)(2,1)S(1)}, bf16[256,384]{1,0:T(8,128)(2,1)S(1)}, u32[]{:S(2)}, u32[]{:S(2)}) collective-permute-start(bf16[256,384]{1,0:T(8,128)(2,1)S(1)} %slice.133), channel_id=1, source_target_pairs={{4,0},{8,4},{12,8},{14,12},{10,14},{6,10},{2,6},{0,2},{5,1},{9,5},... | collective-permute-start | bytes 589832 | tf_op jit(solution)/shard_map/ppermute | solution.py:110
  (4 other events, 20.4 us)

commit v6 on v5

--- a/solution.py
+++ b/solution.py
@@ -36,8 +36,8 @@
     width = entries[0][2].shape[1]
     whole = pl.BlockSpec((depth, width), lambda i, t: (0, 0))
     in_specs = [
-        pl.BlockSpec((1, depth, b.shape[0]), lambda i, t, k=k, h=h, parts=depth // b.shape[0]: (m, 0, t[k] * parts + h))
-        for k, h, b in entries
+        pl.BlockSpec((1, depth, b.shape[0]), lambda i, t, k=k, part=row // b.shape[0], parts=depth // b.shape[0]: (m, 0, t[k] * parts + part))
+        for k, row, b in entries
     ]
     in_specs += [pl.BlockSpec(b.shape, lambda i, t: (0, 0)) for _, _, b in entries] + [whole] * (acc is not None)
     operands = [fisher] * len(entries) + [b for _, _, b in entries] + ([acc] if acc is not None else [])
@@ -93,7 +93,7 @@
     table = jnp.asarray(owners)[lax.axis_index("doc")]
     docs = jnp.swapaxes(documents[0], 0, 1)
 
-    def ring_gather(blocks, state, use, waits):
+    def ring_gather(blocks, state, use, waits, cuts):
         going = [[block, block] for block in blocks]
         fresh = [[(0, 0, block)] for block in blocks]
         final = []
@@ -105,10 +105,9 @@
                     going[m] = ways + going[m][len(ways) :]
                 ways = going[m]
                 if step == n // 2:
-                    half = ways[0].shape[0] // 2
-                    ways = [ways[0][:half], ways[1][half:]]
+                    ways = [ways[0][: cuts[m]], ways[1][cuts[m] :]]
                 going[m] = [lax.ppermute(ways[0], "doc", up), lax.ppermute(ways[1], "doc", down)]
-                arrivals = [(step, 0, going[m][0]), (n - step, step // (n // 2), going[m][1])]
+                arrivals = [(step, 0, going[m][0]), (n - step, cuts[m] * (step // (n // 2)), going[m][1])]
                 if step < n // 2:
                     state[m] = use(m, state[m], fresh[m], False)
                     fresh[m] = arrivals
@@ -117,7 +116,7 @@
         for m in range(modules):
             if m > 0:
                 blocks, _ = lax.optimization_barrier(([block for _, _, block in fresh[m]], state[m - 1]))
-                fresh[m] = [(shift, half, block) for (shift, half, _), block in zip(fresh[m], blocks)]
+                fresh[m] = [(shift, row, block) for (shift, row, _), block in zip(fresh[m], blocks)]
             state[m] = use(m, use(m, state[m], fresh[m], False), final[m], True)
         return state
 
@@ -129,17 +128,17 @@
         blocks.append(lax.optimization_barrier((queries, blocks[-1]))[0][0, m])
     placed = [place(table, doc_order, docs, depth, m) for m in range(modules)]
     waits = {(2, modules - 1): docs, (3, 0): placed[0], (3, modules - 1): placed[1:]}
-    precond = ring_gather(blocks, [None] * modules, add_query, waits)
+    precond = ring_gather(blocks, [None] * modules, add_query, waits, [depth // 2] * modules)
 
     def add_score(m, score, arrivals, last):
-        for shift, half, block in arrivals:
-            rows = block.shape[0]
-            start = shift * depth + half * rows
-            part = dot(placed[m][:, start : start + rows], block)
+        for shift, row, block in arrivals:
+            start = shift * depth + row
+            part = dot(placed[m][:, start : start + block.shape[0]], block)
             score = part if score is None else score + part
         return score
 
-    score = sum(ring_gather(precond, [None] * modules, add_score, {}))
+    cuts = [depth // 2] * (modules - 1) + [depth * 5 // 8]
+    score = sum(ring_gather(precond, [None] * modules, add_score, {}, cuts))
     return score + lax.ppermute(score, "layer", [(0, 1), (1, 0)])
 
 

time: 128 us -> 128 us (level)
    ppermute x16, waiting for transfers between devices: 19 us -> 16.7 us  [ring_gather(): lax.ppermute(ways[1], 'doc', down)]
    ppermute x16, waiting for transfers between devices: 39.5 us -> 41.2 us  [ring_gather(): lax.ppermute(ways[0], 'doc', up)]
where the time goes in v6:
time: 128 us; the launch traced here: 127 us
  waiting for transfers between devices  59.6 us (47%)
  starting transfers between devices  34.4 us (27%)
  Pallas kernels  16.6 us (13%)
  local copies, waits for them, and re-layouts  10.9 us (9%)
  matrix products  4.8 us (4%)
    ppermute x16, waiting for transfers between devices, ring_gather(): lax.ppermute(ways[0], 'doc', up)  41.2 us
    ppermute x16, starting transfers between devices, ring_gather(): lax.ppermute(ways[0], 'doc', up)  29.1 us
    ppermute x16, waiting for transfers between devices, ring_gather(): lax.ppermute(ways[1], 'doc', down)  16.7 us
    pallas_call x10, Pallas kernels, add_precond(): pl.pallas_call(functools.partial(precond_kernel, len(entries), acc is not...  11.4 us
    unnamed x7, local copies, waits for them, and re-layouts  7.96 us
    ppermute x16, starting transfers between devices, ring_gather(): lax.ppermute(ways[1], 'doc', down)  5.2 us
    pallas_call x2, Pallas kernels, place(): pl.pallas_call(place_kernel, out_shape=jax.ShapeDtypeStruct((rows, width)...  5.2 us
    dot_general x18, matrix products, dot(): return jnp.dot(a, b, preferred_element_type=jnp.float32)  4.8 us
  transfers between devices with their start and end apart: 33, of which 26 were waited for; matrix products, arithmetic and copies ran while one was open for 9% of the time, Pallas kernels for 13%

profile of v6, /device:TPU:0, one launch (start us, length us, event | category | flops | bytes accessed | tf_op | source)
XLA Modules:
  0.0 127.4 jit_solution(16713191331290199793)
XLA Ops:
  1.0 3.1 %collective-permute-start = (bf16[512,384]{1,0:T(8,128)(2,1)S(1)}, bf16[512,384]{1,0:T(8,128)(2,1)S(1)}, u32[]{:S(2)}, u32[]{:S(2)}) collective-permute-start(bf16[512,384]{1,0:T(8,128)(2,1)S(1)} %slice_bitcast_fusion.1.refs_1_), channel_id=1, source_target_pairs={{0,4},{4,8},{8,12},{12,14},{14,10},{10,6},{6,2},{2,0},{1,5},{5,9},... | collective-permute-start | bytes 1179656 | tf_op jit(solution)/shard_map/ppermute | solution.py:109
  5.2 2.1 %collective-permute-start.16 = (bf16[512,384]{1,0:T(8,128)(2,1)S(1)}, bf16[512,384]{1,0:T(8,128)(2,1)S(1)}, u32[]{:S(2)}, u32[]{:S(2)}) collective-permute-start(bf16[512,384]{1,0:T(8,128)(2,1)S(1)} %slice_bitcast_fusion.refs_1_), channel_id=1, source_target_pairs={{0,4},{4,8},{8,12},{12,14},{14,10},{10,6},{6,2},{2,0},{1,5},{5,9},... | collective-permute-start | bytes 1179656 | tf_op jit(solution)/shard_map/ppermute | solution.py:109
  7.9 3.4 %copy-done = bf16[1,2,512,4096]{3,2,1,0:T(8,128)(2,1)S(1)} copy-done((bf16[1,2,512,4096]{3,2,1,0:T(8,128)(2,1)S(1)}, bf16[1,2,512,4096]{3,2,1,0:T(8,128)(2,1)}, u32[]{:S(2)}) %copy-start) | copy-done | bytes 8388632
  12.3 1.7 %collective-permute-done.refs_2_ = bf16[512,384]{1,0:T(8,128)(2,1)S(1)} collective-permute-done((bf16[512,384]{1,0:T(8,128)(2,1)S(1)}, bf16[512,384]{1,0:T(8,128)(2,1)S(1)}, u32[]{:S(2)}, u32[]{:S(2)}) %collective-permute-start) | collective-permute-done | bytes 393248 | tf_op jit(solution)/shard_map/ppermute | solution.py:109
  14.0 2.2 %collective-permute-done.1.refs_3_ = bf16[512,384]{1,0:T(8,128)(2,1)S(1)} collective-permute-done((bf16[512,384]{1,0:T(8,128)(2,1)S(1)}, bf16[512,384]{1,0:T(8,128)(2,1)S(1)}, u32[]{:S(2)}, u32[]{:S(2)}) %collective-permute-start.1) | collective-permute-done | bytes 393248 | tf_op jit(solution)/shard_map/ppermute | solution.py:109
  18.2 4.6 %copy.8 = bf16[1,224,2,4096]{3,1,2,0:T(8,128)(2,1)S(1)} copy(bf16[1,224,2,4096]{3,2,1,0:T(2,128)(2,1)} %param.7) | data formatting | bytes 7340032 | tf_op args[2]
  26.6 2.6 %shard_map.57 = bf16[224,4096]{1,0:T(8,128)(2,1)S(1)} custom-call(s32[8]{0:T(128)S(1)} %dynamic-slice_bitcast_fusion.table, s32[1,224]{1,0:T(1,128)S(1)} %copy-done.2, bf16[2,224,4096]{2,1,0:T(8,128)(2,1)S(1)} %bitcast.48), custom_call_target="tpu_custom_call" | custom-call | flops 411041792 | bytes 3670016 | tf_op jit(solution)/shard_map/pallas_call | solution.py:66
  30.8 2.2 %collective-permute-done.3.refs_3_ = bf16[512,384]{1,0:T(8,128)(2,1)S(1)} collective-permute-done((bf16[512,384]{1,0:T(8,128)(2,1)S(1)}, bf16[512,384]{1,0:T(8,128)(2,1)S(1)}, u32[]{:S(2)}, u32[]{:S(2)}) %collective-permute-start.3) | collective-permute-done | bytes 393248 | tf_op jit(solution)/shard_map/ppermute | solution.py:109
  33.0 1.6 %collective-permute-start.4 = (bf16[512,384]{1,0:T(8,128)(2,1)S(1)}, bf16[512,384]{1,0:T(8,128)(2,1)S(1)}, u32[]{:S(2)}, u32[]{:S(2)}) collective-permute-start(bf16[512,384]{1,0:T(8,128)(2,1)S(1)} %collective-permute-done.2.refs_2_), channel_id=1, source_target_pairs={{0,4},{4,8},{8,12},{12,14},{14,10},{10,6},{6,2},{2,0},{1,5},{5,9},... | collective-permute-start | bytes 1179656 | tf_op jit(solution)/shard_map/ppermute | solution.py:109
  35.0 2.6 %shard_map.63 = bf16[224,4096]{1,0:T(8,128)(2,1)S(1)} custom-call(s32[8]{0:T(128)S(1)} %dynamic-slice_bitcast_fusion.table, s32[1,224]{1,0:T(1,128)S(1)} %copy-done.2, bf16[2,224,4096]{2,1,0:T(8,128)(2,1)S(1)} %bitcast.49), custom_call_target="tpu_custom_call" | custom-call | flops 411041792 | bytes 3670016 | tf_op jit(solution)/shard_map/pallas_call | solution.py:66
  39.3 2.2 %collective-permute-done.19.refs_3_ = bf16[512,384]{1,0:T(8,128)(2,1)S(1)} collective-permute-done((bf16[512,384]{1,0:T(8,128)(2,1)S(1)}, bf16[512,384]{1,0:T(8,128)(2,1)S(1)}, u32[]{:S(2)}, u32[]{:S(2)}) %collective-permute-start.19) | collective-permute-done | bytes 393248 | tf_op jit(solution)/shard_map/ppermute | solution.py:109
  44.7 3.0 %collective-permute-done.4.refs_2_ = bf16[512,384]{1,0:T(8,128)(2,1)S(1)} collective-permute-done((bf16[512,384]{1,0:T(8,128)(2,1)S(1)}, bf16[512,384]{1,0:T(8,128)(2,1)S(1)}, u32[]{:S(2)}, u32[]{:S(2)}) %collective-permute-start.4) | collective-permute-done | bytes 393248 | tf_op jit(solution)/shard_map/ppermute | solution.py:109
  47.7 2.2 %collective-permute-start.5 = (bf16[256,384]{1,0:T(8,128)(2,1)S(1)}, bf16[256,384]{1,0:T(8,128)(2,1)S(1)}, u32[]{:S(2)}, u32[]{:S(2)}) collective-permute-start(bf16[256,384]{1,0:T(8,128)(2,1)S(1)} %slice.85), channel_id=1, source_target_pairs={{0,4},{4,8},{8,12},{12,14},{14,10},{10,6},{6,2},{2,0},{1,5},{5,9},... | collective-permute-start | bytes 589832 | tf_op jit(solution)/shard_map/ppermute | solution.py:109
  51.2 4.9 %collective-permute-done.20.refs_2_ = bf16[512,384]{1,0:T(8,128)(2,1)S(1)} collective-permute-done((bf16[512,384]{1,0:T(8,128)(2,1)S(1)}, bf16[512,384]{1,0:T(8,128)(2,1)S(1)}, u32[]{:S(2)}, u32[]{:S(2)}) %collective-permute-start.20) | collective-permute-done | bytes 393248 | tf_op jit(solution)/shard_map/ppermute | solution.py:109
  56.1 2.2 %collective-permute-start.21 = (bf16[256,384]{1,0:T(8,128)(2,1)S(1)}, bf16[256,384]{1,0:T(8,128)(2,1)S(1)}, u32[]{:S(2)}, u32[]{:S(2)}) collective-permute-start(bf16[256,384]{1,0:T(8,128)(2,1)S(1)} %slice.99), channel_id=1, source_target_pairs={{0,4},{4,8},{8,12},{12,14},{14,10},{10,6},{6,2},{2,0},{1,5},{5,9},... | collective-permute-start | bytes 589832 | tf_op jit(solution)/shard_map/ppermute | solution.py:109
  60.3 2.2 %collective-permute-done.7.refs_3_ = bf16[256,384]{1,0:T(8,128)(2,1)S(1)} collective-permute-done((bf16[256,384]{1,0:T(8,128)(2,1)S(1)}, bf16[256,384]{1,0:T(8,128)(2,1)S(1)}, u32[]{:S(2)}, u32[]{:S(2)}) %collective-permute-start.7) | collective-permute-done | bytes 196640 | tf_op jit(solution)/shard_map/ppermute | solution.py:109
  63.5 1.6 %collective-permute-start.8 = (bf16[512,384]{1,0:T(8,128)(2,1)S(1)}, bf16[512,384]{1,0:T(8,128)(2,1)S(1)}, u32[]{:S(2)}, u32[]{:S(2)}) collective-permute-start(bf16[512,384]{1,0:T(8,128)(2,1)S(1)} %shard_map.60), channel_id=1, source_target_pairs={{0,4},{4,8},{8,12},{12,14},{14,10},{10,6},{6,2},{2,0},{1,5},{5,9},... | collective-permute-start | bytes 1179656 | tf_op jit(solution)/shard_map/ppermute | solution.py:109
  67.8 1.6 %collective-permute-start.24 = (bf16[512,384]{1,0:T(8,128)(2,1)S(1)}, bf16[512,384]{1,0:T(8,128)(2,1)S(1)}, u32[]{:S(2)}, u32[]{:S(2)}) collective-permute-start(bf16[512,384]{1,0:T(8,128)(2,1)S(1)} %shard_map.66), channel_id=1, source_target_pairs={{0,4},{4,8},{8,12},{12,14},{14,10},{10,6},{6,2},{2,0},{1,5},{5,9},... | collective-permute-start | bytes 1179656 | tf_op jit(solution)/shard_map/ppermute | solution.py:109
  70.5 5.1 %collective-permute-done.8 = bf16[512,384]{1,0:T(8,128)(2,1)S(1)} collective-permute-done((bf16[512,384]{1,0:T(8,128)(2,1)S(1)}, bf16[512,384]{1,0:T(8,128)(2,1)S(1)}, u32[]{:S(2)}, u32[]{:S(2)}) %collective-permute-start.8) | collective-permute-done | bytes 393248 | tf_op jit(solution)/shard_map/ppermute | solution.py:109
  75.6 1.6 %collective-permute-done.9 = bf16[512,384]{1,0:T(8,128)(2,1)S(1)} collective-permute-done((bf16[512,384]{1,0:T(8,128)(2,1)S(1)}, bf16[512,384]{1,0:T(8,128)(2,1)S(1)}, u32[]{:S(2)}, u32[]{:S(2)}) %collective-permute-start.9) | collective-permute-done | bytes 393248 | tf_op jit(solution)/shard_map/ppermute | solution.py:109
  79.2 4.8 %collective-permute-done.24 = bf16[512,384]{1,0:T(8,128)(2,1)S(1)} collective-permute-done((bf16[512,384]{1,0:T(8,128)(2,1)S(1)}, bf16[512,384]{1,0:T(8,128)(2,1)S(1)}, u32[]{:S(2)}, u32[]{:S(2)}) %collective-permute-start.24) | collective-permute-done | bytes 393248 | tf_op jit(solution)/shard_map/ppermute | solution.py:109
  84.0 1.6 %collective-permute-done.25 = bf16[512,384]{1,0:T(8,128)(2,1)S(1)} collective-permute-done((bf16[512,384]{1,0:T(8,128)(2,1)S(1)}, bf16[512,384]{1,0:T(8,128)(2,1)S(1)}, u32[]{:S(2)}, u32[]{:S(2)}) %collective-permute-start.25) | collective-permute-done | bytes 393248 | tf_op jit(solution)/shard_map/ppermute | solution.py:109
  88.8 3.7 %collective-permute-done.10 = bf16[512,384]{1,0:T(8,128)(2,1)S(1)} collective-permute-done((bf16[512,384]{1,0:T(8,128)(2,1)S(1)}, bf16[512,384]{1,0:T(8,128)(2,1)S(1)}, u32[]{:S(2)}, u32[]{:S(2)}) %collective-permute-start.10) | collective-permute-done | bytes 393248 | tf_op jit(solution)/shard_map/ppermute | solution.py:109
  92.4 1.6 %collective-permute-done.11 = bf16[512,384]{1,0:T(8,128)(2,1)S(1)} collective-permute-done((bf16[512,384]{1,0:T(8,128)(2,1)S(1)}, bf16[512,384]{1,0:T(8,128)(2,1)S(1)}, u32[]{:S(2)}, u32[]{:S(2)}) %collective-permute-start.11) | collective-permute-done | bytes 393248 | tf_op jit(solution)/shard_map/ppermute | solution.py:109
  94.0 1.6 %collective-permute-start.12 = (bf16[512,384]{1,0:T(8,128)(2,1)S(1)}, bf16[512,384]{1,0:T(8,128)(2,1)S(1)}, u32[]{:S(2)}, u32[]{:S(2)}) collective-permute-start(bf16[512,384]{1,0:T(8,128)(2,1)S(1)} %collective-permute-done.10), channel_id=1, source_target_pairs={{0,4},{4,8},{8,12},{12,14},{14,10},{10,6},{6,2},{2,0},{1,5},{5,9},... | collective-permute-start | bytes 1179656 | tf_op jit(solution)/shard_map/ppermute | solution.py:109
  96.0 4.8 %collective-permute-done.26 = bf16[512,384]{1,0:T(8,128)(2,1)S(1)} collective-permute-done((bf16[512,384]{1,0:T(8,128)(2,1)S(1)}, bf16[512,384]{1,0:T(8,128)(2,1)S(1)}, u32[]{:S(2)}, u32[]{:S(2)}) %collective-permute-start.26) | collective-permute-done | bytes 393248 | tf_op jit(solution)/shard_map/ppermute | solution.py:109
  100.9 1.6 %collective-permute-done.27 = bf16[512,384]{1,0:T(8,128)(2,1)S(1)} collective-permute-done((bf16[512,384]{1,0:T(8,128)(2,1)S(1)}, bf16[512,384]{1,0:T(8,128)(2,1)S(1)}, u32[]{:S(2)}, u32[]{:S(2)}) %collective-permute-start.27) | collective-permute-done | bytes 393248 | tf_op jit(solution)/shard_map/ppermute | solution.py:109
  105.6 3.7 %collective-permute-done.12 = bf16[512,384]{1,0:T(8,128)(2,1)S(1)} collective-permute-done((bf16[512,384]{1,0:T(8,128)(2,1)S(1)}, bf16[512,384]{1,0:T(8,128)(2,1)S(1)}, u32[]{:S(2)}, u32[]{:S(2)}) %collective-permute-start.12) | collective-permute-done | bytes 393248 | tf_op jit(solution)/shard_map/ppermute | solution.py:109
  109.3 1.6 %collective-permute-start.14 = (bf16[256,384]{1,0:T(8,128)(2,1)S(1)}, bf16[256,384]{1,0:T(8,128)(2,1)S(1)}, u32[]{:S(2)}, u32[]{:S(2)}) collective-permute-start(bf16[256,384]{1,0:T(8,128)(2,1)S(1)} %slice.95), channel_id=1, source_target_pairs={{0,4},{4,8},{8,12},{12,14},{14,10},{10,6},{6,2},{2,0},{1,5},{5,9},... | collective-permute-start | bytes 589832 | tf_op jit(solution)/shard_map/ppermute | solution.py:109
  111.5 5.8 %collective-permute-done.28 = bf16[512,384]{1,0:T(8,128)(2,1)S(1)} collective-permute-done((bf16[512,384]{1,0:T(8,128)(2,1)S(1)}, bf16[512,384]{1,0:T(8,128)(2,1)S(1)}, u32[]{:S(2)}, u32[]{:S(2)}) %collective-permute-start.28) | collective-permute-done | bytes 393248 | tf_op jit(solution)/shard_map/ppermute | solution.py:109
  117.3 2.0 %collective-permute-start.30 = (bf16[320,384]{1,0:T(8,128)(2,1)S(1)}, bf16[320,384]{1,0:T(8,128)(2,1)S(1)}, u32[]{:S(2)}, u32[]{:S(2)}) collective-permute-start(bf16[320,384]{1,0:T(8,128)(2,1)S(1)} %slice.109), channel_id=1, source_target_pairs={{0,4},{4,8},{8,12},{12,14},{14,10},{10,6},{6,2},{2,0},{1,5},{5,9},... | collective-permute-start | bytes 737288 | tf_op jit(solution)/shard_map/ppermute | solution.py:109
  125.0 1.6 %collective-permute-done.32 = f32[224,384]{1,0:T(8,128)S(1)} collective-permute-done((f32[224,384]{1,0:T(8,128)S(1)}, f32[224,384]{1,0:T(8,128)S(1)}, u32[]{:S(2)}, u32[]{:S(2)}) %collective-permute-start.32) | collective-permute-done | bytes 344096 | tf_op jit(solution)/shard_map/ppermute | solution.py:142
  (83 shorter events, 40.1 us)
Async XLA Ops:
  1.0 12.9 %collective-permute-start = (bf16[512,384]{1,0:T(8,128)(2,1)S(1)}, bf16[512,384]{1,0:T(8,128)(2,1)S(1)}, u32[]{:S(2)}, u32[]{:S(2)}) collective-permute-start(bf16[512,384]{1,0:T(8,128)(2,1)S(1)} %slice_bitcast_fusion.1.refs_1_), channel_id=1, source_target_pairs={{0,4},{4,8},{8,12},{12,14},{14,10},{10,6},{6,2},{2,0},{1,5},{5,9},... | collective-permute-start | bytes 1179656 | tf_op jit(solution)/shard_map/ppermute | solution.py:109
  4.1 12.0 %collective-permute-start.1 = (bf16[512,384]{1,0:T(8,128)(2,1)S(1)}, bf16[512,384]{1,0:T(8,128)(2,1)S(1)}, u32[]{:S(2)}, u32[]{:S(2)}) collective-permute-start(bf16[512,384]{1,0:T(8,128)(2,1)S(1)} %slice_bitcast_fusion.1.refs_1_), channel_id=1, source_target_pairs={{4,0},{8,4},{12,8},{14,12},{10,14},{6,10},{2,6},{0,2},{5,1},{9,5},... | collective-permute-start | bytes 1179656 | tf_op jit(solution)/shard_map/ppermute | solution.py:109
  5.2 18.6 %collective-permute-start.16 = (bf16[512,384]{1,0:T(8,128)(2,1)S(1)}, bf16[512,384]{1,0:T(8,128)(2,1)S(1)}, u32[]{:S(2)}, u32[]{:S(2)}) collective-permute-start(bf16[512,384]{1,0:T(8,128)(2,1)S(1)} %slice_bitcast_fusion.refs_1_), channel_id=1, source_target_pairs={{0,4},{4,8},{8,12},{12,14},{14,10},{10,6},{6,2},{2,0},{1,5},{5,9},... | collective-permute-start | bytes 1179656 | tf_op jit(solution)/shard_map/ppermute | solution.py:109
  7.2 17.3 %collective-permute-start.17 = (bf16[512,384]{1,0:T(8,128)(2,1)S(1)}, bf16[512,384]{1,0:T(8,128)(2,1)S(1)}, u32[]{:S(2)}, u32[]{:S(2)}) collective-permute-start(bf16[512,384]{1,0:T(8,128)(2,1)S(1)} %slice_bitcast_fusion.refs_1_), channel_id=1, source_target_pairs={{4,0},{8,4},{12,8},{14,12},{10,14},{6,10},{2,6},{0,2},{5,1},{9,5},... | collective-permute-start | bytes 1179656 | tf_op jit(solution)/shard_map/ppermute | solution.py:109
  16.2 14.7 %collective-permute-start.2 = (bf16[512,384]{1,0:T(8,128)(2,1)S(1)}, bf16[512,384]{1,0:T(8,128)(2,1)S(1)}, u32[]{:S(2)}, u32[]{:S(2)}) collective-permute-start(bf16[512,384]{1,0:T(8,128)(2,1)S(1)} %collective-permute-done.refs_2_), channel_id=1, source_target_pairs={{0,4},{4,8},{8,12},{12,14},{14,10},{10,6},{6,2},{2,0},{1,5},{5,9},... | collective-permute-start | bytes 1179656 | tf_op jit(solution)/shard_map/ppermute | solution.py:109
  17.7 15.3 %collective-permute-start.3 = (bf16[512,384]{1,0:T(8,128)(2,1)S(1)}, bf16[512,384]{1,0:T(8,128)(2,1)S(1)}, u32[]{:S(2)}, u32[]{:S(2)}) collective-permute-start(bf16[512,384]{1,0:T(8,128)(2,1)S(1)} %collective-permute-done.1.refs_3_), channel_id=1, source_target_pairs={{4,0},{8,4},{12,8},{14,12},{10,14},{6,10},{2,6},{0,2},{5,1},{9,5},... | collective-permute-start | bytes 1179656 | tf_op jit(solution)/shard_map/ppermute | solution.py:109
  24.6 14.7 %collective-permute-start.18 = (bf16[512,384]{1,0:T(8,128)(2,1)S(1)}, bf16[512,384]{1,0:T(8,128)(2,1)S(1)}, u32[]{:S(2)}, u32[]{:S(2)}) collective-permute-start(bf16[512,384]{1,0:T(8,128)(2,1)S(1)} %collective-permute-done.16.refs_2_), channel_id=1, source_target_pairs={{0,4},{4,8},{8,12},{12,14},{14,10},{10,6},{6,2},{2,0},{1,5},{5,9},... | collective-permute-start | bytes 1179656 | tf_op jit(solution)/shard_map/ppermute | solution.py:109
  26.2 15.3 %collective-permute-start.19 = (bf16[512,384]{1,0:T(8,128)(2,1)S(1)}, bf16[512,384]{1,0:T(8,128)(2,1)S(1)}, u32[]{:S(2)}, u32[]{:S(2)}) collective-permute-start(bf16[512,384]{1,0:T(8,128)(2,1)S(1)} %collective-permute-done.17.refs_3_), channel_id=1, source_target_pairs={{4,0},{8,4},{12,8},{14,12},{10,14},{6,10},{2,6},{0,2},{5,1},{9,5},... | collective-permute-start | bytes 1179656 | tf_op jit(solution)/shard_map/ppermute | solution.py:109
  33.0 14.7 %collective-permute-start.4 = (bf16[512,384]{1,0:T(8,128)(2,1)S(1)}, bf16[512,384]{1,0:T(8,128)(2,1)S(1)}, u32[]{:S(2)}, u32[]{:S(2)}) collective-permute-start(bf16[512,384]{1,0:T(8,128)(2,1)S(1)} %collective-permute-done.2.refs_2_), channel_id=1, source_target_pairs={{0,4},{4,8},{8,12},{12,14},{14,10},{10,6},{6,2},{2,0},{1,5},{5,9},... | collective-permute-start | bytes 1179656 | tf_op jit(solution)/shard_map/ppermute | solution.py:109
  34.6 15.3 %collective-permute-start.6 = (bf16[512,384]{1,0:T(8,128)(2,1)S(1)}, bf16[512,384]{1,0:T(8,128)(2,1)S(1)}, u32[]{:S(2)}, u32[]{:S(2)}) collective-permute-start(bf16[512,384]{1,0:T(8,128)(2,1)S(1)} %collective-permute-done.3.refs_3_), channel_id=1, source_target_pairs={{4,0},{8,4},{12,8},{14,12},{10,14},{6,10},{2,6},{0,2},{5,1},{9,5},... | collective-permute-start | bytes 1179656 | tf_op jit(solution)/shard_map/ppermute | solution.py:109
  41.4 14.7 %collective-permute-start.20 = (bf16[512,384]{1,0:T(8,128)(2,1)S(1)}, bf16[512,384]{1,0:T(8,128)(2,1)S(1)}, u32[]{:S(2)}, u32[]{:S(2)}) collective-permute-start(bf16[512,384]{1,0:T(8,128)(2,1)S(1)} %collective-permute-done.18.refs_2_), channel_id=1, source_target_pairs={{0,4},{4,8},{8,12},{12,14},{14,10},{10,6},{6,2},{2,0},{1,5},{5,9},... | collective-permute-start | bytes 1179656 | tf_op jit(solution)/shard_map/ppermute | solution.py:109
  43.0 15.3 %collective-permute-start.22 = (bf16[512,384]{1,0:T(8,128)(2,1)S(1)}, bf16[512,384]{1,0:T(8,128)(2,1)S(1)}, u32[]{:S(2)}, u32[]{:S(2)}) collective-permute-start(bf16[512,384]{1,0:T(8,128)(2,1)S(1)} %collective-permute-done.19.refs_3_), channel_id=1, source_target_pairs={{4,0},{8,4},{12,8},{14,12},{10,14},{6,10},{2,6},{0,2},{5,1},{9,5},... | collective-permute-start | bytes 1179656 | tf_op jit(solution)/shard_map/ppermute | solution.py:109
  47.7 12.6 %collective-permute-start.5 = (bf16[256,384]{1,0:T(8,128)(2,1)S(1)}, bf16[256,384]{1,0:T(8,128)(2,1)S(1)}, u32[]{:S(2)}, u32[]{:S(2)}) collective-permute-start(bf16[256,384]{1,0:T(8,128)(2,1)S(1)} %slice.85), channel_id=1, source_target_pairs={{0,4},{4,8},{8,12},{12,14},{14,10},{10,6},{6,2},{2,0},{1,5},{5,9},... | collective-permute-start | bytes 589832 | tf_op jit(solution)/shard_map/ppermute | solution.py:109
  49.9 12.6 %collective-permute-start.7 = (bf16[256,384]{1,0:T(8,128)(2,1)S(1)}, bf16[256,384]{1,0:T(8,128)(2,1)S(1)}, u32[]{:S(2)}, u32[]{:S(2)}) collective-permute-start(bf16[256,384]{1,0:T(8,128)(2,1)S(1)} %slice.112), channel_id=1, source_target_pairs={{4,0},{8,4},{12,8},{14,12},{10,14},{6,10},{2,6},{0,2},{5,1},{9,5},... | collective-permute-start | bytes 589832 | tf_op jit(solution)/shard_map/ppermute | solution.py:109
  56.1 10.7 %collective-permute-start.21 = (bf16[256,384]{1,0:T(8,128)(2,1)S(1)}, bf16[256,384]{1,0:T(8,128)(2,1)S(1)}, u32[]{:S(2)}, u32[]{:S(2)}) collective-permute-start(bf16[256,384]{1,0:T(8,128)(2,1)S(1)} %slice.99), channel_id=1, source_target_pairs={{0,4},{4,8},{8,12},{12,14},{14,10},{10,6},{6,2},{2,0},{1,5},{5,9},... | collective-permute-start | bytes 589832 | tf_op jit(solution)/shard_map/ppermute | solution.py:109
  58.4 8.5 %collective-permute-start.23 = (bf16[256,384]{1,0:T(8,128)(2,1)S(1)}, bf16[256,384]{1,0:T(8,128)(2,1)S(1)}, u32[]{:S(2)}, u32[]{:S(2)}) collective-permute-start(bf16[256,384]{1,0:T(8,128)(2,1)S(1)} %slice.123), channel_id=1, source_target_pairs={{4,0},{8,4},{12,8},{14,12},{10,14},{6,10},{2,6},{0,2},{5,1},{9,5},... | collective-permute-start | bytes 589832 | tf_op jit(solution)/shard_map/ppermute | solution.py:109
  63.5 12.1 %collective-permute-start.8 = (bf16[512,384]{1,0:T(8,128)(2,1)S(1)}, bf16[512,384]{1,0:T(8,128)(2,1)S(1)}, u32[]{:S(2)}, u32[]{:S(2)}) collective-permute-start(bf16[512,384]{1,0:T(8,128)(2,1)S(1)} %shard_map.60), channel_id=1, source_target_pairs={{0,4},{4,8},{8,12},{12,14},{14,10},{10,6},{6,2},{2,0},{1,5},{5,9},... | collective-permute-start | bytes 1179656 | tf_op jit(solution)/shard_map/ppermute | solution.py:109
  65.1 12.1 %collective-permute-start.9 = (bf16[512,384]{1,0:T(8,128)(2,1)S(1)}, bf16[512,384]{1,0:T(8,128)(2,1)S(1)}, u32[]{:S(2)}, u32[]{:S(2)}) collective-permute-start(bf16[512,384]{1,0:T(8,128)(2,1)S(1)} %shard_map.60), channel_id=1, source_target_pairs={{4,0},{8,4},{12,8},{14,12},{10,14},{6,10},{2,6},{0,2},{5,1},{9,5},... | collective-permute-start | bytes 1179656 | tf_op jit(solution)/shard_map/ppermute | solution.py:109
  67.8 16.2 %collective-permute-start.24 = (bf16[512,384]{1,0:T(8,128)(2,1)S(1)}, bf16[512,384]{1,0:T(8,128)(2,1)S(1)}, u32[]{:S(2)}, u32[]{:S(2)}) collective-permute-start(bf16[512,384]{1,0:T(8,128)(2,1)S(1)} %shard_map.66), channel_id=1, source_target_pairs={{0,4},{4,8},{8,12},{12,14},{14,10},{10,6},{6,2},{2,0},{1,5},{5,9},... | collective-permute-start | bytes 1179656 | tf_op jit(solution)/shard_map/ppermute | solution.py:109
  69.4 16.1 %collective-permute-start.25 = (bf16[512,384]{1,0:T(8,128)(2,1)S(1)}, bf16[512,384]{1,0:T(8,128)(2,1)S(1)}, u32[]{:S(2)}, u32[]{:S(2)}) collective-permute-start(bf16[512,384]{1,0:T(8,128)(2,1)S(1)} %shard_map.66), channel_id=1, source_target_pairs={{4,0},{8,4},{12,8},{14,12},{10,14},{6,10},{2,6},{0,2},{5,1},{9,5},... | collective-permute-start | bytes 1179656 | tf_op jit(solution)/shard_map/ppermute | solution.py:109
  77.2 15.3 %collective-permute-start.10 = (bf16[512,384]{1,0:T(8,128)(2,1)S(1)}, bf16[512,384]{1,0:T(8,128)(2,1)S(1)}, u32[]{:S(2)}, u32[]{:S(2)}) collective-permute-start(bf16[512,384]{1,0:T(8,128)(2,1)S(1)} %collective-permute-done.8), channel_id=1, source_target_pairs={{0,4},{4,8},{8,12},{12,14},{14,10},{10,6},{6,2},{2,0},{1,5},{5,9},... | collective-permute-start | bytes 1179656 | tf_op jit(solution)/shard_map/ppermute | solution.py:109
  78.7 15.3 %collective-permute-start.11 = (bf16[512,384]{1,0:T(8,128)(2,1)S(1)}, bf16[512,384]{1,0:T(8,128)(2,1)S(1)}, u32[]{:S(2)}, u32[]{:S(2)}) collective-permute-start(bf16[512,384]{1,0:T(8,128)(2,1)S(1)} %collective-permute-done.9), channel_id=1, source_target_pairs={{4,0},{8,4},{12,8},{14,12},{10,14},{6,10},{2,6},{0,2},{5,1},{9,5},... | collective-permute-start | bytes 1179656 | tf_op jit(solution)/shard_map/ppermute | solution.py:109
  85.6 15.3 %collective-permute-start.26 = (bf16[512,384]{1,0:T(8,128)(2,1)S(1)}, bf16[512,384]{1,0:T(8,128)(2,1)S(1)}, u32[]{:S(2)}, u32[]{:S(2)}) collective-permute-start(bf16[512,384]{1,0:T(8,128)(2,1)S(1)} %collective-permute-done.24), channel_id=1, source_target_pairs={{0,4},{4,8},{8,12},{12,14},{14,10},{10,6},{6,2},{2,0},{1,5},{5,9},... | collective-permute-start | bytes 1179656 | tf_op jit(solution)/shard_map/ppermute | solution.py:109
  87.2 15.3 %collective-permute-start.27 = (bf16[512,384]{1,0:T(8,128)(2,1)S(1)}, bf16[512,384]{1,0:T(8,128)(2,1)S(1)}, u32[]{:S(2)}, u32[]{:S(2)}) collective-permute-start(bf16[512,384]{1,0:T(8,128)(2,1)S(1)} %collective-permute-done.25), channel_id=1, source_target_pairs={{4,0},{8,4},{12,8},{14,12},{10,14},{6,10},{2,6},{0,2},{5,1},{9,5},... | collective-permute-start | bytes 1179656 | tf_op jit(solution)/shard_map/ppermute | solution.py:109
  94.0 15.3 %collective-permute-start.12 = (bf16[512,384]{1,0:T(8,128)(2,1)S(1)}, bf16[512,384]{1,0:T(8,128)(2,1)S(1)}, u32[]{:S(2)}, u32[]{:S(2)}) collective-permute-start(bf16[512,384]{1,0:T(8,128)(2,1)S(1)} %collective-permute-done.10), channel_id=1, source_target_pairs={{0,4},{4,8},{8,12},{12,14},{14,10},{10,6},{6,2},{2,0},{1,5},{5,9},... | collective-permute-start | bytes 1179656 | tf_op jit(solution)/shard_map/ppermute | solution.py:109
  95.6 15.4 %collective-permute-start.13 = (bf16[512,384]{1,0:T(8,128)(2,1)S(1)}, bf16[512,384]{1,0:T(8,128)(2,1)S(1)}, u32[]{:S(2)}, u32[]{:S(2)}) collective-permute-start(bf16[512,384]{1,0:T(8,128)(2,1)S(1)} %collective-permute-done.11), channel_id=1, source_target_pairs={{4,0},{8,4},{12,8},{14,12},{10,14},{6,10},{2,6},{0,2},{5,1},{9,5},... | collective-permute-start | bytes 1179656 | tf_op jit(solution)/shard_map/ppermute | solution.py:109
  102.4 14.9 %collective-permute-start.28 = (bf16[512,384]{1,0:T(8,128)(2,1)S(1)}, bf16[512,384]{1,0:T(8,128)(2,1)S(1)}, u32[]{:S(2)}, u32[]{:S(2)}) collective-permute-start(bf16[512,384]{1,0:T(8,128)(2,1)S(1)} %collective-permute-done.26), channel_id=1, source_target_pairs={{0,4},{4,8},{8,12},{12,14},{14,10},{10,6},{6,2},{2,0},{1,5},{5,9},... | collective-permute-start | bytes 1179656 | tf_op jit(solution)/shard_map/ppermute | solution.py:109
  104.0 15.4 %collective-permute-start.29 = (bf16[512,384]{1,0:T(8,128)(2,1)S(1)}, bf16[512,384]{1,0:T(8,128)(2,1)S(1)}, u32[]{:S(2)}, u32[]{:S(2)}) collective-permute-start(bf16[512,384]{1,0:T(8,128)(2,1)S(1)} %collective-permute-done.27), channel_id=1, source_target_pairs={{4,0},{8,4},{12,8},{14,12},{10,14},{6,10},{2,6},{0,2},{5,1},{9,5},... | collective-permute-start | bytes 1179656 | tf_op jit(solution)/shard_map/ppermute | solution.py:109
  109.3 11.8 %collective-permute-start.14 = (bf16[256,384]{1,0:T(8,128)(2,1)S(1)}, bf16[256,384]{1,0:T(8,128)(2,1)S(1)}, u32[]{:S(2)}, u32[]{:S(2)}) collective-permute-start(bf16[256,384]{1,0:T(8,128)(2,1)S(1)} %slice.95), channel_id=1, source_target_pairs={{0,4},{4,8},{8,12},{12,14},{14,10},{10,6},{6,2},{2,0},{1,5},{5,9},... | collective-permute-start | bytes 589832 | tf_op jit(solution)/shard_map/ppermute | solution.py:109
  111.0 10.6 %collective-permute-start.15 = (bf16[256,384]{1,0:T(8,128)(2,1)S(1)}, bf16[256,384]{1,0:T(8,128)(2,1)S(1)}, u32[]{:S(2)}, u32[]{:S(2)}) collective-permute-start(bf16[256,384]{1,0:T(8,128)(2,1)S(1)} %slice.122), channel_id=1, source_target_pairs={{4,0},{8,4},{12,8},{14,12},{10,14},{6,10},{2,6},{0,2},{5,1},{9,5},... | collective-permute-start | bytes 589832 | tf_op jit(solution)/shard_map/ppermute | solution.py:109
  117.3 6.4 %collective-permute-start.30 = (bf16[320,384]{1,0:T(8,128)(2,1)S(1)}, bf16[320,384]{1,0:T(8,128)(2,1)S(1)}, u32[]{:S(2)}, u32[]{:S(2)}) collective-permute-start(bf16[320,384]{1,0:T(8,128)(2,1)S(1)} %slice.109), channel_id=1, source_target_pairs={{0,4},{4,8},{8,12},{12,14},{14,10},{10,6},{6,2},{2,0},{1,5},{5,9},... | collective-permute-start | bytes 737288 | tf_op jit(solution)/shard_map/ppermute | solution.py:109
  119.4 5.2 %collective-permute-start.31 = (bf16[192,384]{1,0:T(8,128)(2,1)S(1)}, bf16[192,384]{1,0:T(8,128)(2,1)S(1)}, u32[]{:S(2)}, u32[]{:S(2)}) collective-permute-start(bf16[192,384]{1,0:T(8,128)(2,1)S(1)} %slice.133), channel_id=1, source_target_pairs={{4,0},{8,4},{12,8},{14,12},{10,14},{6,10},{2,6},{0,2},{5,1},{9,5},... | collective-permute-start | bytes 442376 | tf_op jit(solution)/shard_map/ppermute | solution.py:109
  (4 other events, 20.4 us)

commit v7 on v6

--- a/solution.py
+++ b/solution.py
@@ -100,7 +100,7 @@
         for step in range(1, n // 2 + 1):
             for m in range(modules):
                 if step > 1:
-                    ways = going[m] if step < n // 2 else going[m][:1]
+                    ways = going[m] if step < n // 2 or m < modules - 1 else going[m][:1]
                     ways, state[m], _ = lax.optimization_barrier((ways, state[m], waits.get((step, m), ())))
                     going[m] = ways + going[m][len(ways) :]
                 ways = going[m]

time: 128 us -> 128 us (level)
    ppermute x16, waiting for transfers between devices: 16.7 us -> 20.5 us  [ring_gather(): lax.ppermute(ways[1], 'doc', down)]
    ppermute x16, waiting for transfers between devices: 41.2 us -> 37.6 us  [ring_gather(): lax.ppermute(ways[0], 'doc', up)]
  transfers between devices with their start and end apart: 33 -> 33, of which waited for: 26 -> 28; matrix products, arithmetic and copies ran while one was open for 9% -> 9% of each run, Pallas kernels for 13% -> 13%
where the time goes in v7:
time: 128 us; the launch traced here: 127 us
  waiting for transfers between devices  59.8 us (47%)
  starting transfers between devices  34.2 us (27%)
  Pallas kernels  16.6 us (13%)
  local copies, waits for them, and re-layouts  10.9 us (9%)
  matrix products  4.8 us (4%)
    ppermute x16, waiting for transfers between devices, ring_gather(): lax.ppermute(ways[0], 'doc', up)  37.6 us
    ppermute x16, starting transfers between devices, ring_gather(): lax.ppermute(ways[0], 'doc', up)  28.5 us
    ppermute x16, waiting for transfers between devices, ring_gather(): lax.ppermute(ways[1], 'doc', down)  20.5 us
    pallas_call x10, Pallas kernels, add_precond(): pl.pallas_call(functools.partial(precond_kernel, len(entries), acc is not...  11.4 us
    unnamed x7, local copies, waits for them, and re-layouts  7.96 us
    ppermute x16, starting transfers between devices, ring_gather(): lax.ppermute(ways[1], 'doc', down)  5.65 us
    pallas_call x2, Pallas kernels, place(): pl.pallas_call(place_kernel, out_shape=jax.ShapeDtypeStruct((rows, width)...  5.2 us
    dot_general x18, matrix products, dot(): return jnp.dot(a, b, preferred_element_type=jnp.float32)  4.8 us
  transfers between devices with their start and end apart: 33, of which 28 were waited for; matrix products, arithmetic and copies ran while one was open for 9% of the time, Pallas kernels for 13%

profile of v7, /device:TPU:0, one launch (start us, length us, event | category | flops | bytes accessed | tf_op | source)
XLA Modules:
  0.0 127.4 jit_solution(15385744004736162085)
XLA Ops:
  1.0 3.1 %collective-permute-start = (bf16[512,384]{1,0:T(8,128)(2,1)S(1)}, bf16[512,384]{1,0:T(8,128)(2,1)S(1)}, u32[]{:S(2)}, u32[]{:S(2)}) collective-permute-start(bf16[512,384]{1,0:T(8,128)(2,1)S(1)} %slice_bitcast_fusion.1.refs_1_), channel_id=1, source_target_pairs={{0,4},{4,8},{8,12},{12,14},{14,10},{10,6},{6,2},{2,0},{1,5},{5,9},... | collective-permute-start | bytes 1179656 | tf_op jit(solution)/shard_map/ppermute | solution.py:109
  5.2 2.1 %collective-permute-start.16 = (bf16[512,384]{1,0:T(8,128)(2,1)S(1)}, bf16[512,384]{1,0:T(8,128)(2,1)S(1)}, u32[]{:S(2)}, u32[]{:S(2)}) collective-permute-start(bf16[512,384]{1,0:T(8,128)(2,1)S(1)} %slice_bitcast_fusion.refs_1_), channel_id=1, source_target_pairs={{0,4},{4,8},{8,12},{12,14},{14,10},{10,6},{6,2},{2,0},{1,5},{5,9},... | collective-permute-start | bytes 1179656 | tf_op jit(solution)/shard_map/ppermute | solution.py:109
  7.9 3.4 %copy-done = bf16[1,2,512,4096]{3,2,1,0:T(8,128)(2,1)S(1)} copy-done((bf16[1,2,512,4096]{3,2,1,0:T(8,128)(2,1)S(1)}, bf16[1,2,512,4096]{3,2,1,0:T(8,128)(2,1)}, u32[]{:S(2)}) %copy-start) | copy-done | bytes 8388632
  12.3 1.7 %collective-permute-done.refs_2_ = bf16[512,384]{1,0:T(8,128)(2,1)S(1)} collective-permute-done((bf16[512,384]{1,0:T(8,128)(2,1)S(1)}, bf16[512,384]{1,0:T(8,128)(2,1)S(1)}, u32[]{:S(2)}, u32[]{:S(2)}) %collective-permute-start) | collective-permute-done | bytes 393248 | tf_op jit(solution)/shard_map/ppermute | solution.py:109
  14.0 2.2 %collective-permute-done.1.refs_3_ = bf16[512,384]{1,0:T(8,128)(2,1)S(1)} collective-permute-done((bf16[512,384]{1,0:T(8,128)(2,1)S(1)}, bf16[512,384]{1,0:T(8,128)(2,1)S(1)}, u32[]{:S(2)}, u32[]{:S(2)}) %collective-permute-start.1) | collective-permute-done | bytes 393248 | tf_op jit(solution)/shard_map/ppermute | solution.py:109
  18.2 4.6 %copy.8 = bf16[1,224,2,4096]{3,1,2,0:T(8,128)(2,1)S(1)} copy(bf16[1,224,2,4096]{3,2,1,0:T(2,128)(2,1)} %param.7) | data formatting | bytes 7340032 | tf_op args[2]
  26.6 2.6 %shard_map.57 = bf16[224,4096]{1,0:T(8,128)(2,1)S(1)} custom-call(s32[8]{0:T(128)S(1)} %dynamic-slice_bitcast_fusion.table, s32[1,224]{1,0:T(1,128)S(1)} %copy-done.2, bf16[2,224,4096]{2,1,0:T(8,128)(2,1)S(1)} %bitcast.48), custom_call_target="tpu_custom_call" | custom-call | flops 411041792 | bytes 3670016 | tf_op jit(solution)/shard_map/pallas_call | solution.py:66
  30.8 2.2 %collective-permute-done.3.refs_3_ = bf16[512,384]{1,0:T(8,128)(2,1)S(1)} collective-permute-done((bf16[512,384]{1,0:T(8,128)(2,1)S(1)}, bf16[512,384]{1,0:T(8,128)(2,1)S(1)}, u32[]{:S(2)}, u32[]{:S(2)}) %collective-permute-start.3) | collective-permute-done | bytes 393248 | tf_op jit(solution)/shard_map/ppermute | solution.py:109
  35.0 2.6 %shard_map.63 = bf16[224,4096]{1,0:T(8,128)(2,1)S(1)} custom-call(s32[8]{0:T(128)S(1)} %dynamic-slice_bitcast_fusion.table, s32[1,224]{1,0:T(1,128)S(1)} %copy-done.2, bf16[2,224,4096]{2,1,0:T(8,128)(2,1)S(1)} %bitcast.49), custom_call_target="tpu_custom_call" | custom-call | flops 411041792 | bytes 3670016 | tf_op jit(solution)/shard_map/pallas_call | solution.py:66
  39.3 2.2 %collective-permute-done.19.refs_3_ = bf16[512,384]{1,0:T(8,128)(2,1)S(1)} collective-permute-done((bf16[512,384]{1,0:T(8,128)(2,1)S(1)}, bf16[512,384]{1,0:T(8,128)(2,1)S(1)}, u32[]{:S(2)}, u32[]{:S(2)}) %collective-permute-start.19) | collective-permute-done | bytes 393248 | tf_op jit(solution)/shard_map/ppermute | solution.py:109
  44.7 3.0 %collective-permute-done.4.refs_2_ = bf16[512,384]{1,0:T(8,128)(2,1)S(1)} collective-permute-done((bf16[512,384]{1,0:T(8,128)(2,1)S(1)}, bf16[512,384]{1,0:T(8,128)(2,1)S(1)}, u32[]{:S(2)}, u32[]{:S(2)}) %collective-permute-start.4) | collective-permute-done | bytes 393248 | tf_op jit(solution)/shard_map/ppermute | solution.py:109
  47.7 2.2 %collective-permute-done.5.refs_3_ = bf16[512,384]{1,0:T(8,128)(2,1)S(1)} collective-permute-done((bf16[512,384]{1,0:T(8,128)(2,1)S(1)}, bf16[512,384]{1,0:T(8,128)(2,1)S(1)}, u32[]{:S(2)}, u32[]{:S(2)}) %collective-permute-start.5) | collective-permute-done | bytes 393248 | tf_op jit(solution)/shard_map/ppermute | solution.py:109
  49.9 1.6 %collective-permute-start.6 = (bf16[256,384]{1,0:T(8,128)(2,1)S(1)}, bf16[256,384]{1,0:T(8,128)(2,1)S(1)}, u32[]{:S(2)}, u32[]{:S(2)}) collective-permute-start(bf16[256,384]{1,0:T(8,128)(2,1)S(1)} %slice.85), channel_id=1, source_target_pairs={{0,4},{4,8},{8,12},{12,14},{14,10},{10,6},{6,2},{2,0},{1,5},{5,9},... | collective-permute-start | bytes 589832 | tf_op jit(solution)/shard_map/ppermute | solution.py:109
  53.3 2.8 %collective-permute-done.20.refs_2_ = bf16[512,384]{1,0:T(8,128)(2,1)S(1)} collective-permute-done((bf16[512,384]{1,0:T(8,128)(2,1)S(1)}, bf16[512,384]{1,0:T(8,128)(2,1)S(1)}, u32[]{:S(2)}, u32[]{:S(2)}) %collective-permute-start.20) | collective-permute-done | bytes 393248 | tf_op jit(solution)/shard_map/ppermute | solution.py:109
  56.1 2.2 %collective-permute-start.21 = (bf16[256,384]{1,0:T(8,128)(2,1)S(1)}, bf16[256,384]{1,0:T(8,128)(2,1)S(1)}, u32[]{:S(2)}, u32[]{:S(2)}) collective-permute-start(bf16[256,384]{1,0:T(8,128)(2,1)S(1)} %slice.99), channel_id=1, source_target_pairs={{0,4},{4,8},{8,12},{12,14},{14,10},{10,6},{6,2},{2,0},{1,5},{5,9},... | collective-permute-start | bytes 589832 | tf_op jit(solution)/shard_map/ppermute | solution.py:109
  60.3 2.2 %collective-permute-done.7.refs_3_ = bf16[256,384]{1,0:T(8,128)(2,1)S(1)} collective-permute-done((bf16[256,384]{1,0:T(8,128)(2,1)S(1)}, bf16[256,384]{1,0:T(8,128)(2,1)S(1)}, u32[]{:S(2)}, u32[]{:S(2)}) %collective-permute-start.7) | collective-permute-done | bytes 196640 | tf_op jit(solution)/shard_map/ppermute | solution.py:109
  63.5 1.6 %collective-permute-start.8 = (bf16[512,384]{1,0:T(8,128)(2,1)S(1)}, bf16[512,384]{1,0:T(8,128)(2,1)S(1)}, u32[]{:S(2)}, u32[]{:S(2)}) collective-permute-start(bf16[512,384]{1,0:T(8,128)(2,1)S(1)} %shard_map.60), channel_id=1, source_target_pairs={{0,4},{4,8},{8,12},{12,14},{14,10},{10,6},{6,2},{2,0},{1,5},{5,9},... | collective-permute-start | bytes 1179656 | tf_op jit(solution)/shard_map/ppermute | solution.py:109
  67.8 1.6 %collective-permute-start.24 = (bf16[512,384]{1,0:T(8,128)(2,1)S(1)}, bf16[512,384]{1,0:T(8,128)(2,1)S(1)}, u32[]{:S(2)}, u32[]{:S(2)}) collective-permute-start(bf16[512,384]{1,0:T(8,128)(2,1)S(1)} %shard_map.66), channel_id=1, source_target_pairs={{0,4},{4,8},{8,12},{12,14},{14,10},{10,6},{6,2},{2,0},{1,5},{5,9},... | collective-permute-start | bytes 1179656 | tf_op jit(solution)/shard_map/ppermute | solution.py:109
  70.5 5.1 %collective-permute-done.8 = bf16[512,384]{1,0:T(8,128)(2,1)S(1)} collective-permute-done((bf16[512,384]{1,0:T(8,128)(2,1)S(1)}, bf16[512,384]{1,0:T(8,128)(2,1)S(1)}, u32[]{:S(2)}, u32[]{:S(2)}) %collective-permute-start.8) | collective-permute-done | bytes 393248 | tf_op jit(solution)/shard_map/ppermute | solution.py:109
  75.6 1.6 %collective-permute-done.9 = bf16[512,384]{1,0:T(8,128)(2,1)S(1)} collective-permute-done((bf16[512,384]{1,0:T(8,128)(2,1)S(1)}, bf16[512,384]{1,0:T(8,128)(2,1)S(1)}, u32[]{:S(2)}, u32[]{:S(2)}) %collective-permute-start.9) | collective-permute-done | bytes 393248 | tf_op jit(solution)/shard_map/ppermute | solution.py:109
  79.2 4.8 %collective-permute-done.24 = bf16[512,384]{1,0:T(8,128)(2,1)S(1)} collective-permute-done((bf16[512,384]{1,0:T(8,128)(2,1)S(1)}, bf16[512,384]{1,0:T(8,128)(2,1)S(1)}, u32[]{:S(2)}, u32[]{:S(2)}) %collective-permute-start.24) | collective-permute-done | bytes 393248 | tf_op jit(solution)/shard_map/ppermute | solution.py:109
  84.0 1.6 %collective-permute-done.25 = bf16[512,384]{1,0:T(8,128)(2,1)S(1)} collective-permute-done((bf16[512,384]{1,0:T(8,128)(2,1)S(1)}, bf16[512,384]{1,0:T(8,128)(2,1)S(1)}, u32[]{:S(2)}, u32[]{:S(2)}) %collective-permute-start.25) | collective-permute-done | bytes 393248 | tf_op jit(solution)/shard_map/ppermute | solution.py:109
  88.8 3.7 %collective-permute-done.10 = bf16[512,384]{1,0:T(8,128)(2,1)S(1)} collective-permute-done((bf16[512,384]{1,0:T(8,128)(2,1)S(1)}, bf16[512,384]{1,0:T(8,128)(2,1)S(1)}, u32[]{:S(2)}, u32[]{:S(2)}) %collective-permute-start.10) | collective-permute-done | bytes 393248 | tf_op jit(solution)/shard_map/ppermute | solution.py:109
  92.4 1.6 %collective-permute-done.11 = bf16[512,384]{1,0:T(8,128)(2,1)S(1)} collective-permute-done((bf16[512,384]{1,0:T(8,128)(2,1)S(1)}, bf16[512,384]{1,0:T(8,128)(2,1)S(1)}, u32[]{:S(2)}, u32[]{:S(2)}) %collective-permute-start.11) | collective-permute-done | bytes 393248 | tf_op jit(solution)/shard_map/ppermute | solution.py:109
  96.0 4.8 %collective-permute-done.26 = bf16[512,384]{1,0:T(8,128)(2,1)S(1)} collective-permute-done((bf16[512,384]{1,0:T(8,128)(2,1)S(1)}, bf16[512,384]{1,0:T(8,128)(2,1)S(1)}, u32[]{:S(2)}, u32[]{:S(2)}) %collective-permute-start.26) | collective-permute-done | bytes 393248 | tf_op jit(solution)/shard_map/ppermute | solution.py:109
  100.9 1.6 %collective-permute-done.27 = bf16[512,384]{1,0:T(8,128)(2,1)S(1)} collective-permute-done((bf16[512,384]{1,0:T(8,128)(2,1)S(1)}, bf16[512,384]{1,0:T(8,128)(2,1)S(1)}, u32[]{:S(2)}, u32[]{:S(2)}) %collective-permute-start.27) | collective-permute-done | bytes 393248 | tf_op jit(solution)/shard_map/ppermute | solution.py:109
  105.6 3.7 %collective-permute-done.12 = bf16[512,384]{1,0:T(8,128)(2,1)S(1)} collective-permute-done((bf16[512,384]{1,0:T(8,128)(2,1)S(1)}, bf16[512,384]{1,0:T(8,128)(2,1)S(1)}, u32[]{:S(2)}, u32[]{:S(2)}) %collective-permute-start.12) | collective-permute-done | bytes 393248 | tf_op jit(solution)/shard_map/ppermute | solution.py:109
  109.3 1.6 %collective-permute-done.13 = bf16[512,384]{1,0:T(8,128)(2,1)S(1)} collective-permute-done((bf16[512,384]{1,0:T(8,128)(2,1)S(1)}, bf16[512,384]{1,0:T(8,128)(2,1)S(1)}, u32[]{:S(2)}, u32[]{:S(2)}) %collective-permute-start.13) | collective-permute-done | bytes 393248 | tf_op jit(solution)/shard_map/ppermute | solution.py:109
  110.9 1.6 %collective-permute-start.14 = (bf16[256,384]{1,0:T(8,128)(2,1)S(1)}, bf16[256,384]{1,0:T(8,128)(2,1)S(1)}, u32[]{:S(2)}, u32[]{:S(2)}) collective-permute-start(bf16[256,384]{1,0:T(8,128)(2,1)S(1)} %slice.95), channel_id=1, source_target_pairs={{0,4},{4,8},{8,12},{12,14},{14,10},{10,6},{6,2},{2,0},{1,5},{5,9},... | collective-permute-start | bytes 589832 | tf_op jit(solution)/shard_map/ppermute | solution.py:109
  113.1 4.3 %collective-permute-done.28 = bf16[512,384]{1,0:T(8,128)(2,1)S(1)} collective-permute-done((bf16[512,384]{1,0:T(8,128)(2,1)S(1)}, bf16[512,384]{1,0:T(8,128)(2,1)S(1)}, u32[]{:S(2)}, u32[]{:S(2)}) %collective-permute-start.28) | collective-permute-done | bytes 393248 | tf_op jit(solution)/shard_map/ppermute | solution.py:109
  117.3 2.0 %collective-permute-start.30 = (bf16[320,384]{1,0:T(8,128)(2,1)S(1)}, bf16[320,384]{1,0:T(8,128)(2,1)S(1)}, u32[]{:S(2)}, u32[]{:S(2)}) collective-permute-start(bf16[320,384]{1,0:T(8,128)(2,1)S(1)} %slice.109), channel_id=1, source_target_pairs={{0,4},{4,8},{8,12},{12,14},{14,10},{10,6},{6,2},{2,0},{1,5},{5,9},... | collective-permute-start | bytes 737288 | tf_op jit(solution)/shard_map/ppermute | solution.py:109
  125.0 1.6 %collective-permute-done.32 = f32[224,384]{1,0:T(8,128)S(1)} collective-permute-done((f32[224,384]{1,0:T(8,128)S(1)}, f32[224,384]{1,0:T(8,128)S(1)}, u32[]{:S(2)}, u32[]{:S(2)}) %collective-permute-start.32) | collective-permute-done | bytes 344096 | tf_op jit(solution)/shard_map/ppermute | solution.py:142
  (83 shorter events, 43.7 us)
Async XLA Ops:
  1.0 12.9 %collective-permute-start = (bf16[512,384]{1,0:T(8,128)(2,1)S(1)}, bf16[512,384]{1,0:T(8,128)(2,1)S(1)}, u32[]{:S(2)}, u32[]{:S(2)}) collective-permute-start(bf16[512,384]{1,0:T(8,128)(2,1)S(1)} %slice_bitcast_fusion.1.refs_1_), channel_id=1, source_target_pairs={{0,4},{4,8},{8,12},{12,14},{14,10},{10,6},{6,2},{2,0},{1,5},{5,9},... | collective-permute-start | bytes 1179656 | tf_op jit(solution)/shard_map/ppermute | solution.py:109
  4.1 12.0 %collective-permute-start.1 = (bf16[512,384]{1,0:T(8,128)(2,1)S(1)}, bf16[512,384]{1,0:T(8,128)(2,1)S(1)}, u32[]{:S(2)}, u32[]{:S(2)}) collective-permute-start(bf16[512,384]{1,0:T(8,128)(2,1)S(1)} %slice_bitcast_fusion.1.refs_1_), channel_id=1, source_target_pairs={{4,0},{8,4},{12,8},{14,12},{10,14},{6,10},{2,6},{0,2},{5,1},{9,5},... | collective-permute-start | bytes 1179656 | tf_op jit(solution)/shard_map/ppermute | solution.py:109
  5.2 18.6 %collective-permute-start.16 = (bf16[512,384]{1,0:T(8,128)(2,1)S(1)}, bf16[512,384]{1,0:T(8,128)(2,1)S(1)}, u32[]{:S(2)}, u32[]{:S(2)}) collective-permute-start(bf16[512,384]{1,0:T(8,128)(2,1)S(1)} %slice_bitcast_fusion.refs_1_), channel_id=1, source_target_pairs={{0,4},{4,8},{8,12},{12,14},{14,10},{10,6},{6,2},{2,0},{1,5},{5,9},... | collective-permute-start | bytes 1179656 | tf_op jit(solution)/shard_map/ppermute | solution.py:109
  7.2 17.3 %collective-permute-start.17 = (bf16[512,384]{1,0:T(8,128)(2,1)S(1)}, bf16[512,384]{1,0:T(8,128)(2,1)S(1)}, u32[]{:S(2)}, u32[]{:S(2)}) collective-permute-start(bf16[512,384]{1,0:T(8,128)(2,1)S(1)} %slice_bitcast_fusion.refs_1_), channel_id=1, source_target_pairs={{4,0},{8,4},{12,8},{14,12},{10,14},{6,10},{2,6},{0,2},{5,1},{9,5},... | collective-permute-start | bytes 1179656 | tf_op jit(solution)/shard_map/ppermute | solution.py:109
  16.2 14.7 %collective-permute-start.2 = (bf16[512,384]{1,0:T(8,128)(2,1)S(1)}, bf16[512,384]{1,0:T(8,128)(2,1)S(1)}, u32[]{:S(2)}, u32[]{:S(2)}) collective-permute-start(bf16[512,384]{1,0:T(8,128)(2,1)S(1)} %collective-permute-done.refs_2_), channel_id=1, source_target_pairs={{0,4},{4,8},{8,12},{12,14},{14,10},{10,6},{6,2},{2,0},{1,5},{5,9},... | collective-permute-start | bytes 1179656 | tf_op jit(solution)/shard_map/ppermute | solution.py:109
  17.7 15.3 %collective-permute-start.3 = (bf16[512,384]{1,0:T(8,128)(2,1)S(1)}, bf16[512,384]{1,0:T(8,128)(2,1)S(1)}, u32[]{:S(2)}, u32[]{:S(2)}) collective-permute-start(bf16[512,384]{1,0:T(8,128)(2,1)S(1)} %collective-permute-done.1.refs_3_), channel_id=1, source_target_pairs={{4,0},{8,4},{12,8},{14,12},{10,14},{6,10},{2,6},{0,2},{5,1},{9,5},... | collective-permute-start | bytes 1179656 | tf_op jit(solution)/shard_map/ppermute | solution.py:109
  24.6 14.7 %collective-permute-start.18 = (bf16[512,384]{1,0:T(8,128)(2,1)S(1)}, bf16[512,384]{1,0:T(8,128)(2,1)S(1)}, u32[]{:S(2)}, u32[]{:S(2)}) collective-permute-start(bf16[512,384]{1,0:T(8,128)(2,1)S(1)} %collective-permute-done.16.refs_2_), channel_id=1, source_target_pairs={{0,4},{4,8},{8,12},{12,14},{14,10},{10,6},{6,2},{2,0},{1,5},{5,9},... | collective-permute-start | bytes 1179656 | tf_op jit(solution)/shard_map/ppermute | solution.py:109
  26.2 15.3 %collective-permute-start.19 = (bf16[512,384]{1,0:T(8,128)(2,1)S(1)}, bf16[512,384]{1,0:T(8,128)(2,1)S(1)}, u32[]{:S(2)}, u32[]{:S(2)}) collective-permute-start(bf16[512,384]{1,0:T(8,128)(2,1)S(1)} %collective-permute-done.17.refs_3_), channel_id=1, source_target_pairs={{4,0},{8,4},{12,8},{14,12},{10,14},{6,10},{2,6},{0,2},{5,1},{9,5},... | collective-permute-start | bytes 1179656 | tf_op jit(solution)/shard_map/ppermute | solution.py:109
  33.0 14.7 %collective-permute-start.4 = (bf16[512,384]{1,0:T(8,128)(2,1)S(1)}, bf16[512,384]{1,0:T(8,128)(2,1)S(1)}, u32[]{:S(2)}, u32[]{:S(2)}) collective-permute-start(bf16[512,384]{1,0:T(8,128)(2,1)S(1)} %collective-permute-done.2.refs_2_), channel_id=1, source_target_pairs={{0,4},{4,8},{8,12},{12,14},{14,10},{10,6},{6,2},{2,0},{1,5},{5,9},... | collective-permute-start | bytes 1179656 | tf_op jit(solution)/shard_map/ppermute | solution.py:109
  34.6 15.3 %collective-permute-start.5 = (bf16[512,384]{1,0:T(8,128)(2,1)S(1)}, bf16[512,384]{1,0:T(8,128)(2,1)S(1)}, u32[]{:S(2)}, u32[]{:S(2)}) collective-permute-start(bf16[512,384]{1,0:T(8,128)(2,1)S(1)} %collective-permute-done.3.refs_3_), channel_id=1, source_target_pairs={{4,0},{8,4},{12,8},{14,12},{10,14},{6,10},{2,6},{0,2},{5,1},{9,5},... | collective-permute-start | bytes 1179656 | tf_op jit(solution)/shard_map/ppermute | solution.py:109
  41.4 14.7 %collective-permute-start.20 = (bf16[512,384]{1,0:T(8,128)(2,1)S(1)}, bf16[512,384]{1,0:T(8,128)(2,1)S(1)}, u32[]{:S(2)}, u32[]{:S(2)}) collective-permute-start(bf16[512,384]{1,0:T(8,128)(2,1)S(1)} %collective-permute-done.18.refs_2_), channel_id=1, source_target_pairs={{0,4},{4,8},{8,12},{12,14},{14,10},{10,6},{6,2},{2,0},{1,5},{5,9},... | collective-permute-start | bytes 1179656 | tf_op jit(solution)/shard_map/ppermute | solution.py:109
  43.0 15.3 %collective-permute-start.22 = (bf16[512,384]{1,0:T(8,128)(2,1)S(1)}, bf16[512,384]{1,0:T(8,128)(2,1)S(1)}, u32[]{:S(2)}, u32[]{:S(2)}) collective-permute-start(bf16[512,384]{1,0:T(8,128)(2,1)S(1)} %collective-permute-done.19.refs_3_), channel_id=1, source_target_pairs={{4,0},{8,4},{12,8},{14,12},{10,14},{6,10},{2,6},{0,2},{5,1},{9,5},... | collective-permute-start | bytes 1179656 | tf_op jit(solution)/shard_map/ppermute | solution.py:109
  49.9 10.4 %collective-permute-start.6 = (bf16[256,384]{1,0:T(8,128)(2,1)S(1)}, bf16[256,384]{1,0:T(8,128)(2,1)S(1)}, u32[]{:S(2)}, u32[]{:S(2)}) collective-permute-start(bf16[256,384]{1,0:T(8,128)(2,1)S(1)} %slice.85), channel_id=1, source_target_pairs={{0,4},{4,8},{8,12},{12,14},{14,10},{10,6},{6,2},{2,0},{1,5},{5,9},... | collective-permute-start | bytes 589832 | tf_op jit(solution)/shard_map/ppermute | solution.py:109
  51.5 11.0 %collective-permute-start.7 = (bf16[256,384]{1,0:T(8,128)(2,1)S(1)}, bf16[256,384]{1,0:T(8,128)(2,1)S(1)}, u32[]{:S(2)}, u32[]{:S(2)}) collective-permute-start(bf16[256,384]{1,0:T(8,128)(2,1)S(1)} %slice.86), channel_id=1, source_target_pairs={{4,0},{8,4},{12,8},{14,12},{10,14},{6,10},{2,6},{0,2},{5,1},{9,5},... | collective-permute-start | bytes 589832 | tf_op jit(solution)/shard_map/ppermute | solution.py:109
  56.1 10.7 %collective-permute-start.21 = (bf16[256,384]{1,0:T(8,128)(2,1)S(1)}, bf16[256,384]{1,0:T(8,128)(2,1)S(1)}, u32[]{:S(2)}, u32[]{:S(2)}) collective-permute-start(bf16[256,384]{1,0:T(8,128)(2,1)S(1)} %slice.99), channel_id=1, source_target_pairs={{0,4},{4,8},{8,12},{12,14},{14,10},{10,6},{6,2},{2,0},{1,5},{5,9},... | collective-permute-start | bytes 589832 | tf_op jit(solution)/shard_map/ppermute | solution.py:109
  58.4 8.5 %collective-permute-start.23 = (bf16[256,384]{1,0:T(8,128)(2,1)S(1)}, bf16[256,384]{1,0:T(8,128)(2,1)S(1)}, u32[]{:S(2)}, u32[]{:S(2)}) collective-permute-start(bf16[256,384]{1,0:T(8,128)(2,1)S(1)} %slice.121), channel_id=1, source_target_pairs={{4,0},{8,4},{12,8},{14,12},{10,14},{6,10},{2,6},{0,2},{5,1},{9,5},... | collective-permute-start | bytes 589832 | tf_op jit(solution)/shard_map/ppermute | solution.py:109
  63.5 12.1 %collective-permute-start.8 = (bf16[512,384]{1,0:T(8,128)(2,1)S(1)}, bf16[512,384]{1,0:T(8,128)(2,1)S(1)}, u32[]{:S(2)}, u32[]{:S(2)}) collective-permute-start(bf16[512,384]{1,0:T(8,128)(2,1)S(1)} %shard_map.60), channel_id=1, source_target_pairs={{0,4},{4,8},{8,12},{12,14},{14,10},{10,6},{6,2},{2,0},{1,5},{5,9},... | collective-permute-start | bytes 1179656 | tf_op jit(solution)/shard_map/ppermute | solution.py:109
  65.1 12.1 %collective-permute-start.9 = (bf16[512,384]{1,0:T(8,128)(2,1)S(1)}, bf16[512,384]{1,0:T(8,128)(2,1)S(1)}, u32[]{:S(2)}, u32[]{:S(2)}) collective-permute-start(bf16[512,384]{1,0:T(8,128)(2,1)S(1)} %shard_map.60), channel_id=1, source_target_pairs={{4,0},{8,4},{12,8},{14,12},{10,14},{6,10},{2,6},{0,2},{5,1},{9,5},... | collective-permute-start | bytes 1179656 | tf_op jit(solution)/shard_map/ppermute | solution.py:109
  67.8 16.2 %collective-permute-start.24 = (bf16[512,384]{1,0:T(8,128)(2,1)S(1)}, bf16[512,384]{1,0:T(8,128)(2,1)S(1)}, u32[]{:S(2)}, u32[]{:S(2)}) collective-permute-start(bf16[512,384]{1,0:T(8,128)(2,1)S(1)} %shard_map.66), channel_id=1, source_target_pairs={{0,4},{4,8},{8,12},{12,14},{14,10},{10,6},{6,2},{2,0},{1,5},{5,9},... | collective-permute-start | bytes 1179656 | tf_op jit(solution)/shard_map/ppermute | solution.py:109
  69.4 16.1 %collective-permute-start.25 = (bf16[512,384]{1,0:T(8,128)(2,1)S(1)}, bf16[512,384]{1,0:T(8,128)(2,1)S(1)}, u32[]{:S(2)}, u32[]{:S(2)}) collective-permute-start(bf16[512,384]{1,0:T(8,128)(2,1)S(1)} %shard_map.66), channel_id=1, source_target_pairs={{4,0},{8,4},{12,8},{14,12},{10,14},{6,10},{2,6},{0,2},{5,1},{9,5},... | collective-permute-start | bytes 1179656 | tf_op jit(solution)/shard_map/ppermute | solution.py:109
  77.2 15.3 %collective-permute-start.10 = (bf16[512,384]{1,0:T(8,128)(2,1)S(1)}, bf16[512,384]{1,0:T(8,128)(2,1)S(1)}, u32[]{:S(2)}, u32[]{:S(2)}) collective-permute-start(bf16[512,384]{1,0:T(8,128)(2,1)S(1)} %collective-permute-done.8), channel_id=1, source_target_pairs={{0,4},{4,8},{8,12},{12,14},{14,10},{10,6},{6,2},{2,0},{1,5},{5,9},... | collective-permute-start | bytes 1179656 | tf_op jit(solution)/shard_map/ppermute | solution.py:109
  78.7 15.3 %collective-permute-start.11 = (bf16[512,384]{1,0:T(8,128)(2,1)S(1)}, bf16[512,384]{1,0:T(8,128)(2,1)S(1)}, u32[]{:S(2)}, u32[]{:S(2)}) collective-permute-start(bf16[512,384]{1,0:T(8,128)(2,1)S(1)} %collective-permute-done.9), channel_id=1, source_target_pairs={{4,0},{8,4},{12,8},{14,12},{10,14},{6,10},{2,6},{0,2},{5,1},{9,5},... | collective-permute-start | bytes 1179656 | tf_op jit(solution)/shard_map/ppermute | solution.py:109
  85.6 15.3 %collective-permute-start.26 = (bf16[512,384]{1,0:T(8,128)(2,1)S(1)}, bf16[512,384]{1,0:T(8,128)(2,1)S(1)}, u32[]{:S(2)}, u32[]{:S(2)}) collective-permute-start(bf16[512,384]{1,0:T(8,128)(2,1)S(1)} %collective-permute-done.24), channel_id=1, source_target_pairs={{0,4},{4,8},{8,12},{12,14},{14,10},{10,6},{6,2},{2,0},{1,5},{5,9},... | collective-permute-start | bytes 1179656 | tf_op jit(solution)/shard_map/ppermute | solution.py:109
  87.2 15.3 %collective-permute-start.27 = (bf16[512,384]{1,0:T(8,128)(2,1)S(1)}, bf16[512,384]{1,0:T(8,128)(2,1)S(1)}, u32[]{:S(2)}, u32[]{:S(2)}) collective-permute-start(bf16[512,384]{1,0:T(8,128)(2,1)S(1)} %collective-permute-done.25), channel_id=1, source_target_pairs={{4,0},{8,4},{12,8},{14,12},{10,14},{6,10},{2,6},{0,2},{5,1},{9,5},... | collective-permute-start | bytes 1179656 | tf_op jit(solution)/shard_map/ppermute | solution.py:109
  94.0 15.3 %collective-permute-start.12 = (bf16[512,384]{1,0:T(8,128)(2,1)S(1)}, bf16[512,384]{1,0:T(8,128)(2,1)S(1)}, u32[]{:S(2)}, u32[]{:S(2)}) collective-permute-start(bf16[512,384]{1,0:T(8,128)(2,1)S(1)} %collective-permute-done.10), channel_id=1, source_target_pairs={{0,4},{4,8},{8,12},{12,14},{14,10},{10,6},{6,2},{2,0},{1,5},{5,9},... | collective-permute-start | bytes 1179656 | tf_op jit(solution)/shard_map/ppermute | solution.py:109
  95.6 15.3 %collective-permute-start.13 = (bf16[512,384]{1,0:T(8,128)(2,1)S(1)}, bf16[512,384]{1,0:T(8,128)(2,1)S(1)}, u32[]{:S(2)}, u32[]{:S(2)}) collective-permute-start(bf16[512,384]{1,0:T(8,128)(2,1)S(1)} %collective-permute-done.11), channel_id=1, source_target_pairs={{4,0},{8,4},{12,8},{14,12},{10,14},{6,10},{2,6},{0,2},{5,1},{9,5},... | collective-permute-start | bytes 1179656 | tf_op jit(solution)/shard_map/ppermute | solution.py:109
  102.4 14.9 %collective-permute-start.28 = (bf16[512,384]{1,0:T(8,128)(2,1)S(1)}, bf16[512,384]{1,0:T(8,128)(2,1)S(1)}, u32[]{:S(2)}, u32[]{:S(2)}) collective-permute-start(bf16[512,384]{1,0:T(8,128)(2,1)S(1)} %collective-permute-done.26), channel_id=1, source_target_pairs={{0,4},{4,8},{8,12},{12,14},{14,10},{10,6},{6,2},{2,0},{1,5},{5,9},... | collective-permute-start | bytes 1179656 | tf_op jit(solution)/shard_map/ppermute | solution.py:109
  104.0 15.4 %collective-permute-start.29 = (bf16[512,384]{1,0:T(8,128)(2,1)S(1)}, bf16[512,384]{1,0:T(8,128)(2,1)S(1)}, u32[]{:S(2)}, u32[]{:S(2)}) collective-permute-start(bf16[512,384]{1,0:T(8,128)(2,1)S(1)} %collective-permute-done.27), channel_id=1, source_target_pairs={{4,0},{8,4},{12,8},{14,12},{10,14},{6,10},{2,6},{0,2},{5,1},{9,5},... | collective-permute-start | bytes 1179656 | tf_op jit(solution)/shard_map/ppermute | solution.py:109
  110.9 10.2 %collective-permute-start.14 = (bf16[256,384]{1,0:T(8,128)(2,1)S(1)}, bf16[256,384]{1,0:T(8,128)(2,1)S(1)}, u32[]{:S(2)}, u32[]{:S(2)}) collective-permute-start(bf16[256,384]{1,0:T(8,128)(2,1)S(1)} %slice.95), channel_id=1, source_target_pairs={{0,4},{4,8},{8,12},{12,14},{14,10},{10,6},{6,2},{2,0},{1,5},{5,9},... | collective-permute-start | bytes 589832 | tf_op jit(solution)/shard_map/ppermute | solution.py:109
  112.5 9.1 %collective-permute-start.15 = (bf16[256,384]{1,0:T(8,128)(2,1)S(1)}, bf16[256,384]{1,0:T(8,128)(2,1)S(1)}, u32[]{:S(2)}, u32[]{:S(2)}) collective-permute-start(bf16[256,384]{1,0:T(8,128)(2,1)S(1)} %slice.97), channel_id=1, source_target_pairs={{4,0},{8,4},{12,8},{14,12},{10,14},{6,10},{2,6},{0,2},{5,1},{9,5},... | collective-permute-start | bytes 589832 | tf_op jit(solution)/shard_map/ppermute | solution.py:109
  117.3 6.4 %collective-permute-start.30 = (bf16[320,384]{1,0:T(8,128)(2,1)S(1)}, bf16[320,384]{1,0:T(8,128)(2,1)S(1)}, u32[]{:S(2)}, u32[]{:S(2)}) collective-permute-start(bf16[320,384]{1,0:T(8,128)(2,1)S(1)} %slice.109), channel_id=1, source_target_pairs={{0,4},{4,8},{8,12},{12,14},{14,10},{10,6},{6,2},{2,0},{1,5},{5,9},... | collective-permute-start | bytes 737288 | tf_op jit(solution)/shard_map/ppermute | solution.py:109
  119.4 5.2 %collective-permute-start.31 = (bf16[192,384]{1,0:T(8,128)(2,1)S(1)}, bf16[192,384]{1,0:T(8,128)(2,1)S(1)}, u32[]{:S(2)}, u32[]{:S(2)}) collective-permute-start(bf16[192,384]{1,0:T(8,128)(2,1)S(1)} %slice.131), channel_id=1, source_target_pairs={{4,0},{8,4},{12,8},{14,12},{10,14},{6,10},{2,6},{0,2},{5,1},{9,5},... | collective-permute-start | bytes 442376 | tf_op jit(solution)/shard_map/ppermute | solution.py:109
  (4 other events, 20.4 us)
